TPU v7x, 32 devices: a whole 2x2x4 slice. The times are simulated.
32 devices in a mesh: groups: 2 (over x), tensor: 16 (over z, y, core).
Axes of the slice: x: 2, y: 2, z: 4, core: 2. Of those that a mesh axis runs over, the one named last changes fastest.
Arguments:
- tokens: bfloat16 [512, 8192], P(('groups', 'tensor')), parts along dimension 0, may hold values from -6 to 6
- gate_weight: bfloat16 [8192, 16384], P(None, 'tensor'), may hold values from -0.0625 to 0.0625
- up_weight: bfloat16 [8192, 16384], P(None, 'tensor'), may hold values from -0.0625 to 0.0625
- adapter_down_weight: bfloat16 [32, 64, 8192], P(('groups', 'tensor')), parts along dimension 0, may hold values from -0.0625 to 0.0625
- adapter_up_weight: bfloat16 [32, 64, 16384], P(('groups', 'tensor')), parts along dimension 0, may hold values from -0.75 to 0.75
- row_adapter: int32 [512], P('groups'), parts along dimension 0, may hold values from 0 to 15, as said below
- sorted_rows: int32 [512], P('groups'), parts along dimension 0, may hold values from 0 to 255, as said below
- segment_count: int32 [32], P('groups'), parts along dimension 0, may hold values from 1 to 64, as said below
Outputs:
- hidden: bfloat16 [512, 16384], P('groups', 'tensor'), parts along dimension 0
There are 2 independent parts, one for each index of `groups`. A program takes and returns all parts, laid end to end along the dimension named above; an argument that names none is the same for every part. Nothing has to cross between parts.
Inputs may be any that keep to these rules, and one draw needn't show every extreme that they name: Row r uses adapter row_adapter[r]; adapter j is used by segment_count[j] rows. `sorted_rows`: a permutation of the rows; the rows of adapter j stand at positions seg_start[j] to seg_start[j] + segment_count[j] - 1. `segment_count`: the counts sum to 256; some adapter has exactly 64 rows.
All inputs are finite; a program needn't handle non-finite values.
Results may differ from a plain program's by a relative error of at most 0.0036.
Values may be sent and summed in bfloat16 or wider, within the bound.
No kernel may reach another device: no remote copies, remote signals or barrier semaphores. Data moves between devices by JAX's collectives and lax.ppermute only.
A program may use at most 128 MiB of HBM per device.

v0:
```python
import jax
import jax.numpy as jnp
from jax import lax
from jax.sharding import PartitionSpec as P

ROWS_PER_LIMIT = 64


ADAPTER_SCALE = 0.5


def lookup(values_table, indices):
    matches = indices[:, None] == jnp.arange(values_table.shape[0], dtype=jnp.int32)[None, :]
    return jnp.sum(jnp.where(matches, values_table[None, :], 0), axis=1)


def per_device(
    tokens,
    gate_weight,
    up_weight,
    adapter_down_weight,
    adapter_up_weight,
    row_adapter,
    sorted_rows,
    segment_count,
):
    own_index = lax.axis_index("tensor")
    resident_adapters = adapter_down_weight.shape[0]
    rows_all = row_adapter.shape[0]
    seg_start = jnp.cumsum(segment_count) - segment_count
    own_adapters = own_index * resident_adapters + jnp.arange(resident_adapters, dtype=jnp.int32)
    slot_ids = jnp.arange(ROWS_PER_LIMIT, dtype=jnp.int32)
    own_start = lookup(seg_start, own_adapters)
    positions = jnp.clip(own_start[:, None] + slot_ids[None, :], 0, rows_all - 1).reshape(-1)
    wanted = sorted_rows[positions]
    gathered = lax.all_gather(tokens, "tensor", axis=0, tiled=True)
    gate_part = jnp.dot(gathered, gate_weight, preferred_element_type=jnp.float32)
    up_part = jnp.dot(gathered, up_weight, preferred_element_type=jnp.float32)
    selected_rows = gathered[wanted].reshape(resident_adapters, ROWS_PER_LIMIT, tokens.shape[1])
    reduced_rows = jnp.einsum(
        "gqh,glh->gql", selected_rows, adapter_down_weight, preferred_element_type=jnp.float32
    ).astype(jnp.bfloat16)
    output_rows = jnp.einsum(
        "tyj,tjs->tys", reduced_rows, adapter_up_weight, preferred_element_type=jnp.float32
    )
    output_rows = (
        (ADAPTER_SCALE * output_rows)
        .astype(jnp.bfloat16)
        .reshape(resident_adapters * ROWS_PER_LIMIT, adapter_up_weight.shape[2])
    )
    buckets = lax.all_to_all(output_rows, "tensor", split_axis=1, concat_axis=0, tiled=True)
    inverse = (
        jnp.zeros((rows_all,), jnp.int32).at[sorted_rows].set(jnp.arange(rows_all, dtype=jnp.int32))
    )
    slot_row = jnp.clip(inverse - lookup(seg_start, row_adapter), 0, ROWS_PER_LIMIT - 1)
    delta_rows = buckets[row_adapter * ROWS_PER_LIMIT + slot_row]
    return (jax.nn.silu(gate_part) * (up_part + delta_rows.astype(jnp.float32))).astype(
        jnp.bfloat16
    )


def solution(mesh):
    placed = (
        P(("groups", "tensor"), None),
        P(None, "tensor"),
        P(None, "tensor"),
        P(("groups", "tensor"), None, None),
        P(("groups", "tensor"), None, None),
        P("groups"),
        P("groups"),
        P("groups"),
    )
    return jax.shard_map(
        per_device, mesh=mesh, in_specs=placed, out_specs=P("groups", "tensor"), check_vma=False
    )
```

profile of v0, /device:TPU:13, one launch (start us, length us, event | category | flops | bytes accessed | tf_op | source)
XLA Modules:
  0.0 148.9 jit_solution(6563714185962455470)
XLA Ops:
  6.5 0.0 copy-start
  6.5 0.0 all-gather.2.cloned.1.call-start
  6.5 0.7 all-gather.2.cloned.1.call-update
  7.3 0.7 copy.15
  8.0 0.1 reduce.2
  8.2 1.3 fusion.6
  9.4 0.7 fusion.7
  10.1 1.5 gather_fusion
  11.6 49.1 %all-gather.2.cloned.1.call-done = bf16[256,8192]{1,0:T(8,128)(2,1)} async-done(((bf16[16,8192]{1,0:T(8,128)(2,1)}), bf16[256,8192]{1,0:T(8,128)(2,1)}) %all-gather.2.cloned.1.call-update) | async-done | bytes 4194320 | tf_op jit(solution)/shard_map/all_gather | solution.py:36
  60.7 4.9 %gather_fusion.1 = bf16[64,8192]{1,0:T(8,128)(2,1)S(1)} fusion(bf16[256,8192]{1,0:T(8,128)(2,1)} %all-gather.2.cloned.1.call-done, s32[1024]{0:T(1024)S(1)} %pad_clamp_fusion.1), kind=kCustom, calls=%fused_computation.1 | custom fusion | bytes 2097408 | tf_op jit(solution)/shard_map/gather | solution.py:39
  65.6 0.0 copy-done
  65.6 4.2 %fusion = bf16[64,16384]{1,0:T(8,128)(2,1)} fusion(bf16[1,64,16384]{2,1,0:T(8,128)(2,1)S(1)} %copy-done, bf16[64,8192]{1,0:T(8,128)(2,1)S(1)} %gather_fusion.1, bf16[1,64,8192]{2,1,0:T(8,128)(2,1)} %param.11), kind=kOutput, calls=%fused_computation.5 | convolution fusion | flops 203427840 | bytes 6291456 | tf_op jit(solution)/shard_map/tyj,tjs->tys/dot_general | solution.py:43
  69.8 0.0 copy-start.1
  69.8 0.0 copy-start.2
  69.8 3.2 %copy.19 = bf16[8,16,8,1024]{3,2,0,1:T(8,128)(2,1)} copy(bf16[8,16,8,1024]{3,2,1,0:T(8,128)(2,1)} %bitcast.26) | data formatting | bytes 4194304 | tf_op jit(solution)/shard_map/all_to_all | solution.py:51
  73.0 5.5 %all-to-all-start = ((bf16[64,16,1024]{2,0,1:T(8,128)(2,1)}), bf16[64,16,1024]{2,0,1:T(8,128)(2,1)}, u32[]{:S(2)}, u32[]{:S(2)}) async-start(bf16[64,16,1024]{2,0,1:T(8,128)(2,1)} %bitcast.27), calls=%async_computation | async-start | bytes 4194304 | tf_op jit(solution)/shard_map/all_to_all | solution.py:51
  78.5 0.0 copy-done.1
  78.6 1.6 %scatter_custom_fusion = s32[256]{0:T(256)S(1)} fusion(s32[256]{0:T(256)S(1)} %compare_select_fusion.1, s32[256]{0:T(256)S(1)} %iota.18, s32[]{:T(128)} %constant.10.clone.1), kind=kCustom, calls=%fused_computation.26 | custom fusion | bytes 1028 | tf_op jit(solution)/shard_map/scatter | solution.py:53
  80.2 0.0 copy-done.2
  80.2 0.1 select_reduce_fusion
  80.3 12.6 %fusion.11 = f32[256,1024]{1,0:T(8,128)} fusion(bf16[256,8192]{1,0:T(8,128)(2,1)} %all-gather.2.cloned.1.call-done, bf16[8192,1024]{1,0:T(8,128)(2,1)} %param.9), kind=kOutput, calls=%fused_computation.28 | convolution fusion | flops 4294967296 | bytes 22020096 | tf_op jit(solution)/shard_map/dot_general | solution.py:37
  92.9 33.2 %all-to-all-done = bf16[64,16,1024]{2,0,1:T(8,128)(2,1)} async-done(((bf16[64,16,1024]{2,0,1:T(8,128)(2,1)}), bf16[64,16,1024]{2,0,1:T(8,128)(2,1)}, u32[]{:S(2)}, u32[]{:S(2)}) %all-to-all-start) | async-done | bytes 2097184 | tf_op jit(solution)/shard_map/all_to_all | solution.py:51
  126.1 3.4 %gather_fusion.2 = bf16[256,1024]{1,0:T(8,128)(2,1)S(1)} fusion(bf16[1024,1024]{1,0:T(8,128)(2,1)} %bitcast.7, s32[1024]{0:T(1024)S(1)} %pad_clamp_fusion), kind=kCustom, calls=%fused_computation.2 | custom fusion | bytes 1049600 | tf_op jit(solution)/shard_map/gather | solution.py:56
  129.5 12.6 %fusion.3 = bf16[256,1024]{1,0:T(8,128)(2,1)} fusion(bf16[256,8192]{1,0:T(8,128)(2,1)} %all-gather.2.cloned.1.call-done, bf16[8192,1024]{1,0:T(8,128)(2,1)} %param.10, bf16[256,1024]{1,0:T(8,128)(2,1)S(1)} %gather_fusion.2, f32[256,1024]{1,0:T(8,128)} %fusion.11), kind=kOutput, calls=%fused_computation.10 | convolution fusion | flops 4297064448 | bytes 23068672 | tf_op jit(solution)/shard_map/dot_general | solution.py:38
  (8 shorter events, 0.1 us)
Async XLA Ops:
  6.5 59.1 %copy-start = (bf16[1,64,16384]{2,1,0:T(8,128)(2,1)S(1)}, bf16[1,64,16384]{2,1,0:T(8,128)(2,1)}, u32[]{:S(2)}) copy-start(bf16[1,64,16384]{2,1,0:T(8,128)(2,1)} %param.12) | copy-start | bytes 6291460
  6.5 54.2 %all-gather.2.cloned.1.call-start = ((), (), s32[]{:S(2)}) async-start(), calls=%async_computation.1 | async-start | bytes 4456448 | tf_op jit(solution)/shard_map/all_gather | solution.py:36
  69.8 8.7 %copy-start.1 = (s32[256]{0:T(256)S(1)}, s32[256]{0:T(256)}, u32[]{:S(2)}) copy-start(s32[256]{0:T(256)} %param.14) | copy-start | bytes 3076
  69.8 10.3 %copy-start.2 = (s32[256]{0:T(256)S(1)}, s32[256]{0:T(256)}, u32[]{:S(2)}) copy-start(s32[256]{0:T(256)} %param.13) | copy-start | bytes 3076
  73.0 53.1 %all-to-all-start = ((bf16[64,16,1024]{2,0,1:T(8,128)(2,1)}), bf16[64,16,1024]{2,0,1:T(8,128)(2,1)}, u32[]{:S(2)}, u32[]{:S(2)}) async-start(bf16[64,16,1024]{2,0,1:T(8,128)(2,1)} %bitcast.27), calls=%async_computation | async-start | bytes 4194304 | tf_op jit(solution)/shard_map/all_to_all | solution.py:51
Sparse Core Ops, SparseCore 0:
  9.5 51.1 all-gather.1
where the time goes:
time: 149 us
  waiting for transfers between devices  83.1 us (56%)
  matrix products  29.4 us (20%)
  local copies, waits for them, and re-layouts  15.3 us (10%)
  between operations  13.5 us (9%)
  starting transfers between devices  5.54 us (4%)
  other arithmetic  2.23 us (1%)
    all_gather x1, waiting for transfers between devices, per_device(): gathered = lax.all_gather(tokens, 'tensor', axis=0, tiled=True)  49.1 us
    all_to_all x1, waiting for transfers between devices, per_device(): lax.all_to_all(output_rows, 'tensor', split_axis=1, concat_axis=0, tiled=...  33.2 us
    dot_general x1, matrix products, per_device(): jnp.dot(gathered, gate_weight, preferred_element_type=jnp.float32)  12.6 us
    dot_general x1, matrix products, per_device(): up_part = jnp.dot(gathered, up_weight, preferred_element_type=jnp.float32)  12.6 us
    all_to_all x1, starting transfers between devices, per_device(): lax.all_to_all(output_rows, 'tensor', split_axis=1, concat_axis=0, tiled=...  5.53 us
    gather x1, local copies, waits for them, and re-layouts, per_device(): gathered[wanted].reshape(resident_adapters, ROWS_PER_LIMIT, tokens.shape[1])  4.88 us
    dot_general x1, matrix products, per_device(): jnp.einsum('tyj,tjs->tys', reduced_rows, adapter_up_weight, preferred_ele...  4.18 us
    gather x1, local copies, waits for them, and re-layouts, per_device(): delta_rows = buckets[row_adapter * ROWS_PER_LIMIT + slot_row]  3.42 us
  transfers between devices with their start and end apart: 2, of which 2 were waited for; matrix products, arithmetic and copies ran while one was open for 13% of the time, Pallas kernels for 0%

commit v1 on v0

v1 whole, which is shorter than its diff:
```python
import jax
import jax.numpy as jnp
from jax import lax
from jax.sharding import PartitionSpec as P

ADAPTER_SCALE = 0.5


def per_device(
    tokens,
    gate_weight,
    up_weight,
    adapter_down_weight,
    adapter_up_weight,
    row_adapter,
    sorted_rows,
    segment_count,
):
    own_index = lax.axis_index("tensor")
    resident, rank, width = adapter_down_weight.shape
    rows_all = row_adapter.shape[0]
    up_maps = lax.all_to_all(
        adapter_up_weight.reshape(resident * rank, -1), "tensor", split_axis=1, concat_axis=0, tiled=True
    )
    gathered = lax.all_gather(tokens, "tensor", axis=0, tiled=True)
    shrunk = lax.dot_general(
        adapter_down_weight.reshape(resident * rank, width),
        gathered,
        (((1,), (1,)), ((), ())),
        preferred_element_type=jnp.float32,
    ).astype(jnp.bfloat16)
    own_adapters = own_index * resident + jnp.arange(resident, dtype=jnp.int32)
    uses = jnp.repeat(own_adapters, rank)[:, None] == row_adapter[None, :]
    shrunk = jnp.where(uses, shrunk, jnp.zeros_like(shrunk))
    shrunk_all = lax.all_gather(shrunk, "tensor", axis=0, tiled=True)
    gate_part = jnp.dot(gathered, gate_weight, preferred_element_type=jnp.float32)
    up_part = jnp.dot(gathered, up_weight, preferred_element_type=jnp.float32)
    delta = lax.dot_general(
        shrunk_all, up_maps, (((0,), (0,)), ((), ())), preferred_element_type=jnp.float32
    )
    delta = (ADAPTER_SCALE * delta).astype(jnp.bfloat16)
    return (jax.nn.silu(gate_part) * (up_part + delta.astype(jnp.float32))).astype(jnp.bfloat16)


def solution(mesh):
    placed = (
        P(("groups", "tensor"), None),
        P(None, "tensor"),
        P(None, "tensor"),
        P(("groups", "tensor"), None, None),
        P(("groups", "tensor"), None, None),
        P("groups"),
        P("groups"),
        P("groups"),
    )
    return jax.shard_map(
        per_device, mesh=mesh, in_specs=placed, out_specs=P("groups", "tensor"), check_vma=False
    )
```

time: 149 us -> 143 us (0.960)
  the two profiles are of different devices: /device:TPU:13 before, /device:TPU:0 now
where the time goes in v1:
time: 143 us
  waiting for transfers between devices  68.4 us (48%)
  blocking collectives  25.4 us (18%)
  matrix products  22.7 us (16%)
  between operations  13.5 us (9%)
  starting transfers between devices  7.39 us (5%)
  local copies, waits for them, and re-layouts  5.33 us (4%)
    all_gather x1, waiting for transfers between devices, per_device(): gathered = lax.all_gather(tokens, 'tensor', axis=0, tiled=True)  67.7 us
    all_gather x1, blocking collectives, per_device(): shrunk_all = lax.all_gather(shrunk, 'tensor', axis=0, tiled=True)  25.4 us
    dot_general x1, matrix products, per_device(): jnp.dot(gathered, gate_weight, preferred_element_type=jnp.float32)  11.8 us
    all_to_all x1, starting transfers between devices, per_device(): lax.all_to_all(adapter_up_weight.reshape(resident * rank, -1), 'tensor',...  7.39 us
    dot_general x1, matrix products, per_device(): up_part = jnp.dot(gathered, up_weight, preferred_element_type=jnp.float32)  5.39 us
    dot_general x1, matrix products, per_device(): lax.dot_general(adapter_down_weight.reshape(resident * rank, width), gath...  3.58 us
  transfers between devices with their start and end apart: 2, of which 1 were waited for; matrix products, arithmetic and copies ran while one was open for 6% of the time, Pallas kernels for 0%

profile of v1, /device:TPU:0, one launch (start us, length us, event | category | flops | bytes accessed | tf_op | source)
XLA Modules:
  0.0 142.8 jit_solution(15399682660289249464)
XLA Ops:
  6.5 0.0 copy-start
  6.5 0.0 all-gather.2.cloned.1.call-start
  6.5 0.7 all-gather.2.cloned.1.call-update
  7.3 2.8 %copy.9 = bf16[8,8,16,1024]{3,2,1,0:T(8,128)(2,1)S(1)} copy(bf16[8,8,16,1024]{3,1,2,0:T(8,128)(2,1)} %bitcast.18) | data formatting | bytes 4194304
  10.1 0.0 copy-start.2
  10.1 2.5 %copy.8 = bf16[64,16,1024]{2,0,1:T(8,128)(2,1)} copy(bf16[64,16,1024]{2,1,0:T(8,128)(2,1)S(1)} %bitcast.17) | data formatting | bytes 4194304 | tf_op jit(solution)/shard_map/all_to_all | solution.py:22
  12.6 7.4 %all-to-all-start = ((bf16[64,16,1024]{2,0,1:T(8,128)(2,1)}), bf16[64,16,1024]{2,0,1:T(8,128)(2,1)S(1)}, u32[]{:S(2)}, u32[]{:S(2)}) async-start(bf16[64,16,1024]{2,0,1:T(8,128)(2,1)} %copy.8), calls=%async_computation | async-start | bytes 4194304 | tf_op jit(solution)/shard_map/all_to_all | solution.py:22
  20.0 0.0 copy-done.2
  20.0 67.7 %all-gather.2.cloned.1.call-done = bf16[256,8192]{1,0:T(8,128)(2,1)} async-done(((bf16[16,8192]{1,0:T(8,128)(2,1)}), bf16[256,8192]{1,0:T(8,128)(2,1)}) %all-gather.2.cloned.1.call-update) | async-done | bytes 4194320 | tf_op jit(solution)/shard_map/all_gather | solution.py:25
  87.7 0.0 copy-done
  87.7 3.6 %fusion.4 = bf16[64,256]{1,0:T(8,128)(2,1)S(1)} fusion(bf16[256,8192]{1,0:T(8,128)(2,1)} %all-gather.2.cloned.1.call-done, bf16[1,64,8192]{2,1,0:T(8,128)(2,1)S(1)} %copy-done, pred[256]{0:T(512)(128)(4,1)S(1)} %broadcast_compare_fusion), kind=kOutput, calls=%fused_computation.7 | convolution fusion | flops 268468224 | bytes 5275904 | tf_op jit(solution)/shard_map/dot_general | solution.py:26
  91.3 25.4 %all_gather.7 = bf16[1024,256]{1,0:T(8,128)(2,1)} all-gather(bf16[64,256]{1,0:T(8,128)(2,1)S(1)} %fusion.4), channel_id=1, replica_groups=mesh['groups'=2,'tensor'=16] {'tensor'}, dimensions={0}, use_global_device_ids=true | all-gather | bytes 557056 | tf_op jit(solution)/shard_map/all_gather | solution.py:35
  116.7 0.0 all-to-all-done
  116.7 0.0 slice-start
  116.7 1.9 %fusion.2 = f32[256,1024]{1,0:T(8,128)S(1)} fusion(bf16[1024,256]{1,0:T(8,128)(2,1)} %all_gather.7, bf16[1024,1024]{1,0:T(8,128)(2,1)S(1)} %bitcast.16), kind=kOutput, calls=%fused_computation.4 | convolution fusion | flops 537657344 | bytes 3670016 | tf_op jit(solution)/shard_map/dot_general | solution.py:38
  118.6 0.0 copy-start.1
  118.7 0.0 slice-start.1
  118.7 0.0 slice-start.2
  118.7 0.0 slice-start.3
  118.7 11.8 %fusion.6 = f32[256,1024]{1,0:T(8,128)S(1)} fusion(bf16[256,8192]{1,0:T(8,128)(2,1)} %all-gather.2.cloned.1.call-done, bf16[8192,1024]{1,0:T(8,128)(2,1)} %param.9), kind=kOutput, calls=%fused_computation.10 | convolution fusion | flops 4294967296 | bytes 22020096 | tf_op jit(solution)/shard_map/dot_general | solution.py:36
  130.5 0.0 slice-done
  130.5 0.0 copy-done.1
  130.5 0.0 slice-done.1
  130.5 0.0 slice-done.2
  130.5 0.0 slice-done.3
  130.5 5.4 %fusion.3 = bf16[256,1024]{1,0:T(8,128)(2,1)} fusion(f32[256,1024]{1,0:T(8,128)S(1)} %fusion.2, bf16[256,8192]{1,0:T(8,128)(2,1)S(1)} %copy-done.1, bf16[8192,1024]{1,0:T(8,128)(2,1)S(1)} %bitcast.20, f32[256,1024]{1,0:T(8,128)S(1)} %fusion.6), kind=kOutput, calls=%fused_computation.5 | convolution fusion | flops 4296802304 | bytes 23592960 | tf_op jit(solution)/shard_map/dot_general | solution.py:37
  (2 shorter events, 0.0 us)
Async XLA Ops:
  6.5 81.2 %copy-start = (bf16[1,64,8192]{2,1,0:T(8,128)(2,1)S(1)}, bf16[1,64,8192]{2,1,0:T(8,128)(2,1)}, u32[]{:S(2)}) copy-start(bf16[1,64,8192]{2,1,0:T(8,128)(2,1)} %param.11) | copy-start | bytes 3145732
  6.5 81.1 %all-gather.2.cloned.1.call-start = ((), (), s32[]{:S(2)}) async-start(), calls=%async_computation.1 | async-start | bytes 4456448 | tf_op jit(solution)/shard_map/all_gather | solution.py:25
  10.1 9.9 %copy-start.2 = (s32[256]{0:T(256)S(1)}, s32[256]{0:T(256)}, u32[]{:S(2)}) copy-start(s32[256]{0:T(256)} %param.13) | copy-start | bytes 3076
  12.6 104.1 %all-to-all-start = ((bf16[64,16,1024]{2,0,1:T(8,128)(2,1)}), bf16[64,16,1024]{2,0,1:T(8,128)(2,1)S(1)}, u32[]{:S(2)}, u32[]{:S(2)}) async-start(bf16[64,16,1024]{2,0,1:T(8,128)(2,1)} %copy.8), calls=%async_computation | async-start | bytes 4194304 | tf_op jit(solution)/shard_map/all_to_all | solution.py:22
  116.7 13.8 %slice-start = ((s8[16777216]{0:T(1024)(128)(4,1)}), s8[4194304]{0:T(1024)(128)(4,1)S(1)}, s32[]{:S(2)}) async-start(s8[16777216]{0:T(1024)(128)(4,1)} %bitcast.19), calls=%async_computation.2 | async-start | bytes 8388608
  118.6 11.8 %copy-start.1 = (bf16[256,8192]{1,0:T(8,128)(2,1)S(1)}, bf16[256,8192]{1,0:T(8,128)(2,1)}, u32[]{:S(2)}) copy-start(bf16[256,8192]{1,0:T(8,128)(2,1)} %all-gather.2.cloned.1.call-done) | copy-start | bytes 12582916
  118.7 11.8 %slice-start.1 = ((s8[16777216]{0:T(1024)(128)(4,1)}), s8[4194304]{0:T(1024)(128)(4,1)S(1)}, s32[]{:S(2)}) async-start(s8[16777216]{0:T(1024)(128)(4,1)} %bitcast.19), calls=%async_computation.3 | async-start | bytes 8388608
  118.7 11.8 %slice-start.2 = ((s8[16777216]{0:T(1024)(128)(4,1)}), s8[4194304]{0:T(1024)(128)(4,1)S(1)}, s32[]{:S(2)}) async-start(s8[16777216]{0:T(1024)(128)(4,1)} %bitcast.19), calls=%async_computation.4 | async-start | bytes 8388608
  118.7 11.8 %slice-start.3 = ((s8[16777216]{0:T(1024)(128)(4,1)}), s8[4194304]{0:T(1024)(128)(4,1)S(1)}, s32[]{:S(2)}) async-start(s8[16777216]{0:T(1024)(128)(4,1)} %bitcast.19), calls=%async_computation.5 | async-start | bytes 8388608
Sparse Core Ops, SparseCore 0:
  9.5 78.1 all-gather.1

commit v2 on v1

v2 whole, which is shorter than its diff:
```python
import functools

import jax
import jax.numpy as jnp
from jax import lax
from jax.experimental import pallas as pl
from jax.experimental.pallas import tpu as pltpu
from jax.sharding import PartitionSpec as P

ADAPTER_SCALE = 0.5
CORES = 2
MIB = 1024 * 1024


def chip_ring(chips):
    return list(range(0, chips, 2)) + list(range(chips - 1, 0, -2))


def ring_gather(block, axis):
    size = lax.axis_size(axis)
    me = lax.axis_index(axis)
    chips = size // CORES
    ring = chip_ring(chips)
    place = [ring.index(c) for c in range(chips)]
    ring_table = jnp.array(ring, jnp.int32)
    my_place = jnp.array(place, jnp.int32)[me // CORES]
    core = me % CORES

    def moved(value, shift):
        pairs = [
            (ring[p] * CORES + k, ring[(p + shift) % chips] * CORES + k)
            for p in range(chips)
            for k in range(CORES)
        ]
        return lax.ppermute(value, axis, pairs)

    def other_core(value):
        return lax.ppermute(value, axis, [(d, d ^ 1) for d in range(size)])

    pieces = []

    def arrived(value, column, distance):
        chip = ring_table[(my_place + distance) % chips]
        pieces.append((value, column, chip * CORES + core))
        pieces.append((other_core(value), column, chip * CORES + 1 - core))

    arrived(block, 0, 0)
    right = left = block
    for step in range(1, chips // 2):
        right = moved(right, 1)
        left = moved(left, -1)
        arrived(right, 0, -step)
        arrived(left, 0, step)
    half = block.shape[1] // 2
    far = chips // 2
    arrived(moved(right[:, :half], 1), 0, far)
    arrived(moved(left[:, half:], -1), half, far)
    return pieces


def assemble(spots, columns, piece_refs, tokens_vmem, sems):
    copies = []
    for i, ref in enumerate(piece_refs):
        rows, width = ref.shape
        start = pl.multiple_of(spots[i] * rows, rows)
        copies.append(
            pltpu.make_async_copy(
                ref, tokens_vmem.at[pl.ds(start, rows), pl.ds(columns[i], width)], sems.at[i]
            )
        )
    for copy in copies:
        copy.start()
    for copy in copies:
        copy.wait()


def split_kernel(in_ref, out_ref):
    out_ref[0] = in_ref[...]


def split_columns(weights, parts):
    rows, columns = weights.shape
    width = columns // parts
    return pl.pallas_call(
        split_kernel,
        grid=(parts,),
        in_specs=[pl.BlockSpec((rows, width), lambda i: (0, i))],
        out_specs=pl.BlockSpec((1, rows, width), lambda i: (i, 0, 0)),
        out_shape=jax.ShapeDtypeStruct((parts, rows, width), weights.dtype),
        name="split_columns",
    )(weights)


def shrink_kernel(columns, pieces, spots, users_ref, down_ref, *refs):
    piece_refs = refs[:pieces]
    out_ref, tokens_vmem, sems = refs[pieces:]
    assemble(spots, columns, piece_refs, tokens_vmem, sems)
    shrunk = lax.dot_general(
        tokens_vmem[...], down_ref[...], (((1,), (1,)), ((), ())), preferred_element_type=jnp.float32
    )
    turned = jnp.transpose(shrunk)
    out_ref[...] = jnp.where(users_ref[...] != 0, turned, 0.0).astype(out_ref.dtype)


def shrink(spots, columns, pieces, users, down):
    ranks, width = down.shape
    rows = users.shape[1]
    any_spec = pl.BlockSpec(memory_space=pl.ANY)
    return pl.pallas_call(
        functools.partial(shrink_kernel, columns, len(pieces)),
        grid_spec=pltpu.PrefetchScalarGridSpec(
            num_scalar_prefetch=1,
            grid=(1,),
            in_specs=[
                pl.BlockSpec((ranks, rows), lambda i, s: (0, 0)),
                pl.BlockSpec((ranks, width), lambda i, s: (0, 0)),
            ]
            + [any_spec] * len(pieces),
            out_specs=pl.BlockSpec((ranks, rows), lambda i, s: (0, 0)),
            scratch_shapes=[
                pltpu.VMEM((rows, width), jnp.bfloat16),
                pltpu.SemaphoreType.DMA((len(pieces),)),
            ],
        ),
        out_shape=jax.ShapeDtypeStruct((ranks, rows), jnp.bfloat16),
        compiler_params=pltpu.CompilerParams(vmem_limit_bytes=40 * MIB),
        cost_estimate=pl.CostEstimate(
            flops=2 * rows * width * ranks, bytes_accessed=2 * (rows + ranks) * width, transcendentals=0
        ),
        name="shrink",
    )(spots, users, down, *pieces)


def project_kernel(columns, pieces, spots, weight_ref, *refs):
    piece_refs = refs[:pieces]
    out_ref, tokens_vmem, sems = refs[pieces:]
    depth = weight_ref.shape[0]
    k = pl.program_id(1)

    @pl.when((pl.program_id(0) == 0) & (k == 0))
    def _():
        assemble(spots, columns, piece_refs, tokens_vmem, sems)

    part = jnp.dot(
        tokens_vmem[:, pl.ds(pl.multiple_of(k * depth, depth), depth)],
        weight_ref[...],
        preferred_element_type=jnp.float32,
    )

    @pl.when(k == 0)
    def _():
        out_ref[...] = part

    @pl.when(k > 0)
    def _():
        out_ref[...] += part


def project(spots, columns, pieces, weight, rows):
    width, units = weight.shape
    tile = min(256, units)
    depth = min(4096, width)
    any_spec = pl.BlockSpec(memory_space=pl.ANY)
    return pl.pallas_call(
        functools.partial(project_kernel, columns, len(pieces)),
        grid_spec=pltpu.PrefetchScalarGridSpec(
            num_scalar_prefetch=1,
            grid=(units // tile, width // depth),
            in_specs=[pl.BlockSpec((depth, tile), lambda n, k, s: (k, n))] + [any_spec] * len(pieces),
            out_specs=pl.BlockSpec((rows, tile), lambda n, k, s: (0, n)),
            scratch_shapes=[
                pltpu.VMEM((rows, width), jnp.bfloat16),
                pltpu.SemaphoreType.DMA((len(pieces),)),
            ],
        ),
        out_shape=jax.ShapeDtypeStruct((rows, units), jnp.float32),
        compiler_params=pltpu.CompilerParams(vmem_limit_bytes=40 * MIB),
        cost_estimate=pl.CostEstimate(
            flops=2 * rows * width * units, bytes_accessed=2 * (rows + units) * width, transcendentals=0
        ),
        name="project",
    )(spots, weight, *pieces)


def combine_kernel(pieces, ranks, holders, gate_ref, up_ref, maps_ref, *refs):
    piece_refs = refs[:pieces]
    out_ref, shrunk_vmem, sems = refs[pieces:]

    @pl.when(pl.program_id(0) == 0)
    def _():
        copies = []
        for ref in piece_refs:
            for part in range(ref.shape[0] // ranks):
                i = len(copies)
                start = pl.multiple_of(holders[i] * ranks, ranks)
                copies.append(
                    pltpu.make_async_copy(
                        ref.at[pl.ds(part * ranks, ranks)],
                        shrunk_vmem.at[pl.ds(start, ranks)],
                        sems.at[i],
                    )
                )
        for copy in copies:
            copy.start()
        for copy in copies:
            copy.wait()

    delta = lax.dot_general(
        shrunk_vmem[...], maps_ref[...], (((0,), (0,)), ((), ())), preferred_element_type=jnp.float32
    )
    delta = (ADAPTER_SCALE * delta).astype(jnp.bfloat16).astype(jnp.float32)
    gate = gate_ref[...]
    out_ref[...] = (gate / (1.0 + jnp.exp(-gate)) * (up_ref[...] + delta)).astype(out_ref.dtype)


def combine(holders, pieces, gate, up, maps, ranks):
    rows, units = gate.shape
    ranks_all = maps.shape[0]
    tile = min(256, units)
    any_spec = pl.BlockSpec(memory_space=pl.ANY)
    return pl.pallas_call(
        functools.partial(combine_kernel, len(pieces), ranks),
        grid_spec=pltpu.PrefetchScalarGridSpec(
            num_scalar_prefetch=1,
            grid=(units // tile,),
            in_specs=[
                pl.BlockSpec((rows, tile), lambda n, s: (0, n)),
                pl.BlockSpec((rows, tile), lambda n, s: (0, n)),
                pl.BlockSpec((ranks_all, tile), lambda n, s: (0, n)),
            ]
            + [any_spec] * len(pieces),
            out_specs=pl.BlockSpec((rows, tile), lambda n, s: (0, n)),
            scratch_shapes=[
                pltpu.VMEM((ranks_all, rows), jnp.bfloat16),
                pltpu.SemaphoreType.DMA((ranks_all // ranks,)),
            ],
        ),
        out_shape=jax.ShapeDtypeStruct((rows, units), jnp.bfloat16),
        compiler_params=pltpu.CompilerParams(vmem_limit_bytes=48 * MIB),
        cost_estimate=pl.CostEstimate(
            flops=2 * rows * ranks_all * units, bytes_accessed=10 * rows * units, transcendentals=rows * units
        ),
        name="combine",
    )(holders, gate, up, maps, *pieces)


def per_device(
    tokens,
    gate_weight,
    up_weight,
    adapter_down_weight,
    adapter_up_weight,
    row_adapter,
    sorted_rows,
    segment_count,
):
    axis = "tensor"
    size = lax.axis_size(axis)
    me = lax.axis_index(axis)
    resident, rank, width = adapter_down_weight.shape
    ranks = resident * rank
    rows = row_adapter.shape[0]

    own_maps = split_columns(adapter_up_weight.reshape(ranks, -1), size)
    maps = lax.all_to_all(own_maps, axis, split_axis=0, concat_axis=0, tiled=True)
    maps = maps.reshape(size * ranks, -1)

    found = ring_gather(tokens, axis)
    pieces = [piece for piece, _, _ in found]
    columns = [column for _, column, _ in found]
    spots = jnp.stack([spot for _, _, spot in found]).astype(jnp.int32)

    own_adapters = me * resident + jnp.arange(resident, dtype=jnp.int32)
    users = (jnp.repeat(own_adapters, rank)[:, None] == row_adapter[None, :]).astype(jnp.int32)
    shrunk = shrink(spots, columns, pieces, users, adapter_down_weight.reshape(ranks, width))

    near = min(4, size)
    plane = [shrunk]
    for flip in range(1, near):
        plane.append(lax.ppermute(shrunk, axis, [(d, d ^ flip) for d in range(size)]))
    plane_all = jnp.concatenate(plane, axis=0)
    plane_spots = [me ^ flip for flip in range(near)]
    shrunk_pieces = [plane_all]
    for shift in range(1, size // near):
        shrunk_pieces.append(
            lax.ppermute(plane_all, axis, [(d, (d + shift * near) % size) for d in range(size)])
        )
    gate = project(spots, columns, pieces, gate_weight, rows)
    up = project(spots, columns, pieces, up_weight, rows)
    holders = jnp.stack(
        [
            (me // near - shift) % (size // near) * near + ((me % near) ^ flip)
            for shift in range(size // near)
            for flip in range(near)
        ]
    ).astype(jnp.int32)
    return combine(holders, shrunk_pieces, gate, up, maps, ranks)


def solution(mesh):
    placed = (
        P(("groups", "tensor"), None),
        P(None, "tensor"),
        P(None, "tensor"),
        P(("groups", "tensor"), None, None),
        P(("groups", "tensor"), None, None),
        P("groups"),
        P("groups"),
        P("groups"),
    )
    return jax.shard_map(
        per_device, mesh=mesh, in_specs=placed, out_specs=P("groups", "tensor"), check_vma=False
    )
```

time: 143 us -> 165 us (1.15)
  Pallas kernels: 0 us -> 42.7 us
  starting transfers between devices: 7.39 us -> 39.2 us
  blocking collectives: 25.4 us -> 0 us
  matrix products: 22.7 us -> 0 us
  waiting for transfers between devices: 68.4 us -> 47.2 us
  local copies, waits for them, and re-layouts: 5.33 us -> 22.9 us
  between operations: 13.5 us -> 11.8 us
    all_gather x1 -> x0, waiting for transfers between devices: 67.7 us -> none  [per_device(): gathered = lax.all_gather(tokens, 'tensor', axis=0, tiled=True)]
    ppermute x0 -> x23, waiting for transfers between devices: none -> 47.2 us  [the longest x8 45.7 us: moved(): return lax.ppermute(value, axis, pairs)]
    pallas_call x0 -> x5, Pallas kernels: none -> 42.7 us  [the longest x2 25.7 us: project(): pl.pallas_call(functools.partial(project_kernel, columns, len(pieces)), g...]
    ppermute x0 -> x23, starting transfers between devices: none -> 31.7 us  [the longest x8 24.6 us: moved(): return lax.ppermute(value, axis, pairs)]
    all_gather x1 -> x0, blocking collectives: 25.4 us -> none  [per_device(): shrunk_all = lax.all_gather(shrunk, 'tensor', axis=0, tiled=True)]
    dot_general x4 -> x0, matrix products: 22.7 us -> none  [the longest x1 11.8 us: per_device(): jnp.dot(gathered, gate_weight, preferred_element_type=jnp.float32)]
    unnamed x15 -> x68, local copies, waits for them, and re-layouts: 2.84 us -> 20.1 us
    all_to_all x1 -> x0, local copies, waits for them, and re-layouts: 2.49 us -> none  [per_device(): lax.all_to_all(adapter_up_weight.reshape(resident * rank, -1), 'tensor',...]
  transfers between devices with their start and end apart: 2 -> 24, of which waited for: 1 -> 5; matrix products, arithmetic and copies ran while one was open for 6% -> 2% of each run, Pallas kernels for 0% -> 18%
where the time goes in v2:
time: 165 us; the launch traced here: 164 us
  waiting for transfers between devices  47.2 us (29%)
  Pallas kernels  42.7 us (26%)
  starting transfers between devices  39.2 us (24%)
  local copies, waits for them, and re-layouts  22.9 us (14%)
  between operations  11.8 us (7%)
    ppermute x8, waiting for transfers between devices, moved(): return lax.ppermute(value, axis, pairs)  45.7 us
    pallas_call x2, Pallas kernels, project(): pl.pallas_call(functools.partial(project_kernel, columns, len(pieces)), g...  25.7 us
    ppermute x8, starting transfers between devices, moved(): return lax.ppermute(value, axis, pairs)  24.6 us
    unnamed x68, local copies, waits for them, and re-layouts  20.1 us
    pallas_call x1, Pallas kernels, split_columns(): pl.pallas_call(split_kernel, grid=(parts,), in_specs=[pl.BlockSpec((rows,...  9.44 us
    all_to_all x1, starting transfers between devices, per_device(): lax.all_to_all(own_maps, axis, split_axis=0, concat_axis=0, tiled=True)  7.53 us
    pallas_call x1, Pallas kernels, combine(): pl.pallas_call(functools.partial(combine_kernel, len(pieces), ranks), gri...  4.2 us
    ppermute x3, starting transfers between devices, per_device(): lax.ppermute(plane_all, axis, [(d, (d + shift * near) % size) for d in ra...  3.54 us
  transfers between devices with their start and end apart: 24, of which 5 were waited for; matrix products, arithmetic and copies ran while one was open for 2% of the time, Pallas kernels for 18%

profile of v2, /device:TPU:0, one launch (start us, length us, event | category | flops | bytes accessed | tf_op | source)
XLA Modules:
  0.0 163.9 jit_solution(3827588031114161431)
XLA Ops:
  0.0 9.4 %split_columns.1 = bf16[16,64,1024]{2,1,0:T(8,128)(2,1)} custom-call(bf16[64,16384]{1,0:T(8,128)(2,1)} %bitcast.46), custom_call_target="tpu_custom_call" | custom-call | tf_op jit(solution)/shard_map/split_columns/pallas_call | solution.py:84
  9.5 7.5 %all-to-all-start = ((bf16[16,64,1024]{2,1,0:T(8,128)(2,1)}), bf16[16,64,1024]{2,1,0:T(8,128)(2,1)S(1)}, u32[]{:S(2)}, u32[]{:S(2)}) async-start(bf16[16,64,1024]{2,1,0:T(8,128)(2,1)} %split_columns.1), calls=%async_computation | async-start | bytes 4194304 | tf_op jit(solution)/shard_map/all_to_all | solution.py:265
  17.0 2.0 %collective-permute-start.3 = (bf16[16,8192]{1,0:T(8,128)(2,1)S(1)}, bf16[16,8192]{1,0:T(8,128)(2,1)S(1)}, u32[]{:S(2)}, u32[]{:S(2)}) collective-permute-start(bf16[16,8192]{1,0:T(8,128)(2,1)S(1)} %copy-done.4), channel_id=1, source_target_pairs={{0,2},{1,3},{4,0},{5,1},{8,4},{9,5},{12,8},{13,9},{14,12},{15,13},... | collective-permute-start | bytes 786440 | tf_op jit(solution)/shard_map/ppermute | solution.py:35
  19.1 34.8 %collective-permute-done.3.refs_4_ = bf16[16,8192]{1,0:T(8,128)(2,1)S(1)} collective-permute-done((bf16[16,8192]{1,0:T(8,128)(2,1)S(1)}, bf16[16,8192]{1,0:T(8,128)(2,1)S(1)}, u32[]{:S(2)}, u32[]{:S(2)}) %collective-permute-start.3) | collective-permute-done | bytes 262176 | tf_op jit(solution)/shard_map/ppermute | solution.py:35
  53.9 5.7 %collective-permute-start.7 = (bf16[16,8192]{1,0:T(8,128)(2,1)S(1)}, bf16[16,8192]{1,0:T(8,128)(2,1)S(1)}, u32[]{:S(2)}, u32[]{:S(2)}) collective-permute-start(bf16[16,8192]{1,0:T(8,128)(2,1)S(1)} %collective-permute-done.3.refs_4_), channel_id=1, source_target_pairs={{0,2},{1,3},{4,0},{5,1},{8,4},{9,5},{12,8},{13,9},{14,12},{15,13},... | collective-permute-start | bytes 786440 | tf_op jit(solution)/shard_map/ppermute | solution.py:35
  59.5 12.8 %collective-permute-start.5 = (bf16[16,8192]{1,0:T(8,128)(2,1)S(1)}, bf16[16,8192]{1,0:T(8,128)(2,1)}, u32[]{:S(2)}, u32[]{:S(2)}) collective-permute-start(bf16[16,8192]{1,0:T(8,128)(2,1)S(1)} %collective-permute-done.1.refs_2_), channel_id=1, source_target_pairs={{0,4},{1,5},{4,8},{5,9},{8,12},{9,13},{12,14},{13,15},{14,10},{15,... | collective-permute-start | bytes 786440 | tf_op jit(solution)/shard_map/ppermute | solution.py:35
  72.3 6.0 %collective-permute-done.7.refs_8_ = bf16[16,8192]{1,0:T(8,128)(2,1)S(1)} collective-permute-done((bf16[16,8192]{1,0:T(8,128)(2,1)S(1)}, bf16[16,8192]{1,0:T(8,128)(2,1)S(1)}, u32[]{:S(2)}, u32[]{:S(2)}) %collective-permute-start.7) | collective-permute-done | bytes 262176 | tf_op jit(solution)/shard_map/ppermute | solution.py:35
  78.3 2.0 %collective-permute-start.9 = (bf16[16,8192]{1,0:T(8,128)(2,1)}, bf16[16,8192]{1,0:T(8,128)(2,1)S(1)}, u32[]{:S(2)}, u32[]{:S(2)}) collective-permute-start(bf16[16,8192]{1,0:T(8,128)(2,1)} %collective-permute-done.5.refs_6_), channel_id=1, source_target_pairs={{0,4},{1,5},{4,8},{5,9},{8,12},{9,13},{12,14},{13,15},{14,10},{15,... | collective-permute-start | bytes 786440 | tf_op jit(solution)/shard_map/ppermute | solution.py:35
  80.9 4.8 %collective-permute-done.11.refs_12_ = bf16[16,8192]{1,0:T(8,128)(2,1)S(1)} collective-permute-done((bf16[16,8192]{1,0:T(8,128)(2,1)S(1)}, bf16[16,8192]{1,0:T(8,128)(2,1)S(1)}, u32[]{:S(2)}, u32[]{:S(2)}) %collective-permute-start.11) | collective-permute-done | bytes 262176 | tf_op jit(solution)/shard_map/ppermute | solution.py:35
  88.7 1.7 %collective-permute-start.13 = (bf16[16,4096]{1,0:T(8,128)(2,1)}, bf16[16,4096]{1,0:T(8,128)(2,1)}, u32[]{:S(2)}, u32[]{:S(2)}) collective-permute-start(bf16[16,4096]{1,0:T(8,128)(2,1)} %slice.8), channel_id=1, source_target_pairs={{0,4},{1,5},{4,8},{5,9},{8,12},{9,13},{12,14},{13,15},{14,10},{15,... | collective-permute-start | bytes 393224 | tf_op jit(solution)/shard_map/ppermute | solution.py:35
  108.4 0.9 copy-done.11
  109.3 0.9 copy-done.14
  110.3 0.9 copy-done.16
  111.2 0.9 copy-done.18
  112.2 0.9 copy-done.21
  113.1 1.2 copy-done.22
  114.4 3.4 %shrink.1 = bf16[64,256]{1,0:T(8,128)(2,1)S(1)} custom-call(s32[18]{0:T(128)S(1)} %stack.137.spots, s32[64,256]{1,0:T(8,128)S(1)} %eq.59.users_ref, bf16[64,8192]{1,0:T(8,128)(2,1)S(1)} %bitcast.45, bf16[16,8192]{1,0:T(8,128)(2,1)S(1)} %copy-done.4, bf16[16,8192]{1,0:T(8,128)(2,1)S(1)} %copy-done.14, bf16[16,8192]{1,0:T(8,128)(2,1)S(1)} %collective-permute-done.1.refs_2_, ...), custom_call_target="tpu_custom_call" | custom-call | flops 268435456 | bytes 5242880 | tf_op jit(solution)/shard_map/shrink/pallas_call | solution.py:109
  117.9 1.7 %collective-permute-start.18 = (bf16[64,256]{1,0:T(8,128)(2,1)S(1)}, bf16[64,256]{1,0:T(8,128)(2,1)S(1)}, u32[]{:S(2)}, u32[]{:S(2)}) collective-permute-start(bf16[64,256]{1,0:T(8,128)(2,1)S(1)} %shrink.1), channel_id=1, source_target_pairs={{0,2},{1,3},{2,0},{3,1},{4,6},{5,7},{6,4},{7,5},{8,10},{9,11},{10,... | collective-permute-start | bytes 98312 | tf_op jit(solution)/shard_map/ppermute | solution.py:280
  119.7 0.9 copy-done.3
  120.7 0.9 copy-done.7
  121.6 0.9 copy-done.9
  122.6 12.8 %project.3.up_ref = f32[256,1024]{1,0:T(8,128)S(1)} custom-call(s32[18]{0:T(128)S(1)} %stack.137.spots, bf16[8192,1024]{1,0:T(8,128)(2,1)} %weight_ref.3, bf16[16,8192]{1,0:T(8,128)(2,1)S(1)} %copy-done.5, bf16[16,8192]{1,0:T(8,128)(2,1)S(1)} %copy-done.14, bf16[16,8192]{1,0:T(8,128)(2,1)S(1)} %copy-done.9, bf16[16,8192]{1,0:T(8,128)(2,1)S(1)} %copy-done.19, ...), custom_call_target="tpu_custom_call" | custom-call | flops 4294967296 | bytes 20971520 | tf_op jit(solution)/shard_map/project/pallas_call | solution.py:164
  135.5 1.2 collective-permute-start.22
  136.7 1.7 %collective-permute-start.21 = (bf16[256,256]{1,0:T(8,128)(2,1)S(1)}, bf16[256,256]{1,0:T(8,128)(2,1)S(1)}, u32[]{:S(2)}, u32[]{:S(2)}) collective-permute-start(bf16[256,256]{1,0:T(8,128)(2,1)S(1)} %pad_maximum_fusion.refs_0_), channel_id=1, source_target_pairs={{0,8},{1,9},{2,10},{3,11},{4,12},{5,13},{6,14},{7,15},{8,0},{9,1},... | collective-permute-start | bytes 393224 | tf_op jit(solution)/shard_map/ppermute | solution.py:286
  139.0 12.8 %project.2.gate_ref = f32[256,1024]{1,0:T(8,128)S(1)} custom-call(s32[18]{0:T(128)S(1)} %stack.137.spots, bf16[8192,1024]{1,0:T(8,128)(2,1)} %weight_ref.2, bf16[16,8192]{1,0:T(8,128)(2,1)S(1)} %copy-done.5, bf16[16,8192]{1,0:T(8,128)(2,1)S(1)} %copy-done.14, bf16[16,8192]{1,0:T(8,128)(2,1)S(1)} %copy-done.9, bf16[16,8192]{1,0:T(8,128)(2,1)S(1)} %copy-done.19, ...), custom_call_target="tpu_custom_call" | custom-call | flops 4294967296 | bytes 20971520 | tf_op jit(solution)/shard_map/project/pallas_call | solution.py:164
  151.9 1.0 copy-done
  154.8 1.2 copy-done.1
  156.1 0.9 copy-done.24
  157.0 0.9 copy-done.26
  157.9 0.9 copy-done.28
  158.8 0.9 copy-done.30
  159.7 4.2 %combine.1 = bf16[256,1024]{1,0:T(8,128)(2,1)} custom-call(s32[16]{0:T(128)S(1)} %stack.120.holders, f32[256,1024]{1,0:T(8,128)S(1)} %copy-done.1, f32[256,1024]{1,0:T(8,128)S(1)} %project.3.up_ref, bf16[1024,1024]{1,0:T(8,128)(2,1)S(1)} %bitcast.44, bf16[256,256]{1,0:T(8,128)(2,1)S(1)} %copy-done.24, bf16[256,256]{1,0:T(8,128)(2,1)S(1)} %copy-done.30, ...), custom_call_target="tpu_custom_call" | custom-call | flops 536870912 | bytes 2621440 | tf_op jit(solution)/shard_map/combine/pallas_call | solution.py:221
  (98 shorter events, 12.7 us)
Async XLA Ops:
  9.4 7.6 %copy-start.4 = (bf16[16,8192]{1,0:T(8,128)(2,1)S(1)}, bf16[16,8192]{1,0:T(8,128)(2,1)}, u32[]{:S(2)}) copy-start(bf16[16,8192]{1,0:T(8,128)(2,1)} %refs_0_.5) | copy-start | bytes 786436
  9.4 83.7 %copy-start.33 = (s32[8]{0:T(128)S(1)}, s32[8]{0:T(128)}, u32[]{:S(2)}) copy-start(s32[8]{0:T(128)} %constant.211.clone) | copy-start | bytes 100
  9.4 90.7 %copy-start.31 = (s32[8]{0:T(128)S(1)}, s32[8]{0:T(128)}, u32[]{:S(2)}) copy-start(s32[8]{0:T(128)} %constant.210.clone) | copy-start | bytes 100
  9.4 97.4 %copy-start.32 = (s32[256]{0:T(256)S(1)}, s32[256]{0:T(256)}, u32[]{:S(2)}) copy-start(s32[256]{0:T(256)} %param.15) | copy-start | bytes 3076
  9.5 145.4 %all-to-all-start = ((bf16[16,64,1024]{2,1,0:T(8,128)(2,1)}), bf16[16,64,1024]{2,1,0:T(8,128)(2,1)S(1)}, u32[]{:S(2)}, u32[]{:S(2)}) async-start(bf16[16,64,1024]{2,1,0:T(8,128)(2,1)} %split_columns.1), calls=%async_computation | async-start | bytes 4194304 | tf_op jit(solution)/shard_map/all_to_all | solution.py:265
  17.0 36.9 %collective-permute-start.3 = (bf16[16,8192]{1,0:T(8,128)(2,1)S(1)}, bf16[16,8192]{1,0:T(8,128)(2,1)S(1)}, u32[]{:S(2)}, u32[]{:S(2)}) collective-permute-start(bf16[16,8192]{1,0:T(8,128)(2,1)S(1)} %copy-done.4), channel_id=1, source_target_pairs={{0,2},{1,3},{4,0},{5,1},{8,4},{9,5},{12,8},{13,9},{14,12},{15,13},... | collective-permute-start | bytes 786440 | tf_op jit(solution)/shard_map/ppermute | solution.py:35
  19.0 40.6 %collective-permute-start.1 = (bf16[16,8192]{1,0:T(8,128)(2,1)S(1)}, bf16[16,8192]{1,0:T(8,128)(2,1)S(1)}, u32[]{:S(2)}, u32[]{:S(2)}) collective-permute-start(bf16[16,8192]{1,0:T(8,128)(2,1)S(1)} %copy-done.4), channel_id=1, source_target_pairs={{0,4},{1,5},{4,8},{5,9},{8,12},{9,13},{12,14},{13,15},{14,10},{15,... | collective-permute-start | bytes 786440 | tf_op jit(solution)/shard_map/ppermute | solution.py:35
  53.9 63.9 %copy-start.6 = (bf16[16,8192]{1,0:T(8,128)(2,1)}, bf16[16,8192]{1,0:T(8,128)(2,1)S(1)}, u32[]{:S(2)}) copy-start(bf16[16,8192]{1,0:T(8,128)(2,1)S(1)} %collective-permute-done.3.refs_4_) | copy-start | bytes 786436
  53.9 24.5 %collective-permute-start.7 = (bf16[16,8192]{1,0:T(8,128)(2,1)S(1)}, bf16[16,8192]{1,0:T(8,128)(2,1)S(1)}, u32[]{:S(2)}, u32[]{:S(2)}) collective-permute-start(bf16[16,8192]{1,0:T(8,128)(2,1)S(1)} %collective-permute-done.3.refs_4_), channel_id=1, source_target_pairs={{0,2},{1,3},{4,0},{5,1},{8,4},{9,5},{12,8},{13,9},{14,12},{15,13},... | collective-permute-start | bytes 786440 | tf_op jit(solution)/shard_map/ppermute | solution.py:35
  59.5 58.2 %copy-start.8 = (bf16[16,8192]{1,0:T(8,128)(2,1)}, bf16[16,8192]{1,0:T(8,128)(2,1)S(1)}, u32[]{:S(2)}) copy-start(bf16[16,8192]{1,0:T(8,128)(2,1)S(1)} %collective-permute-done.1.refs_2_) | copy-start | bytes 786436
  59.5 18.8 %collective-permute-start.5 = (bf16[16,8192]{1,0:T(8,128)(2,1)S(1)}, bf16[16,8192]{1,0:T(8,128)(2,1)}, u32[]{:S(2)}, u32[]{:S(2)}) collective-permute-start(bf16[16,8192]{1,0:T(8,128)(2,1)S(1)} %collective-permute-done.1.refs_2_), channel_id=1, source_target_pairs={{0,4},{1,5},{4,8},{5,9},{8,12},{9,13},{12,14},{13,15},{14,10},{15,... | collective-permute-start | bytes 786440 | tf_op jit(solution)/shard_map/ppermute | solution.py:35
  78.3 7.4 %collective-permute-start.11 = (bf16[16,8192]{1,0:T(8,128)(2,1)S(1)}, bf16[16,8192]{1,0:T(8,128)(2,1)S(1)}, u32[]{:S(2)}, u32[]{:S(2)}) collective-permute-start(bf16[16,8192]{1,0:T(8,128)(2,1)S(1)} %collective-permute-done.7.refs_8_), channel_id=1, source_target_pairs={{0,2},{1,3},{4,0},{5,1},{8,4},{9,5},{12,8},{13,9},{14,12},{15,13},... | collective-permute-start | bytes 786440 | tf_op jit(solution)/shard_map/ppermute | solution.py:35
  78.3 8.7 %collective-permute-start.9 = (bf16[16,8192]{1,0:T(8,128)(2,1)}, bf16[16,8192]{1,0:T(8,128)(2,1)S(1)}, u32[]{:S(2)}, u32[]{:S(2)}) collective-permute-start(bf16[16,8192]{1,0:T(8,128)(2,1)} %collective-permute-done.5.refs_6_), channel_id=1, source_target_pairs={{0,4},{1,5},{4,8},{5,9},{8,12},{9,13},{12,14},{13,15},{14,10},{15,... | collective-permute-start | bytes 786440 | tf_op jit(solution)/shard_map/ppermute | solution.py:35
  80.4 7.7 %collective-permute-start = (bf16[16,8192]{1,0:T(8,128)(2,1)S(1)}, bf16[16,8192]{1,0:T(8,128)(2,1)S(1)}, u32[]{:S(2)}, u32[]{:S(2)}) collective-permute-start(bf16[16,8192]{1,0:T(8,128)(2,1)S(1)} %copy-done.4), channel_id=1, source_target_pairs={{0,1},{1,0},{2,3},{3,2},{4,5},{5,4},{6,7},{7,6},{8,9},{9,8},{10,11... | collective-permute-start | bytes 786440 | tf_op jit(solution)/shard_map/ppermute | solution.py:38
  80.4 10.1 %collective-permute-start.4 = (bf16[16,8192]{1,0:T(8,128)(2,1)S(1)}, bf16[16,8192]{1,0:T(8,128)(2,1)S(1)}, u32[]{:S(2)}, u32[]{:S(2)}) collective-permute-start(bf16[16,8192]{1,0:T(8,128)(2,1)S(1)} %collective-permute-done.3.refs_4_), channel_id=1, source_target_pairs={{0,1},{1,0},{2,3},{3,2},{4,5},{5,4},{6,7},{7,6},{8,9},{9,8},{10,11... | collective-permute-start | bytes 786440 | tf_op jit(solution)/shard_map/ppermute | solution.py:38
  80.9 10.3 %collective-permute-start.2 = (bf16[16,8192]{1,0:T(8,128)(2,1)S(1)}, bf16[16,8192]{1,0:T(8,128)(2,1)S(1)}, u32[]{:S(2)}, u32[]{:S(2)}) collective-permute-start(bf16[16,8192]{1,0:T(8,128)(2,1)S(1)} %collective-permute-done.1.refs_2_), channel_id=1, source_target_pairs={{0,1},{1,0},{2,3},{3,2},{4,5},{5,4},{6,7},{7,6},{8,9},{9,8},{10,11... | collective-permute-start | bytes 786440 | tf_op jit(solution)/shard_map/ppermute | solution.py:38
  85.7 6.7 %collective-permute-start.8 = (bf16[16,8192]{1,0:T(8,128)(2,1)S(1)}, bf16[16,8192]{1,0:T(8,128)(2,1)S(1)}, u32[]{:S(2)}, u32[]{:S(2)}) collective-permute-start(bf16[16,8192]{1,0:T(8,128)(2,1)S(1)} %collective-permute-done.7.refs_8_), channel_id=1, source_target_pairs={{0,1},{1,0},{2,3},{3,2},{4,5},{5,4},{6,7},{7,6},{8,9},{9,8},{10,11... | collective-permute-start | bytes 786440 | tf_op jit(solution)/shard_map/ppermute | solution.py:38
  87.1 30.7 %copy-start.2 = (bf16[16,8192]{1,0:T(8,128)(2,1)}, bf16[16,8192]{1,0:T(8,128)(2,1)S(1)}, u32[]{:S(2)}) copy-start(bf16[16,8192]{1,0:T(8,128)(2,1)S(1)} %collective-permute-done.9.refs_10_) | copy-start | bytes 786436
  87.1 19.1 %collective-permute-start.15 = (bf16[16,4096]{1,0:T(8,128)(2,1)}, bf16[16,4096]{1,0:T(8,128)(2,1)S(1)}, u32[]{:S(2)}, u32[]{:S(2)}) collective-permute-start(bf16[16,4096]{1,0:T(8,128)(2,1)} %slice.9), channel_id=1, source_target_pairs={{0,2},{1,3},{4,0},{5,1},{8,4},{9,5},{12,8},{13,9},{14,12},{15,13},... | collective-permute-start | bytes 393224 | tf_op jit(solution)/shard_map/ppermute | solution.py:35
  88.7 18.1 %collective-permute-start.13 = (bf16[16,4096]{1,0:T(8,128)(2,1)}, bf16[16,4096]{1,0:T(8,128)(2,1)}, u32[]{:S(2)}, u32[]{:S(2)}) collective-permute-start(bf16[16,4096]{1,0:T(8,128)(2,1)} %slice.8), channel_id=1, source_target_pairs={{0,4},{1,5},{4,8},{5,9},{8,12},{9,13},{12,14},{13,15},{14,10},{15,... | collective-permute-start | bytes 393224 | tf_op jit(solution)/shard_map/ppermute | solution.py:35
  91.2 15.7 %collective-permute-start.6 = (bf16[16,8192]{1,0:T(8,128)(2,1)}, bf16[16,8192]{1,0:T(8,128)(2,1)}, u32[]{:S(2)}, u32[]{:S(2)}) collective-permute-start(bf16[16,8192]{1,0:T(8,128)(2,1)} %collective-permute-done.5.refs_6_), channel_id=1, source_target_pairs={{0,1},{1,0},{2,3},{3,2},{4,5},{5,4},{6,7},{7,6},{8,9},{9,8},{10,11... | collective-permute-start | bytes 786440 | tf_op jit(solution)/shard_map/ppermute | solution.py:38
  91.9 16.5 %collective-permute-start.12 = (bf16[16,8192]{1,0:T(8,128)(2,1)S(1)}, bf16[16,8192]{1,0:T(8,128)(2,1)}, u32[]{:S(2)}, u32[]{:S(2)}) collective-permute-start(bf16[16,8192]{1,0:T(8,128)(2,1)S(1)} %collective-permute-done.11.refs_12_), channel_id=1, source_target_pairs={{0,1},{1,0},{2,3},{3,2},{4,5},{5,4},{6,7},{7,6},{8,9},{9,8},{10,11... | collective-permute-start | bytes 786440 | tf_op jit(solution)/shard_map/ppermute | solution.py:38
  93.1 15.3 %collective-permute-start.10 = (bf16[16,8192]{1,0:T(8,128)(2,1)S(1)}, bf16[16,8192]{1,0:T(8,128)(2,1)}, u32[]{:S(2)}, u32[]{:S(2)}) collective-permute-start(bf16[16,8192]{1,0:T(8,128)(2,1)S(1)} %collective-permute-done.9.refs_10_), channel_id=1, source_target_pairs={{0,1},{1,0},{2,3},{3,2},{4,5},{5,4},{6,7},{7,6},{8,9},{9,8},{10,11... | collective-permute-start | bytes 786440 | tf_op jit(solution)/shard_map/ppermute | solution.py:38
  106.2 1.6 collective-permute-start.16
  106.8 1.6 collective-permute-start.14
  117.8 17.6 %collective-permute-start.19 = (bf16[64,256]{1,0:T(8,128)(2,1)S(1)}, bf16[64,256]{1,0:T(8,128)(2,1)S(1)}, u32[]{:S(2)}, u32[]{:S(2)}) collective-permute-start(bf16[64,256]{1,0:T(8,128)(2,1)S(1)} %shrink.1), channel_id=1, source_target_pairs={{0,3},{1,2},{2,1},{3,0},{4,7},{5,6},{6,5},{7,4},{8,11},{9,10},{10,... | collective-permute-start | bytes 98312 | tf_op jit(solution)/shard_map/ppermute | solution.py:280
  117.9 17.5 %collective-permute-start.18 = (bf16[64,256]{1,0:T(8,128)(2,1)S(1)}, bf16[64,256]{1,0:T(8,128)(2,1)S(1)}, u32[]{:S(2)}, u32[]{:S(2)}) collective-permute-start(bf16[64,256]{1,0:T(8,128)(2,1)S(1)} %shrink.1), channel_id=1, source_target_pairs={{0,2},{1,3},{2,0},{3,1},{4,6},{5,7},{6,4},{7,5},{8,10},{9,11},{10,... | collective-permute-start | bytes 98312 | tf_op jit(solution)/shard_map/ppermute | solution.py:280
  119.6 15.8 %collective-permute-start.17 = (bf16[64,256]{1,0:T(8,128)(2,1)S(1)}, bf16[64,256]{1,0:T(8,128)(2,1)S(1)}, u32[]{:S(2)}, u32[]{:S(2)}) collective-permute-start(bf16[64,256]{1,0:T(8,128)(2,1)S(1)} %shrink.1), channel_id=1, source_target_pairs={{0,1},{1,0},{2,3},{3,2},{4,5},{5,4},{6,7},{7,6},{8,9},{9,8},{10,11... | collective-permute-start | bytes 98312 | tf_op jit(solution)/shard_map/ppermute | solution.py:280
  135.5 16.4 %copy-start.23 = (bf16[256,256]{1,0:T(8,128)(2,1)}, bf16[256,256]{1,0:T(8,128)(2,1)S(1)}, u32[]{:S(2)}) copy-start(bf16[256,256]{1,0:T(8,128)(2,1)S(1)} %pad_maximum_fusion.refs_0_) | copy-start | bytes 393220
  135.5 17.4 %collective-permute-start.22 = (bf16[256,256]{1,0:T(8,128)(2,1)S(1)}, bf16[256,256]{1,0:T(8,128)(2,1)S(1)}, u32[]{:S(2)}, u32[]{:S(2)}) collective-permute-start(bf16[256,256]{1,0:T(8,128)(2,1)S(1)} %pad_maximum_fusion.refs_0_), channel_id=1, source_target_pairs={{0,12},{1,13},{2,14},{3,15},{4,0},{5,1},{6,2},{7,3},{8,4},{9,5},{1... | collective-permute-start | bytes 393224 | tf_op jit(solution)/shard_map/ppermute | solution.py:286
  136.7 16.8 %collective-permute-start.21 = (bf16[256,256]{1,0:T(8,128)(2,1)S(1)}, bf16[256,256]{1,0:T(8,128)(2,1)S(1)}, u32[]{:S(2)}, u32[]{:S(2)}) collective-permute-start(bf16[256,256]{1,0:T(8,128)(2,1)S(1)} %pad_maximum_fusion.refs_0_), channel_id=1, source_target_pairs={{0,8},{1,9},{2,10},{3,11},{4,12},{5,13},{6,14},{7,15},{8,0},{9,1},... | collective-permute-start | bytes 393224 | tf_op jit(solution)/shard_map/ppermute | solution.py:286
  138.4 15.8 %collective-permute-start.20 = (bf16[256,256]{1,0:T(8,128)(2,1)S(1)}, bf16[256,256]{1,0:T(8,128)(2,1)S(1)}, u32[]{:S(2)}, u32[]{:S(2)}) collective-permute-start(bf16[256,256]{1,0:T(8,128)(2,1)S(1)} %pad_maximum_fusion.refs_0_), channel_id=1, source_target_pairs={{0,4},{1,5},{2,6},{3,7},{4,8},{5,9},{6,10},{7,11},{8,12},{9,13},{1... | collective-permute-start | bytes 393224 | tf_op jit(solution)/shard_map/ppermute | solution.py:286
  (26 other events, 36.1 us)

commit v3 on v2

v3 whole, which is shorter than its diff:
```python
import functools

import jax
import jax.numpy as jnp
from jax import lax
from jax.experimental import pallas as pl
from jax.experimental.pallas import tpu as pltpu
from jax.sharding import PartitionSpec as P

ADAPTER_SCALE = 0.5
CORES = 2
MIB = 1024 * 1024


def chip_ring(chips):
    return list(range(0, chips, 2)) + list(range(chips - 1, 0, -2))


def ring_gather(block, axis, extra, prepare):
    size = lax.axis_size(axis)
    chips = size // CORES
    ring = chip_ring(chips)

    def moved(value, shift):
        pairs = [
            (ring[p] * CORES + k, ring[(p + shift) % chips] * CORES + k)
            for p in range(chips)
            for k in range(CORES)
        ]
        return lax.ppermute(value, axis, pairs)

    def other_core(value):
        return lax.ppermute(value, axis, [(d, d ^ 1) for d in range(size)])

    pieces = []
    where = [[] for _ in range(size)]

    def arrived(value, column, distance):
        pieces.append((value, column))
        pieces.append((other_core(value), column))
        for device in range(size):
            chip = ring[(ring.index(device // CORES) + distance) % chips]
            core = device % CORES
            where[device] += [chip * CORES + core, chip * CORES + 1 - core]

    arrived(block, 0, 0)
    right = left = block
    for step in range(1, chips // 2):
        if step == 2:
            extra, right, left = lax.optimization_barrier((extra, right, left))
            extra = prepare(extra)
        if step == 3:
            extra, right, left = lax.optimization_barrier((extra, right, left))
        right = moved(right, 1)
        left = moved(left, -1)
        arrived(right, 0, -step)
        arrived(left, 0, step)
    half = block.shape[1] // 2
    far = chips // 2
    arrived(moved(right[:, :half], 1), 0, far)
    arrived(moved(left[:, half:], -1), half, far)
    return pieces, where, extra


def assemble(spots, columns, piece_refs, tokens_vmem, sems):
    copies = []
    for i, ref in enumerate(piece_refs):
        rows, width = ref.shape
        start = pl.multiple_of(spots[i] * rows, rows)
        copies.append(
            pltpu.make_async_copy(
                ref, tokens_vmem.at[pl.ds(start, rows), pl.ds(columns[i], width)], sems.at[i]
            )
        )
    for copy in copies:
        copy.start()
    for copy in copies:
        copy.wait()


def split_kernel(in_ref, out_ref):
    width = out_ref.shape[2]
    for part in range(out_ref.shape[0]):
        out_ref[part] = in_ref[:, part * width : (part + 1) * width]


def split_columns(weights, parts):
    rows, columns = weights.shape
    width = columns // parts
    group = min(4, parts)
    return pl.pallas_call(
        split_kernel,
        grid=(parts // group,),
        in_specs=[pl.BlockSpec((rows, group * width), lambda i: (0, i))],
        out_specs=pl.BlockSpec((group, rows, width), lambda i: (i, 0, 0)),
        out_shape=jax.ShapeDtypeStruct((parts, rows, width), weights.dtype),
        name="split_columns",
    )(weights)


HBM_SPEC = pl.BlockSpec(memory_space=pltpu.HBM)


def shrink_kernel(columns, pieces, rank, place, users_ref, down_ref, *refs):
    piece_refs = refs[:pieces]
    out_ref, tokens_vmem, sems = refs[pieces:]
    assemble(place, columns, piece_refs, tokens_vmem, sems)
    ranks = down_ref.shape[0]
    resident = ranks // rank
    shrunk = lax.dot_general(
        tokens_vmem[...], down_ref[...], (((1,), (1,)), ((), ())), preferred_element_type=jnp.float32
    )
    turned = jnp.transpose(shrunk)
    total = jnp.zeros(out_ref.shape, jnp.float32)
    for r in range(resident):
        mine = users_ref[...] == place[pieces] * resident + r
        total += jnp.where(mine, turned[r * rank : (r + 1) * rank], 0.0)
    out_ref[...] = total.astype(out_ref.dtype)


def shrink(place, columns, pieces, row_adapter, down, rank):
    ranks, width = down.shape
    rows = row_adapter.shape[0]
    return pl.pallas_call(
        functools.partial(shrink_kernel, columns, len(pieces), rank),
        grid_spec=pltpu.PrefetchScalarGridSpec(
            num_scalar_prefetch=1,
            grid=(1,),
            in_specs=[
                pl.BlockSpec((1, rows), lambda i, s: (0, 0)),
                pl.BlockSpec((ranks, width), lambda i, s: (0, 0)),
            ]
            + [HBM_SPEC] * len(pieces),
            out_specs=pl.BlockSpec((rank, rows), lambda i, s: (0, 0)),
            scratch_shapes=[
                pltpu.VMEM((rows, width), jnp.bfloat16),
                pltpu.SemaphoreType.DMA((len(pieces),)),
            ],
        ),
        out_shape=jax.ShapeDtypeStruct((rank, rows), jnp.bfloat16),
        compiler_params=pltpu.CompilerParams(vmem_limit_bytes=40 * MIB),
        cost_estimate=pl.CostEstimate(
            flops=2 * rows * width * ranks, bytes_accessed=2 * (rows + ranks) * width, transcendentals=0
        ),
        name="shrink",
    )(place, row_adapter.reshape(1, rows), down, *pieces)


def project_kernel(columns, pieces, place, gate_weight_ref, up_weight_ref, *refs):
    piece_refs = refs[:pieces]
    gate_ref, up_ref, tokens_vmem, sems = refs[pieces:]
    depth = gate_weight_ref.shape[0]
    k = pl.program_id(0)

    @pl.when(k == 0)
    def _():
        assemble(place, columns, piece_refs, tokens_vmem, sems)
        gate_ref[...] = jnp.zeros_like(gate_ref)
        up_ref[...] = jnp.zeros_like(up_ref)

    tokens = tokens_vmem[:, pl.ds(pl.multiple_of(k * depth, depth), depth)]
    gate_ref[...] += jnp.dot(tokens, gate_weight_ref[...], preferred_element_type=jnp.float32)
    up_ref[...] += jnp.dot(tokens, up_weight_ref[...], preferred_element_type=jnp.float32)

    @pl.when(k == pl.num_programs(0) - 1)
    def _():
        gate = gate_ref[...]
        gate_ref[...] = gate / (1.0 + jnp.exp(-gate))


def project(place, columns, pieces, gate_weight, up_weight, rows):
    width, units = gate_weight.shape
    depth = min(1024, width)
    weight_spec = pl.BlockSpec((depth, units), lambda k, s: (k, 0))
    out_spec = pl.BlockSpec((rows, units), lambda k, s: (0, 0))
    out = jax.ShapeDtypeStruct((rows, units), jnp.float32)
    return pl.pallas_call(
        functools.partial(project_kernel, columns, len(pieces)),
        grid_spec=pltpu.PrefetchScalarGridSpec(
            num_scalar_prefetch=1,
            grid=(width // depth,),
            in_specs=[weight_spec, weight_spec] + [HBM_SPEC] * len(pieces),
            out_specs=[out_spec, out_spec],
            scratch_shapes=[
                pltpu.VMEM((rows, width), jnp.bfloat16),
                pltpu.SemaphoreType.DMA((len(pieces),)),
            ],
        ),
        out_shape=[out, out],
        compiler_params=pltpu.CompilerParams(vmem_limit_bytes=48 * MIB),
        cost_estimate=pl.CostEstimate(
            flops=4 * rows * width * units,
            bytes_accessed=2 * (rows + 2 * units) * width,
            transcendentals=rows * units,
        ),
        name="project",
    )(place, gate_weight, up_weight, *pieces)


def combine_kernel(pieces, users_ref, gate_ref, up_ref, maps_ref, *refs):
    piece_refs = refs[:pieces]
    out_ref, shrunk_vmem = refs[pieces:]
    rank, rows = piece_refs[0].shape

    @pl.when(pl.program_id(0) == 0)
    def _():
        total = piece_refs[0][...].astype(jnp.float32)
        for ref in piece_refs[1:]:
            total += ref[...].astype(jnp.float32)
        pair = jnp.transpose(jnp.concatenate([total, total], axis=0))
        users = users_ref[...]
        column = lax.broadcasted_iota(jnp.int32, pair.shape, 1)
        for start in range(0, shrunk_vmem.shape[1], 2 * rank):
            mine = users == (start + column) // rank
            shrunk_vmem[:, start : start + 2 * rank] = jnp.where(mine, pair, 0.0).astype(jnp.bfloat16)

    delta = jnp.dot(shrunk_vmem[...], maps_ref[...], preferred_element_type=jnp.float32)
    delta = (ADAPTER_SCALE * delta).astype(jnp.bfloat16).astype(jnp.float32)
    out_ref[...] = (gate_ref[...] * (up_ref[...] + delta)).astype(out_ref.dtype)


def combine(row_adapter, pieces, gate, up, maps):
    rows, units = gate.shape
    ranks_all = maps.shape[0]
    rank = pieces[0].shape[0]
    tile = min(512, units)
    users = jnp.broadcast_to(row_adapter[:, None], (rows, 2 * rank))
    column_spec = pl.BlockSpec((rows, tile), lambda n: (0, n))
    return pl.pallas_call(
        functools.partial(combine_kernel, len(pieces)),
        grid=(units // tile,),
        in_specs=[
            pl.BlockSpec((rows, 2 * rank), lambda n: (0, 0)),
            column_spec,
            column_spec,
            pl.BlockSpec((ranks_all, tile), lambda n: (0, n)),
        ]
        + [pl.BlockSpec((rank, rows), lambda n: (0, 0))] * len(pieces),
        out_specs=column_spec,
        scratch_shapes=[pltpu.VMEM((rows, ranks_all), jnp.bfloat16)],
        out_shape=jax.ShapeDtypeStruct((rows, units), jnp.bfloat16),
        compiler_params=pltpu.CompilerParams(vmem_limit_bytes=48 * MIB),
        cost_estimate=pl.CostEstimate(
            flops=2 * rows * ranks_all * units, bytes_accessed=10 * rows * units, transcendentals=0
        ),
        name="combine",
    )(users, gate, up, maps, *pieces)


def per_device(
    tokens,
    gate_weight,
    up_weight,
    adapter_down_weight,
    adapter_up_weight,
    row_adapter,
    sorted_rows,
    segment_count,
):
    axis = "tensor"
    size = lax.axis_size(axis)
    me = lax.axis_index(axis)
    resident, rank, width = adapter_down_weight.shape
    ranks = resident * rank
    rows = row_adapter.shape[0]

    found, where, own_maps = ring_gather(
        tokens, axis, adapter_up_weight.reshape(ranks, -1), lambda weights: split_columns(weights, size)
    )
    pieces = [piece for piece, _ in found]
    columns = [column for _, column in found]
    table = jnp.array([row + [device] for device, row in enumerate(where)], jnp.int32)
    place = lax.dynamic_index_in_dim(table, me, 0, keepdims=False)

    own_maps, pieces[-2], pieces[-4] = lax.optimization_barrier((own_maps, pieces[-2], pieces[-4]))
    maps = lax.all_to_all(own_maps, axis, split_axis=0, concat_axis=0, tiled=True)
    maps = maps.reshape(size * ranks, -1)

    shrunk = shrink(place, columns, pieces, row_adapter, adapter_down_weight.reshape(ranks, width), rank)
    near = min(4, size)
    plane = shrunk
    for flip in range(1, near):
        plane = plane + lax.ppermute(shrunk, axis, [(d, d ^ flip) for d in range(size)])
    shrunk_pieces = [plane]
    for shift in range(1, size // near):
        shrunk_pieces.append(
            lax.ppermute(plane, axis, [(d, (d + shift * near) % size) for d in range(size)])
        )
    gate, up = project(place, columns, pieces, gate_weight, up_weight, rows)
    return combine(row_adapter, shrunk_pieces, gate, up, maps)


def solution(mesh):
    placed = (
        P(("groups", "tensor"), None),
        P(None, "tensor"),
        P(None, "tensor"),
        P(("groups", "tensor"), None, None),
        P(("groups", "tensor"), None, None),
        P("groups"),
        P("groups"),
        P("groups"),
    )
    return jax.shard_map(
        per_device, mesh=mesh, in_specs=placed, out_specs=P("groups", "tensor"), check_vma=False
    )
```

time: 165 us -> 101 us (0.61)
  waiting for transfers between devices: 47.2 us -> 23.9 us
  Pallas kernels: 42.7 us -> 29 us
  starting transfers between devices: 39.2 us -> 26.4 us
  between operations: 11.8 us -> 0.22 us
  local copies, waits for them, and re-layouts: 22.9 us -> 20.5 us
    ppermute x8, waiting for transfers between devices: 45.7 us -> 19.1 us  [moved(): return lax.ppermute(value, axis, pairs)]
    ppermute x8, starting transfers between devices: 24.6 us -> 9.21 us  [moved(): return lax.ppermute(value, axis, pairs)]
    pallas_call x3, Pallas kernels: 17 us -> 9.37 us  [the longest x1 3.81 us: split_columns(): pl.pallas_call(split_kernel, grid=(parts // group,), in_specs=[pl.BlockSp...]
    pallas_call x2 -> x1, Pallas kernels: 25.7 us -> 19.6 us  [project(): pl.pallas_call(functools.partial(project_kernel, columns, len(pieces)), g...]
    ppermute x3, starting transfers between devices: 3.54 us -> 7.77 us  [per_device(): lax.ppermute(plane, axis, [(d, (d + shift * near) % size) for d in range(...]
    ppermute x3, waiting for transfers between devices: 0.01 us -> 4.02 us  [per_device(): lax.ppermute(shrunk, axis, [(d, d ^ flip) for d in range(size)])]
    all_to_all x1, starting transfers between devices: 7.53 us -> 4.81 us  [per_device(): lax.all_to_all(own_maps, axis, split_axis=0, concat_axis=0, tiled=True)]
    unnamed x68 -> x70, local copies, waits for them, and re-layouts: 20.1 us -> 19.7 us
  transfers between devices with their start and end apart: 24 -> 24, of which waited for: 5 -> 12; matrix products, arithmetic and copies ran while one was open for 2% -> 1% of each run, Pallas kernels for 18% -> 27%
where the time goes in v3:
time: 101 us; the launch traced here: 100 us
  Pallas kernels  29 us (29%)
  starting transfers between devices  26.4 us (26%)
  waiting for transfers between devices  23.9 us (24%)
  local copies, waits for them, and re-layouts  20.5 us (20%)
    unnamed x70, local copies, waits for them, and re-layouts  19.7 us
    pallas_call x1, Pallas kernels, project(): pl.pallas_call(functools.partial(project_kernel, columns, len(pieces)), g...  19.6 us
    ppermute x8, waiting for transfers between devices, moved(): return lax.ppermute(value, axis, pairs)  19.1 us
    ppermute x8, starting transfers between devices, moved(): return lax.ppermute(value, axis, pairs)  9.21 us
    ppermute x3, starting transfers between devices, per_device(): lax.ppermute(plane, axis, [(d, (d + shift * near) % size) for d in range(...  7.77 us
    all_to_all x1, starting transfers between devices, per_device(): lax.all_to_all(own_maps, axis, split_axis=0, concat_axis=0, tiled=True)  4.81 us
    ppermute x3, waiting for transfers between devices, per_device(): lax.ppermute(shrunk, axis, [(d, d ^ flip) for d in range(size)])  4.02 us
    pallas_call x1, Pallas kernels, split_columns(): pl.pallas_call(split_kernel, grid=(parts // group,), in_specs=[pl.BlockSp...  3.81 us
  transfers between devices with their start and end apart: 24, of which 12 were waited for; matrix products, arithmetic and copies ran while one was open for 1% of the time, Pallas kernels for 27%

profile of v3, /device:TPU:0, one launch (start us, length us, event | category | flops | bytes accessed | tf_op | source)
XLA Modules:
  0.0 100.1 jit_solution(4314710303157972068)
XLA Ops:
  0.0 3.0 %collective-permute-start.1 = (bf16[16,8192]{1,0:T(8,128)(2,1)}, bf16[16,8192]{1,0:T(8,128)(2,1)S(1)}, u32[]{:S(2)}, u32[]{:S(2)}) collective-permute-start(bf16[16,8192]{1,0:T(8,128)(2,1)} %refs_0_.3), channel_id=1, source_target_pairs={{0,4},{1,5},{4,8},{5,9},{8,12},{9,13},{12,14},{13,15},{14,10},{15,... | collective-permute-start | bytes 786440 | tf_op jit(solution)/shard_map/ppermute | solution.py:30
  3.0 6.5 %collective-permute-done.1.refs_2_ = bf16[16,8192]{1,0:T(8,128)(2,1)S(1)} collective-permute-done((bf16[16,8192]{1,0:T(8,128)(2,1)}, bf16[16,8192]{1,0:T(8,128)(2,1)S(1)}, u32[]{:S(2)}, u32[]{:S(2)}) %collective-permute-start.1) | collective-permute-done | bytes 262176 | tf_op jit(solution)/shard_map/ppermute | solution.py:30
  9.5 1.5 %collective-permute-done.3.refs_4_ = bf16[16,8192]{1,0:T(8,128)(2,1)S(1)} collective-permute-done((bf16[16,8192]{1,0:T(8,128)(2,1)}, bf16[16,8192]{1,0:T(8,128)(2,1)S(1)}, u32[]{:S(2)}, u32[]{:S(2)}) %collective-permute-start.3) | collective-permute-done | bytes 262176 | tf_op jit(solution)/shard_map/ppermute | solution.py:30
  11.0 1.6 %collective-permute-start.5 = (bf16[16,8192]{1,0:T(8,128)(2,1)S(1)}, bf16[16,8192]{1,0:T(8,128)(2,1)S(1)}, u32[]{:S(2)}, u32[]{:S(2)}) collective-permute-start(bf16[16,8192]{1,0:T(8,128)(2,1)S(1)} %collective-permute-done.1.refs_2_), channel_id=1, source_target_pairs={{0,4},{1,5},{4,8},{5,9},{8,12},{9,13},{12,14},{13,15},{14,10},{15,... | collective-permute-start | bytes 786440 | tf_op jit(solution)/shard_map/ppermute | solution.py:30
  13.0 3.8 %split_columns.1 = bf16[16,64,1024]{2,1,0:T(8,128)(2,1)} custom-call(bf16[64,16384]{1,0:T(8,128)(2,1)} %bitcast.9), custom_call_target="tpu_custom_call" | custom-call | tf_op jit(solution)/shard_map/split_columns/pallas_call | solution.py:91
  16.8 1.0 %collective-permute-done.5.refs_6_ = bf16[16,8192]{1,0:T(8,128)(2,1)S(1)} collective-permute-done((bf16[16,8192]{1,0:T(8,128)(2,1)S(1)}, bf16[16,8192]{1,0:T(8,128)(2,1)S(1)}, u32[]{:S(2)}, u32[]{:S(2)}) %collective-permute-start.5) | collective-permute-done | bytes 262176 | tf_op jit(solution)/shard_map/ppermute | solution.py:30
  17.9 1.3 %collective-permute-done.7.refs_8_ = bf16[16,8192]{1,0:T(8,128)(2,1)S(1)} collective-permute-done((bf16[16,8192]{1,0:T(8,128)(2,1)S(1)}, bf16[16,8192]{1,0:T(8,128)(2,1)S(1)}, u32[]{:S(2)}, u32[]{:S(2)}) %collective-permute-start.7) | collective-permute-done | bytes 262176 | tf_op jit(solution)/shard_map/ppermute | solution.py:30
  19.6 1.6 %collective-permute-start.9 = (bf16[16,8192]{1,0:T(8,128)(2,1)S(1)}, bf16[16,8192]{1,0:T(8,128)(2,1)S(1)}, u32[]{:S(2)}, u32[]{:S(2)}) collective-permute-start(bf16[16,8192]{1,0:T(8,128)(2,1)S(1)} %collective-permute-done.5.refs_6_), channel_id=1, source_target_pairs={{0,4},{1,5},{4,8},{5,9},{8,12},{9,13},{12,14},{13,15},{14,10},{15,... | collective-permute-start | bytes 786440 | tf_op jit(solution)/shard_map/ppermute | solution.py:30
  21.2 5.3 %collective-permute-done.11.refs_12_ = bf16[16,8192]{1,0:T(8,128)(2,1)S(1)} collective-permute-done((bf16[16,8192]{1,0:T(8,128)(2,1)S(1)}, bf16[16,8192]{1,0:T(8,128)(2,1)S(1)}, u32[]{:S(2)}, u32[]{:S(2)}) %collective-permute-start.11) | collective-permute-done | bytes 262176 | tf_op jit(solution)/shard_map/ppermute | solution.py:30
  27.2 1.6 %collective-permute-start.14 = (bf16[16,4096]{1,0:T(8,128)(2,1)S(1)}, bf16[16,4096]{1,0:T(8,128)(2,1)S(1)}, u32[]{:S(2)}, u32[]{:S(2)}) collective-permute-start(bf16[16,4096]{1,0:T(8,128)(2,1)S(1)} %slice.9), channel_id=1, source_target_pairs={{0,4},{1,5},{4,8},{5,9},{8,12},{9,13},{12,14},{13,15},{14,10},{15,... | collective-permute-start | bytes 393224 | tf_op jit(solution)/shard_map/ppermute | solution.py:30
  28.8 2.7 %collective-permute-done.13.refs_16_ = bf16[16,4096]{1,0:T(8,128)(2,1)S(1)} collective-permute-done((bf16[16,4096]{1,0:T(8,128)(2,1)S(1)}, bf16[16,4096]{1,0:T(8,128)(2,1)S(1)}, u32[]{:S(2)}, u32[]{:S(2)}) %collective-permute-start.13) | collective-permute-done | bytes 131104 | tf_op jit(solution)/shard_map/ppermute | solution.py:30
  32.9 4.8 %all-to-all-start = ((bf16[16,64,1024]{2,1,0:T(8,128)(2,1)}), bf16[16,64,1024]{2,1,0:T(8,128)(2,1)S(1)}, u32[]{:S(2)}, u32[]{:S(2)}) async-start(bf16[16,64,1024]{2,1,0:T(8,128)(2,1)} %split_columns.1), calls=%async_computation | async-start | bytes 4194304 | tf_op jit(solution)/shard_map/all_to_all | solution.py:276
  44.6 0.9 copy-done.2
  45.5 0.9 copy-done.5
  46.5 0.9 copy-done.8
  47.4 0.9 copy-done.11
  48.4 0.9 copy-done.14
  49.3 0.9 copy-done.17
  50.3 1.2 %copy-done.22 = bf16[1,64,8192]{2,1,0:T(8,128)(2,1)S(1)} copy-done((bf16[1,64,8192]{2,1,0:T(8,128)(2,1)S(1)}, bf16[1,64,8192]{2,1,0:T(8,128)(2,1)}, u32[]{:S(2)}) %copy-start.22) | copy-done | bytes 1048600
  51.5 0.9 copy-done.24
  52.5 3.4 %shrink.1 = bf16[64,256]{1,0:T(8,128)(2,1)S(1)} custom-call(s32[19]{0:T(128)S(1)} %dynamic-slice_bitcast_fusion.place, s32[1,256]{1,0:T(1,128)S(1)} %bitcast.8, bf16[64,8192]{1,0:T(8,128)(2,1)S(1)} %bitcast.7, bf16[16,8192]{1,0:T(8,128)(2,1)S(1)} %copy-done, bf16[16,8192]{1,0:T(8,128)(2,1)S(1)} %copy-done.8, ...), custom_call_target="tpu_custom_call" | custom-call | flops 268435456 | bytes 5242880 | tf_op jit(solution)/shard_map/shrink/pallas_call | solution.py:124
  56.1 1.9 %collective-permute-start.18 = (bf16[64,256]{1,0:T(8,128)(2,1)S(1)}, bf16[64,256]{1,0:T(8,128)(2,1)S(1)}, u32[]{:S(2)}, u32[]{:S(2)}) collective-permute-start(bf16[64,256]{1,0:T(8,128)(2,1)S(1)} %shrink.1), channel_id=1, source_target_pairs={{0,2},{1,3},{2,0},{3,1},{4,6},{5,7},{6,4},{7,5},{8,10},{9,11},{10,... | collective-permute-start | bytes 98312 | tf_op jit(solution)/shard_map/ppermute | solution.py:283
  58.0 3.4 %collective-permute-done.18 = bf16[64,256]{1,0:T(8,128)(2,1)S(1)} collective-permute-done((bf16[64,256]{1,0:T(8,128)(2,1)S(1)}, bf16[64,256]{1,0:T(8,128)(2,1)S(1)}, u32[]{:S(2)}, u32[]{:S(2)}) %collective-permute-start.18) | collective-permute-done | bytes 32800 | tf_op jit(solution)/shard_map/ppermute | solution.py:283
  62.0 2.0 %collective-permute-start.20 = (bf16[64,256]{1,0:T(8,128)(2,1)S(1)}, bf16[64,256]{1,0:T(8,128)(2,1)S(1)}, u32[]{:S(2)}, u32[]{:S(2)}) collective-permute-start(bf16[64,256]{1,0:T(8,128)(2,1)S(1)} %add_add_fusion.refs_0_), channel_id=1, source_target_pairs={{0,4},{1,5},{2,6},{3,7},{4,8},{5,9},{6,10},{7,11},{8,12},{9,13},{1... | collective-permute-start | bytes 98312 | tf_op jit(solution)/shard_map/ppermute | solution.py:287
  64.0 3.7 %collective-permute-start.21 = (bf16[64,256]{1,0:T(8,128)(2,1)S(1)}, bf16[64,256]{1,0:T(8,128)(2,1)S(1)}, u32[]{:S(2)}, u32[]{:S(2)}) collective-permute-start(bf16[64,256]{1,0:T(8,128)(2,1)S(1)} %add_add_fusion.refs_0_), channel_id=1, source_target_pairs={{0,8},{1,9},{2,10},{3,11},{4,12},{5,13},{6,14},{7,15},{8,0},{9,1},... | collective-permute-start | bytes 98312 | tf_op jit(solution)/shard_map/ppermute | solution.py:287
  67.7 2.1 %collective-permute-start.22 = (bf16[64,256]{1,0:T(8,128)(2,1)S(1)}, bf16[64,256]{1,0:T(8,128)(2,1)S(1)}, u32[]{:S(2)}, u32[]{:S(2)}) collective-permute-start(bf16[64,256]{1,0:T(8,128)(2,1)S(1)} %add_add_fusion.refs_0_), channel_id=1, source_target_pairs={{0,12},{1,13},{2,14},{3,15},{4,0},{5,1},{6,2},{7,3},{8,4},{9,5},{1... | collective-permute-start | bytes 98312 | tf_op jit(solution)/shard_map/ppermute | solution.py:287
  69.9 19.6 %project.1 = (f32[256,1024]{1,0:T(8,128)S(1)}, f32[256,1024]{1,0:T(8,128)}) custom-call(s32[19]{0:T(128)S(1)} %dynamic-slice_bitcast_fusion.place, bf16[8192,1024]{1,0:T(8,128)(2,1)} %gate_weight_ref.1, bf16[8192,1024]{1,0:T(8,128)(2,1)} %up_weight_ref.1, bf16[16,8192]{1,0:T(8,128)(2,1)S(1)} %copy-done, bf16[16,8192]{1,0:T(8,128)(2,1)S(1)} %copy-done.9, ...), custom_call_target="tpu_custom_call" | custom-call | flops 8589934592 | bytes 37748736 | tf_op jit(solution)/shard_map/project/pallas_call | solution.py:177
  89.5 1.0 copy-done.19
  92.4 1.2 %copy-done.20 = f32[256,1024]{1,0:T(8,128)S(1)} copy-done((f32[256,1024]{1,0:T(8,128)S(1)}, f32[256,1024]{1,0:T(8,128)}, u32[]{:S(2)}) %copy-start.20) | copy-done | bytes 1048600
  93.7 1.2 %copy-done.21 = f32[256,1024]{1,0:T(8,128)S(1)} copy-done((f32[256,1024]{1,0:T(8,128)S(1)}, f32[256,1024]{1,0:T(8,128)}, u32[]{:S(2)}) %copy-start.21) | copy-done | bytes 1048600
  94.9 0.8 copy-done.27
  97.9 2.1 %combine.1 = bf16[256,1024]{1,0:T(8,128)(2,1)} custom-call(s32[256,128]{1,0:T(8,128)S(1)} %broadcast_in_dim.2.users_ref, f32[256,1024]{1,0:T(8,128)S(1)} %copy-done.20, f32[256,1024]{1,0:T(8,128)S(1)} %copy-done.21, bf16[1024,1024]{1,0:T(8,128)(2,1)S(1)} %bitcast.6, bf16[64,256]{1,0:T(8,128)(2,1)S(1)} %copy-done.27, bf16[64,256]{1,0:T(8,128)(2,1)S(1)} %copy-done.29, ...), custom_call_target="tpu_custom_call" | custom-call | flops 536870912 | bytes 2621440 | tf_op jit(solution)/shard_map/combine/pallas_call | solution.py:229
  (95 shorter events, 14.8 us)
Async XLA Ops:
  0.0 9.5 %collective-permute-start.1 = (bf16[16,8192]{1,0:T(8,128)(2,1)}, bf16[16,8192]{1,0:T(8,128)(2,1)S(1)}, u32[]{:S(2)}, u32[]{:S(2)}) collective-permute-start(bf16[16,8192]{1,0:T(8,128)(2,1)} %refs_0_.3), channel_id=1, source_target_pairs={{0,4},{1,5},{4,8},{5,9},{8,12},{9,13},{12,14},{13,15},{14,10},{15,... | collective-permute-start | bytes 786440 | tf_op jit(solution)/shard_map/ppermute | solution.py:30
  3.0 8.0 %collective-permute-start.3 = (bf16[16,8192]{1,0:T(8,128)(2,1)}, bf16[16,8192]{1,0:T(8,128)(2,1)S(1)}, u32[]{:S(2)}, u32[]{:S(2)}) collective-permute-start(bf16[16,8192]{1,0:T(8,128)(2,1)} %refs_0_.3), channel_id=1, source_target_pairs={{0,2},{1,3},{4,0},{5,1},{8,4},{9,5},{12,8},{13,9},{14,12},{15,13},... | collective-permute-start | bytes 786440 | tf_op jit(solution)/shard_map/ppermute | solution.py:30
  11.0 6.9 %collective-permute-start.5 = (bf16[16,8192]{1,0:T(8,128)(2,1)S(1)}, bf16[16,8192]{1,0:T(8,128)(2,1)S(1)}, u32[]{:S(2)}, u32[]{:S(2)}) collective-permute-start(bf16[16,8192]{1,0:T(8,128)(2,1)S(1)} %collective-permute-done.1.refs_2_), channel_id=1, source_target_pairs={{0,4},{1,5},{4,8},{5,9},{8,12},{9,13},{12,14},{13,15},{14,10},{15,... | collective-permute-start | bytes 786440 | tf_op jit(solution)/shard_map/ppermute | solution.py:30
  12.6 6.6 %collective-permute-start.7 = (bf16[16,8192]{1,0:T(8,128)(2,1)S(1)}, bf16[16,8192]{1,0:T(8,128)(2,1)S(1)}, u32[]{:S(2)}, u32[]{:S(2)}) collective-permute-start(bf16[16,8192]{1,0:T(8,128)(2,1)S(1)} %collective-permute-done.3.refs_4_), channel_id=1, source_target_pairs={{0,2},{1,3},{4,0},{5,1},{8,4},{9,5},{12,8},{13,9},{14,12},{15,13},... | collective-permute-start | bytes 786440 | tf_op jit(solution)/shard_map/ppermute | solution.py:30
  19.2 7.3 %collective-permute-start.11 = (bf16[16,8192]{1,0:T(8,128)(2,1)S(1)}, bf16[16,8192]{1,0:T(8,128)(2,1)S(1)}, u32[]{:S(2)}, u32[]{:S(2)}) collective-permute-start(bf16[16,8192]{1,0:T(8,128)(2,1)S(1)} %collective-permute-done.7.refs_8_), channel_id=1, source_target_pairs={{0,2},{1,3},{4,0},{5,1},{8,4},{9,5},{12,8},{13,9},{14,12},{15,13},... | collective-permute-start | bytes 786440 | tf_op jit(solution)/shard_map/ppermute | solution.py:30
  19.6 7.5 %collective-permute-start.9 = (bf16[16,8192]{1,0:T(8,128)(2,1)S(1)}, bf16[16,8192]{1,0:T(8,128)(2,1)S(1)}, u32[]{:S(2)}, u32[]{:S(2)}) collective-permute-start(bf16[16,8192]{1,0:T(8,128)(2,1)S(1)} %collective-permute-done.5.refs_6_), channel_id=1, source_target_pairs={{0,4},{1,5},{4,8},{5,9},{8,12},{9,13},{12,14},{13,15},{14,10},{15,... | collective-permute-start | bytes 786440 | tf_op jit(solution)/shard_map/ppermute | solution.py:30
  26.5 5.0 %collective-permute-start.13 = (bf16[16,4096]{1,0:T(8,128)(2,1)S(1)}, bf16[16,4096]{1,0:T(8,128)(2,1)S(1)}, u32[]{:S(2)}, u32[]{:S(2)}) collective-permute-start(bf16[16,4096]{1,0:T(8,128)(2,1)S(1)} %slice.8), channel_id=1, source_target_pairs={{0,2},{1,3},{4,0},{5,1},{8,4},{9,5},{12,8},{13,9},{14,12},{15,13},... | collective-permute-start | bytes 393224 | tf_op jit(solution)/shard_map/ppermute | solution.py:30
  27.2 17.4 %copy-start.34 = (s32[256]{0:T(256)S(1)}, s32[256]{0:T(256)}, u32[]{:S(2)}) copy-start(s32[256]{0:T(256)} %param.14) | copy-start | bytes 3076
  27.2 5.0 %collective-permute-start.14 = (bf16[16,4096]{1,0:T(8,128)(2,1)S(1)}, bf16[16,4096]{1,0:T(8,128)(2,1)S(1)}, u32[]{:S(2)}, u32[]{:S(2)}) collective-permute-start(bf16[16,4096]{1,0:T(8,128)(2,1)S(1)} %slice.9), channel_id=1, source_target_pairs={{0,4},{1,5},{4,8},{5,9},{8,12},{9,13},{12,14},{13,15},{14,10},{15,... | collective-permute-start | bytes 393224 | tf_op jit(solution)/shard_map/ppermute | solution.py:30
  32.9 59.5 %all-to-all-start = ((bf16[16,64,1024]{2,1,0:T(8,128)(2,1)}), bf16[16,64,1024]{2,1,0:T(8,128)(2,1)S(1)}, u32[]{:S(2)}, u32[]{:S(2)}) async-start(bf16[16,64,1024]{2,1,0:T(8,128)(2,1)} %split_columns.1), calls=%async_computation | async-start | bytes 4194304 | tf_op jit(solution)/shard_map/all_to_all | solution.py:276
  37.7 1.6 %collective-permute-start = (bf16[16,8192]{1,0:T(8,128)(2,1)S(1)}, bf16[16,8192]{1,0:T(8,128)(2,1)S(1)}, u32[]{:S(2)}, u32[]{:S(2)}) collective-permute-start(bf16[16,8192]{1,0:T(8,128)(2,1)S(1)} %copy-done), channel_id=1, source_target_pairs={{0,1},{1,0},{2,3},{3,2},{4,5},{5,4},{6,7},{7,6},{8,9},{9,8},{10,11... | collective-permute-start | bytes 786440 | tf_op jit(solution)/shard_map/ppermute | solution.py:33
  38.2 2.2 %collective-permute-start.2 = (bf16[16,8192]{1,0:T(8,128)(2,1)S(1)}, bf16[16,8192]{1,0:T(8,128)(2,1)S(1)}, u32[]{:S(2)}, u32[]{:S(2)}) collective-permute-start(bf16[16,8192]{1,0:T(8,128)(2,1)S(1)} %collective-permute-done.1.refs_2_), channel_id=1, source_target_pairs={{0,1},{1,0},{2,3},{3,2},{4,5},{5,4},{6,7},{7,6},{8,9},{9,8},{10,11... | collective-permute-start | bytes 786440 | tf_op jit(solution)/shard_map/ppermute | solution.py:33
  38.3 3.0 %collective-permute-start.4 = (bf16[16,8192]{1,0:T(8,128)(2,1)S(1)}, bf16[16,8192]{1,0:T(8,128)(2,1)S(1)}, u32[]{:S(2)}, u32[]{:S(2)}) collective-permute-start(bf16[16,8192]{1,0:T(8,128)(2,1)S(1)} %collective-permute-done.3.refs_4_), channel_id=1, source_target_pairs={{0,1},{1,0},{2,3},{3,2},{4,5},{5,4},{6,7},{7,6},{8,9},{9,8},{10,11... | collective-permute-start | bytes 786440 | tf_op jit(solution)/shard_map/ppermute | solution.py:33
  38.7 3.7 %collective-permute-start.6 = (bf16[16,8192]{1,0:T(8,128)(2,1)}, bf16[16,8192]{1,0:T(8,128)(2,1)S(1)}, u32[]{:S(2)}, u32[]{:S(2)}) collective-permute-start(bf16[16,8192]{1,0:T(8,128)(2,1)} %copy-done.1), channel_id=1, source_target_pairs={{0,1},{1,0},{2,3},{3,2},{4,5},{5,4},{6,7},{7,6},{8,9},{9,8},{10,11... | collective-permute-start | bytes 786440 | tf_op jit(solution)/shard_map/ppermute | solution.py:33
  38.8 5.1 %collective-permute-start.8 = (bf16[16,8192]{1,0:T(8,128)(2,1)}, bf16[16,8192]{1,0:T(8,128)(2,1)}, u32[]{:S(2)}, u32[]{:S(2)}) collective-permute-start(bf16[16,8192]{1,0:T(8,128)(2,1)} %copy-done.4), channel_id=1, source_target_pairs={{0,1},{1,0},{2,3},{3,2},{4,5},{5,4},{6,7},{7,6},{8,9},{9,8},{10,11... | collective-permute-start | bytes 786440 | tf_op jit(solution)/shard_map/ppermute | solution.py:33
  40.0 4.5 %collective-permute-start.10 = (bf16[16,8192]{1,0:T(8,128)(2,1)S(1)}, bf16[16,8192]{1,0:T(8,128)(2,1)}, u32[]{:S(2)}, u32[]{:S(2)}) collective-permute-start(bf16[16,8192]{1,0:T(8,128)(2,1)S(1)} %collective-permute-done.9.refs_10_), channel_id=1, source_target_pairs={{0,1},{1,0},{2,3},{3,2},{4,5},{5,4},{6,7},{7,6},{8,9},{9,8},{10,11... | collective-permute-start | bytes 786440 | tf_op jit(solution)/shard_map/ppermute | solution.py:33
  41.1 3.5 %collective-permute-start.12 = (bf16[16,8192]{1,0:T(8,128)(2,1)S(1)}, bf16[16,8192]{1,0:T(8,128)(2,1)}, u32[]{:S(2)}, u32[]{:S(2)}) collective-permute-start(bf16[16,8192]{1,0:T(8,128)(2,1)S(1)} %collective-permute-done.11.refs_12_), channel_id=1, source_target_pairs={{0,1},{1,0},{2,3},{3,2},{4,5},{5,4},{6,7},{7,6},{8,9},{9,8},{10,11... | collective-permute-start | bytes 786440 | tf_op jit(solution)/shard_map/ppermute | solution.py:33
  42.0 1.9 %collective-permute-start.15 = (bf16[16,4096]{1,0:T(8,128)(2,1)}, bf16[16,4096]{1,0:T(8,128)(2,1)}, u32[]{:S(2)}, u32[]{:S(2)}) collective-permute-start(bf16[16,4096]{1,0:T(8,128)(2,1)} %copy-done.23), channel_id=1, source_target_pairs={{0,1},{1,0},{2,3},{3,2},{4,5},{5,4},{6,7},{7,6},{8,9},{9,8},{10,11... | collective-permute-start | bytes 393224 | tf_op jit(solution)/shard_map/ppermute | solution.py:33
  43.1 1.5 %collective-permute-start.16 = (bf16[16,4096]{1,0:T(8,128)(2,1)S(1)}, bf16[16,4096]{1,0:T(8,128)(2,1)}, u32[]{:S(2)}, u32[]{:S(2)}) collective-permute-start(bf16[16,4096]{1,0:T(8,128)(2,1)S(1)} %collective-permute-done.13.refs_16_), channel_id=1, source_target_pairs={{0,1},{1,0},{2,3},{3,2},{4,5},{5,4},{6,7},{7,6},{8,9},{9,8},{10,11... | collective-permute-start | bytes 393224 | tf_op jit(solution)/shard_map/ppermute | solution.py:33
  52.4 17.4 %copy-start.6 = (bf16[16,8192]{1,0:T(8,128)(2,1)S(1)}, bf16[16,8192]{1,0:T(8,128)(2,1)}, u32[]{:S(2)}) copy-start(bf16[16,8192]{1,0:T(8,128)(2,1)} %copy-done.4) | copy-start | bytes 786436
  52.4 17.4 %copy-start.9 = (bf16[16,8192]{1,0:T(8,128)(2,1)S(1)}, bf16[16,8192]{1,0:T(8,128)(2,1)}, u32[]{:S(2)}) copy-start(bf16[16,8192]{1,0:T(8,128)(2,1)} %copy-done.7) | copy-start | bytes 786436
  52.4 17.4 %copy-start.12 = (bf16[16,8192]{1,0:T(8,128)(2,1)S(1)}, bf16[16,8192]{1,0:T(8,128)(2,1)}, u32[]{:S(2)}) copy-start(bf16[16,8192]{1,0:T(8,128)(2,1)} %copy-done.10) | copy-start | bytes 786436
  52.4 17.4 %copy-start.15 = (bf16[16,8192]{1,0:T(8,128)(2,1)S(1)}, bf16[16,8192]{1,0:T(8,128)(2,1)}, u32[]{:S(2)}) copy-start(bf16[16,8192]{1,0:T(8,128)(2,1)} %copy-done.13) | copy-start | bytes 786436
  52.4 17.4 %copy-start.18 = (bf16[16,8192]{1,0:T(8,128)(2,1)S(1)}, bf16[16,8192]{1,0:T(8,128)(2,1)}, u32[]{:S(2)}) copy-start(bf16[16,8192]{1,0:T(8,128)(2,1)} %copy-done.16) | copy-start | bytes 786436
  52.5 17.4 %copy-start.25 = (bf16[16,4096]{1,0:T(8,128)(2,1)S(1)}, bf16[16,4096]{1,0:T(8,128)(2,1)}, u32[]{:S(2)}) copy-start(bf16[16,4096]{1,0:T(8,128)(2,1)} %copy-done.23) | copy-start | bytes 393220
  55.9 2.1 %collective-permute-start.17 = (bf16[64,256]{1,0:T(8,128)(2,1)S(1)}, bf16[64,256]{1,0:T(8,128)(2,1)S(1)}, u32[]{:S(2)}, u32[]{:S(2)}) collective-permute-start(bf16[64,256]{1,0:T(8,128)(2,1)S(1)} %shrink.1), channel_id=1, source_target_pairs={{0,1},{1,0},{2,3},{3,2},{4,5},{5,4},{6,7},{7,6},{8,9},{9,8},{10,11... | collective-permute-start | bytes 98312 | tf_op jit(solution)/shard_map/ppermute | solution.py:283
  56.1 5.3 %collective-permute-start.18 = (bf16[64,256]{1,0:T(8,128)(2,1)S(1)}, bf16[64,256]{1,0:T(8,128)(2,1)S(1)}, u32[]{:S(2)}, u32[]{:S(2)}) collective-permute-start(bf16[64,256]{1,0:T(8,128)(2,1)S(1)} %shrink.1), channel_id=1, source_target_pairs={{0,2},{1,3},{2,0},{3,1},{4,6},{5,7},{6,4},{7,5},{8,10},{9,11},{10,... | collective-permute-start | bytes 98312 | tf_op jit(solution)/shard_map/ppermute | solution.py:283
  58.0 4.0 %collective-permute-start.19 = (bf16[64,256]{1,0:T(8,128)(2,1)S(1)}, bf16[64,256]{1,0:T(8,128)(2,1)S(1)}, u32[]{:S(2)}, u32[]{:S(2)}) collective-permute-start(bf16[64,256]{1,0:T(8,128)(2,1)S(1)} %shrink.1), channel_id=1, source_target_pairs={{0,3},{1,2},{2,1},{3,0},{4,7},{5,6},{6,5},{7,4},{8,11},{9,10},{10,... | collective-permute-start | bytes 98312 | tf_op jit(solution)/shard_map/ppermute | solution.py:283
  62.0 27.5 %copy-start.26 = (bf16[64,256]{1,0:T(8,128)(2,1)}, bf16[64,256]{1,0:T(8,128)(2,1)S(1)}, u32[]{:S(2)}) copy-start(bf16[64,256]{1,0:T(8,128)(2,1)S(1)} %add_add_fusion.refs_0_) | copy-start | bytes 98308
  62.0 28.4 %collective-permute-start.20 = (bf16[64,256]{1,0:T(8,128)(2,1)S(1)}, bf16[64,256]{1,0:T(8,128)(2,1)S(1)}, u32[]{:S(2)}, u32[]{:S(2)}) collective-permute-start(bf16[64,256]{1,0:T(8,128)(2,1)S(1)} %add_add_fusion.refs_0_), channel_id=1, source_target_pairs={{0,4},{1,5},{2,6},{3,7},{4,8},{5,9},{6,10},{7,11},{8,12},{9,13},{1... | collective-permute-start | bytes 98312 | tf_op jit(solution)/shard_map/ppermute | solution.py:287
  64.0 27.1 %collective-permute-start.21 = (bf16[64,256]{1,0:T(8,128)(2,1)S(1)}, bf16[64,256]{1,0:T(8,128)(2,1)S(1)}, u32[]{:S(2)}, u32[]{:S(2)}) collective-permute-start(bf16[64,256]{1,0:T(8,128)(2,1)S(1)} %add_add_fusion.refs_0_), channel_id=1, source_target_pairs={{0,8},{1,9},{2,10},{3,11},{4,12},{5,13},{6,14},{7,15},{8,0},{9,1},... | collective-permute-start | bytes 98312 | tf_op jit(solution)/shard_map/ppermute | solution.py:287
  67.7 24.0 %collective-permute-start.22 = (bf16[64,256]{1,0:T(8,128)(2,1)S(1)}, bf16[64,256]{1,0:T(8,128)(2,1)S(1)}, u32[]{:S(2)}, u32[]{:S(2)}) collective-permute-start(bf16[64,256]{1,0:T(8,128)(2,1)S(1)} %add_add_fusion.refs_0_), channel_id=1, source_target_pairs={{0,12},{1,13},{2,14},{3,15},{4,0},{5,1},{6,2},{7,3},{8,4},{9,5},{1... | collective-permute-start | bytes 98312 | tf_op jit(solution)/shard_map/ppermute | solution.py:287
  (27 other events, 75.0 us)

commit v4 on v3

--- a/solution.py
+++ b/solution.py
@@ -16,7 +16,7 @@
     return list(range(0, chips, 2)) + list(range(chips - 1, 0, -2))
 
 
-def ring_gather(block, axis, extra, prepare):
+def ring_gather(block, axis, beside):
     size = lax.axis_size(axis)
     chips = size // CORES
     ring = chip_ring(chips)
@@ -46,20 +46,17 @@
     arrived(block, 0, 0)
     right = left = block
     for step in range(1, chips // 2):
-        if step == 2:
-            extra, right, left = lax.optimization_barrier((extra, right, left))
-            extra = prepare(extra)
-        if step == 3:
-            extra, right, left = lax.optimization_barrier((extra, right, left))
         right = moved(right, 1)
         left = moved(left, -1)
+        right, left = beside(step, (right, left))
         arrived(right, 0, -step)
         arrived(left, 0, step)
     half = block.shape[1] // 2
     far = chips // 2
-    arrived(moved(right[:, :half], 1), 0, far)
-    arrived(moved(left[:, half:], -1), half, far)
-    return pieces, where, extra
+    ends = beside(far, (moved(right[:, :half], 1), moved(left[:, half:], -1)))
+    arrived(ends[0], 0, far)
+    arrived(ends[1], half, far)
+    return pieces, where
 
 
 def assemble(spots, columns, piece_refs, tokens_vmem, sems):
@@ -78,27 +75,37 @@
         copy.wait()
 
 
-def split_kernel(in_ref, out_ref):
-    width = out_ref.shape[2]
-    for part in range(out_ref.shape[0]):
-        out_ref[part] = in_ref[:, part * width : (part + 1) * width]
-
-
-def split_columns(weights, parts):
-    rows, columns = weights.shape
-    width = columns // parts
-    group = min(4, parts)
+ANY_SPEC = pl.BlockSpec(memory_space=pl.ANY)
+
+
+def cut_kernel(parts, units, me, maps_ref, *refs):
+    outs, sems = refs[:-1], refs[-1]
+    copies = []
+    for i, part in enumerate(parts):
+        start = pl.multiple_of((me[0] ^ part) * units, units)
+        copies.append(pltpu.make_async_copy(maps_ref.at[:, pl.ds(start, units)], outs[i], sems.at[i]))
+    for copy in copies:
+        copy.start()
+    for copy in copies:
+        copy.wait()
+
+
+def cut_columns(me, maps, parts, size):
+    ranks, columns = maps.shape
+    units = columns // size
     return pl.pallas_call(
-        split_kernel,
-        grid=(parts // group,),
-        in_specs=[pl.BlockSpec((rows, group * width), lambda i: (0, i))],
-        out_specs=pl.BlockSpec((group, rows, width), lambda i: (i, 0, 0)),
-        out_shape=jax.ShapeDtypeStruct((parts, rows, width), weights.dtype),
-        name="split_columns",
-    )(weights)
-
-
-HBM_SPEC = pl.BlockSpec(memory_space=pltpu.HBM)
+        functools.partial(cut_kernel, parts, units),
+        grid_spec=pltpu.PrefetchScalarGridSpec(
+            num_scalar_prefetch=1,
+            grid=(1,),
+            in_specs=[ANY_SPEC],
+            out_specs=[ANY_SPEC] * len(parts),
+            scratch_shapes=[pltpu.SemaphoreType.DMA((len(parts),))],
+        ),
+        out_shape=[jax.ShapeDtypeStruct((ranks, units), maps.dtype)] * len(parts),
+        cost_estimate=pl.CostEstimate(flops=0, bytes_accessed=4 * ranks * columns, transcendentals=0),
+        name="cut_columns",
+    )(me, maps)
 
 
 def shrink_kernel(columns, pieces, rank, place, users_ref, down_ref, *refs):
@@ -130,7 +137,7 @@
                 pl.BlockSpec((1, rows), lambda i, s: (0, 0)),
                 pl.BlockSpec((ranks, width), lambda i, s: (0, 0)),
             ]
-            + [HBM_SPEC] * len(pieces),
+            + [ANY_SPEC] * len(pieces),
             out_specs=pl.BlockSpec((rank, rows), lambda i, s: (0, 0)),
             scratch_shapes=[
                 pltpu.VMEM((rows, width), jnp.bfloat16),
@@ -138,7 +145,7 @@
             ],
         ),
         out_shape=jax.ShapeDtypeStruct((rank, rows), jnp.bfloat16),
-        compiler_params=pltpu.CompilerParams(vmem_limit_bytes=40 * MIB),
+        compiler_params=pltpu.CompilerParams(vmem_limit_bytes=rows * width * 2 + 8 * MIB),
         cost_estimate=pl.CostEstimate(
             flops=2 * rows * width * ranks, bytes_accessed=2 * (rows + ranks) * width, transcendentals=0
         ),
@@ -179,7 +186,7 @@
         grid_spec=pltpu.PrefetchScalarGridSpec(
             num_scalar_prefetch=1,
             grid=(width // depth,),
-            in_specs=[weight_spec, weight_spec] + [HBM_SPEC] * len(pieces),
+            in_specs=[weight_spec, weight_spec] + [ANY_SPEC] * len(pieces),
             out_specs=[out_spec, out_spec],
             scratch_shapes=[
                 pltpu.VMEM((rows, width), jnp.bfloat16),
@@ -187,7 +194,7 @@
             ],
         ),
         out_shape=[out, out],
-        compiler_params=pltpu.CompilerParams(vmem_limit_bytes=48 * MIB),
+        compiler_params=pltpu.CompilerParams(vmem_limit_bytes=rows * width * 2 + 20 * MIB),
         cost_estimate=pl.CostEstimate(
             flops=4 * rows * width * units,
             bytes_accessed=2 * (rows + 2 * units) * width,
@@ -197,54 +204,79 @@
     )(place, gate_weight, up_weight, *pieces)
 
 
-def combine_kernel(pieces, users_ref, gate_ref, up_ref, maps_ref, *refs):
-    piece_refs = refs[:pieces]
-    out_ref, shrunk_vmem = refs[pieces:]
+def combine_kernel(parts, shrunk_pieces, me, users_ref, gate_ref, up_ref, own_ref, *refs):
+    part_refs = refs[: len(parts)]
+    piece_refs = refs[len(parts) : len(parts) + shrunk_pieces]
+    out_ref, shrunk_vmem, maps_vmem, sems = refs[len(parts) + shrunk_pieces :]
     rank, rows = piece_refs[0].shape
-
-    @pl.when(pl.program_id(0) == 0)
+    ranks, units = part_refs[0].shape
+    resident = ranks // rank
+    tile = out_ref.shape[1]
+    n = pl.program_id(0)
+
+    @pl.when(n == 0)
     def _():
+        start = pl.multiple_of(me[0] * units, units)
+        copies = [pltpu.make_async_copy(own_ref.at[:, pl.ds(start, units)], maps_vmem.at[pl.ds(0, ranks)], sems.at[0])]
+        for i, ref in enumerate(part_refs):
+            copies.append(
+                pltpu.make_async_copy(ref, maps_vmem.at[pl.ds((i + 1) * ranks, ranks)], sems.at[i + 1])
+            )
+        for copy in copies:
+            copy.start()
         total = piece_refs[0][...].astype(jnp.float32)
         for ref in piece_refs[1:]:
             total += ref[...].astype(jnp.float32)
         pair = jnp.transpose(jnp.concatenate([total, total], axis=0))
         users = users_ref[...]
-        column = lax.broadcasted_iota(jnp.int32, pair.shape, 1)
-        for start in range(0, shrunk_vmem.shape[1], 2 * rank):
-            mine = users == (start + column) // rank
-            shrunk_vmem[:, start : start + 2 * rank] = jnp.where(mine, pair, 0.0).astype(jnp.bfloat16)
-
-    delta = jnp.dot(shrunk_vmem[...], maps_ref[...], preferred_element_type=jnp.float32)
+        first = lax.broadcasted_iota(jnp.int32, pair.shape, 1) < rank
+        adapters = [(me[0] ^ part) * resident + r for part in (0,) + parts for r in range(resident)]
+        for i in range(0, len(adapters), 2):
+            mine = users == jnp.where(first, adapters[i], adapters[i + 1])
+            shrunk_vmem[:, i * rank : (i + 2) * rank] = jnp.where(mine, pair, 0.0).astype(jnp.bfloat16)
+        for copy in copies:
+            copy.wait()
+
+    maps = maps_vmem[:, pl.ds(pl.multiple_of(n * tile, tile), tile)]
+    delta = jnp.dot(shrunk_vmem[...], maps, preferred_element_type=jnp.float32)
     delta = (ADAPTER_SCALE * delta).astype(jnp.bfloat16).astype(jnp.float32)
     out_ref[...] = (gate_ref[...] * (up_ref[...] + delta)).astype(out_ref.dtype)
 
 
-def combine(row_adapter, pieces, gate, up, maps):
+def combine(me, row_adapter, gate, up, own_maps, parts, map_parts, pieces):
     rows, units = gate.shape
-    ranks_all = maps.shape[0]
+    ranks = own_maps.shape[0]
+    ranks_all = ranks * (1 + len(parts))
     rank = pieces[0].shape[0]
     tile = min(512, units)
     users = jnp.broadcast_to(row_adapter[:, None], (rows, 2 * rank))
-    column_spec = pl.BlockSpec((rows, tile), lambda n: (0, n))
+    column_spec = pl.BlockSpec((rows, tile), lambda n, s: (0, n))
     return pl.pallas_call(
-        functools.partial(combine_kernel, len(pieces)),
-        grid=(units // tile,),
-        in_specs=[
-            pl.BlockSpec((rows, 2 * rank), lambda n: (0, 0)),
-            column_spec,
-            column_spec,
-            pl.BlockSpec((ranks_all, tile), lambda n: (0, n)),
-        ]
-        + [pl.BlockSpec((rank, rows), lambda n: (0, 0))] * len(pieces),
-        out_specs=column_spec,
-        scratch_shapes=[pltpu.VMEM((rows, ranks_all), jnp.bfloat16)],
+        functools.partial(combine_kernel, parts, len(pieces)),
+        grid_spec=pltpu.PrefetchScalarGridSpec(
+            num_scalar_prefetch=1,
+            grid=(units // tile,),
+            in_specs=[pl.BlockSpec((rows, 2 * rank), lambda n, s: (0, 0)), column_spec, column_spec, ANY_SPEC]
+            + [ANY_SPEC] * len(parts)
+            + [pl.BlockSpec((rank, rows), lambda n, s: (0, 0))] * len(pieces),
+            out_specs=column_spec,
+            scratch_shapes=[
+                pltpu.VMEM((rows, ranks_all), jnp.bfloat16),
+                pltpu.VMEM((ranks_all, units), jnp.bfloat16),
+                pltpu.SemaphoreType.DMA((1 + len(parts),)),
+            ],
+        ),
         out_shape=jax.ShapeDtypeStruct((rows, units), jnp.bfloat16),
-        compiler_params=pltpu.CompilerParams(vmem_limit_bytes=48 * MIB),
+        compiler_params=pltpu.CompilerParams(vmem_limit_bytes=rows * ranks_all * 2 + 16 * MIB),
         cost_estimate=pl.CostEstimate(
             flops=2 * rows * ranks_all * units, bytes_accessed=10 * rows * units, transcendentals=0
         ),
         name="combine",
-    )(users, gate, up, maps, *pieces)
+    )(me, users, gate, up, own_maps, *map_parts, *pieces)
+
+
+def exchange_order(size):
+    return tuple(sorted(range(1, size), key=lambda part: -(part // 4)))
 
 
 def per_device(
@@ -263,18 +295,33 @@
     resident, rank, width = adapter_down_weight.shape
     ranks = resident * rank
     rows = row_adapter.shape[0]
-
-    found, where, own_maps = ring_gather(
-        tokens, axis, adapter_up_weight.reshape(ranks, -1), lambda weights: split_columns(weights, size)
-    )
+    me_array = me.astype(jnp.int32).reshape(1)
+
+    own_maps = adapter_up_weight.reshape(ranks, -1)
+    parts = exchange_order(size)
+    released = {2: 4, 3: 4}
+    last_step = size // CORES // 2
+    cut = []
+    map_parts = []
+
+    def beside(step, values):
+        nonlocal cut
+        if step == 1:
+            maps, *values = lax.optimization_barrier((own_maps, *values))
+            cut = cut_columns(me_array, maps, parts, size)
+            return values
+        count = released.get(step, 0) if step < last_step else len(parts)
+        done = len(map_parts)
+        chosen, values = lax.optimization_barrier((cut[done : done + count], values))
+        for part, value in zip(parts[done:], chosen):
+            map_parts.append(lax.ppermute(value, axis, [(d, d ^ part) for d in range(size)]))
+        return values
+
+    found, where = ring_gather(tokens, axis, beside)
     pieces = [piece for piece, _ in found]
     columns = [column for _, column in found]
     table = jnp.array([row + [device] for device, row in enumerate(where)], jnp.int32)
     place = lax.dynamic_index_in_dim(table, me, 0, keepdims=False)
-
-    own_maps, pieces[-2], pieces[-4] = lax.optimization_barrier((own_maps, pieces[-2], pieces[-4]))
-    maps = lax.all_to_all(own_maps, axis, split_axis=0, concat_axis=0, tiled=True)
-    maps = maps.reshape(size * ranks, -1)
 
     shrunk = shrink(place, columns, pieces, row_adapter, adapter_down_weight.reshape(ranks, width), rank)
     near = min(4, size)
@@ -287,7 +334,7 @@
             lax.ppermute(plane, axis, [(d, (d + shift * near) % size) for d in range(size)])
         )
     gate, up = project(place, columns, pieces, gate_weight, up_weight, rows)
-    return combine(row_adapter, shrunk_pieces, gate, up, maps)
+    return combine(me_array, row_adapter, gate, up, own_maps, parts, map_parts, shrunk_pieces)
 
 
 def solution(mesh):

time: 101 us -> 178 us (1.76)
  Pallas kernels: 29 us -> 85 us
  waiting for transfers between devices: 23.9 us -> 42.2 us
  starting transfers between devices: 26.4 us -> 37.7 us
  local copies, waits for them, and re-layouts: 20.5 us -> 12.3 us
    pallas_call x2, Pallas kernels: 5.94 us -> 65.9 us  [the longest x1 60.8 us: cut_columns(): pl.pallas_call(functools.partial(cut_kernel, parts, units), grid_spec=plt...]
    ppermute x0 -> x15, waiting for transfers between devices: none -> 30.4 us  [beside(): lax.ppermute(value, axis, [(d, d ^ part) for d in range(size)])]
    ppermute x0 -> x15, starting transfers between devices: none -> 21.7 us  [beside(): lax.ppermute(value, axis, [(d, d ^ part) for d in range(size)])]
    unnamed x70 -> x26, local copies, waits for them, and re-layouts: 19.7 us -> 11.5 us
    ppermute x8, waiting for transfers between devices: 19.1 us -> 11.8 us  [moved(): return lax.ppermute(value, axis, pairs)]
    all_to_all x1 -> x0, starting transfers between devices: 4.81 us -> none  [per_device(): lax.all_to_all(own_maps, axis, split_axis=0, concat_axis=0, tiled=True)]
    ppermute x3, starting transfers between devices: 7.77 us -> 2.98 us  [per_device(): lax.ppermute(plane, axis, [(d, (d + shift * near) % size) for d in range(...]
    ppermute x3, waiting for transfers between devices: 4.02 us -> 0.01 us  [per_device(): lax.ppermute(shrunk, axis, [(d, d ^ flip) for d in range(size)])]
  transfers between devices with their start and end apart: 24 -> 38, of which waited for: 12 -> 13; matrix products, arithmetic and copies ran while one was open for 1% -> 0% of each run, Pallas kernels for 27% -> 45%
where the time goes in v4:
time: 178 us
  Pallas kernels  85 us (48%)
  waiting for transfers between devices  42.2 us (24%)
  starting transfers between devices  37.7 us (21%)
  local copies, waits for them, and re-layouts  12.3 us (7%)
    pallas_call x1, Pallas kernels, cut_columns(): pl.pallas_call(functools.partial(cut_kernel, parts, units), grid_spec=plt...  60.8 us
    ppermute x15, waiting for transfers between devices, beside(): lax.ppermute(value, axis, [(d, d ^ part) for d in range(size)])  30.4 us
    ppermute x15, starting transfers between devices, beside(): lax.ppermute(value, axis, [(d, d ^ part) for d in range(size)])  21.7 us
    pallas_call x1, Pallas kernels, project(): pl.pallas_call(functools.partial(project_kernel, columns, len(pieces)), g...  15.7 us
    ppermute x8, waiting for transfers between devices, moved(): return lax.ppermute(value, axis, pairs)  11.8 us
    unnamed x26, local copies, waits for them, and re-layouts  11.5 us
    ppermute x8, starting transfers between devices, moved(): return lax.ppermute(value, axis, pairs)  9.26 us
    pallas_call x1, Pallas kernels, combine(): pl.pallas_call(functools.partial(combine_kernel, parts, len(pieces)), gri...  5.1 us
  transfers between devices with their start and end apart: 38, of which 13 were waited for; matrix products, arithmetic and copies ran while one was open for 0% of the time, Pallas kernels for 45%

profile of v4, /device:TPU:0, one launch (start us, length us, event | category | flops | bytes accessed | tf_op | source)
XLA Modules:
  0.0 177.5 jit_solution(4324072839023412036)
XLA Ops:
  0.0 3.0 %collective-permute-start.1 = (bf16[16,8192]{1,0:T(8,128)(2,1)}, bf16[16,8192]{1,0:T(8,128)(2,1)S(1)}, u32[]{:S(2)}, u32[]{:S(2)}) collective-permute-start(bf16[16,8192]{1,0:T(8,128)(2,1)} %refs_0_.3), channel_id=1, source_target_pairs={{0,4},{1,5},{4,8},{5,9},{8,12},{9,13},{12,14},{13,15},{14,10},{15,... | collective-permute-start | bytes 786440 | tf_op jit(solution)/shard_map/ppermute | solution.py:30
  3.0 6.5 %collective-permute-done.1.refs_2_ = bf16[16,8192]{1,0:T(8,128)(2,1)S(1)} collective-permute-done((bf16[16,8192]{1,0:T(8,128)(2,1)}, bf16[16,8192]{1,0:T(8,128)(2,1)S(1)}, u32[]{:S(2)}, u32[]{:S(2)}) %collective-permute-start.1) | collective-permute-done | bytes 262176 | tf_op jit(solution)/shard_map/ppermute | solution.py:30
  9.5 1.5 collective-permute-done.2.refs_4_
  11.0 1.6 collective-permute-start.5
  13.0 60.8 %cut_columns.1 = (bf16[64,1024]{1,0:T(8,128)(2,1)}, bf16[64,1024]{1,0:T(8,128)(2,1)}, bf16[64,1024]{1,0:T(8,128)(2,1)}, bf16[64,1024]{1,0:T(8,128)(2,1)}, bf16[6...) custom-call(s32[1]{0:T(128)} %bitcast.me, ...), custom_call_target="tpu_custom_call" | custom-call | bytes 4194304 | tf_op jit(solution)/shard_map/cut_columns/pallas_call | solution.py:96
  74.2 1.7 collective-permute-start.9
  76.4 3.8 %collective-permute-done.10.refs_12_ = bf16[16,8192]{1,0:T(8,128)(2,1)S(1)} collective-permute-done((bf16[16,8192]{1,0:T(8,128)(2,1)S(1)}, bf16[16,8192]{1,0:T(8,128)(2,1)S(1)}, u32[]{:S(2)}, u32[]{:S(2)}) %collective-permute-start.10) | collective-permute-done | bytes 262176 | tf_op jit(solution)/shard_map/ppermute | solution.py:30
  80.3 3.5 %collective-permute-start.17 = (bf16[64,1024]{1,0:T(8,128)(2,1)}, bf16[64,1024]{1,0:T(8,128)(2,1)S(1)}, u32[]{:S(2)}, u32[]{:S(2)}) collective-permute-start(bf16[64,1024]{1,0:T(8,128)(2,1)} %get-tuple-element.72), channel_id=1, source_target_pairs={{0,12},{1,13},{2,14},{3,15},{4,8},{5,9},{6,10},{7,11},{8,4},{9,5},... | collective-permute-start | bytes 393224 | tf_op jit(solution)/shard_map/ppermute | solution.py:317
  84.7 1.9 %collective-permute-start.14 = (bf16[16,4096]{1,0:T(8,128)(2,1)S(1)}, bf16[16,4096]{1,0:T(8,128)(2,1)}, u32[]{:S(2)}, u32[]{:S(2)}) collective-permute-start(bf16[16,4096]{1,0:T(8,128)(2,1)S(1)} %slice.7), channel_id=1, source_target_pairs={{0,2},{1,3},{4,0},{5,1},{8,4},{9,5},{12,8},{13,9},{14,12},{15,13},... | collective-permute-start | bytes 393224 | tf_op jit(solution)/shard_map/ppermute | solution.py:30
  86.6 1.4 collective-permute-done.17.refs_0_
  88.7 2.1 %collective-permute-done.18.refs_1_ = bf16[64,1024]{1,0:T(8,128)(2,1)S(1)} collective-permute-done((bf16[64,1024]{1,0:T(8,128)(2,1)}, bf16[64,1024]{1,0:T(8,128)(2,1)S(1)}, u32[]{:S(2)}, u32[]{:S(2)}) %collective-permute-start.18) | collective-permute-done | bytes 131104 | tf_op jit(solution)/shard_map/ppermute | solution.py:317
  91.5 2.5 %collective-permute-start.19 = (bf16[64,1024]{1,0:T(8,128)(2,1)}, bf16[64,1024]{1,0:T(8,128)(2,1)S(1)}, u32[]{:S(2)}, u32[]{:S(2)}) collective-permute-start(bf16[64,1024]{1,0:T(8,128)(2,1)} %get-tuple-element.74), channel_id=1, source_target_pairs={{0,14},{1,15},{2,12},{3,13},{4,10},{5,11},{6,8},{7,9},{8,6},{9,7},... | collective-permute-start | bytes 393224 | tf_op jit(solution)/shard_map/ppermute | solution.py:317
  94.4 5.0 %collective-permute-done.19.refs_2_ = bf16[64,1024]{1,0:T(8,128)(2,1)S(1)} collective-permute-done((bf16[64,1024]{1,0:T(8,128)(2,1)}, bf16[64,1024]{1,0:T(8,128)(2,1)S(1)}, u32[]{:S(2)}, u32[]{:S(2)}) %collective-permute-start.19) | collective-permute-done | bytes 131104 | tf_op jit(solution)/shard_map/ppermute | solution.py:317
  100.6 3.2 %collective-permute-start.20 = (bf16[64,1024]{1,0:T(8,128)(2,1)}, bf16[64,1024]{1,0:T(8,128)(2,1)S(1)}, u32[]{:S(2)}, u32[]{:S(2)}) collective-permute-start(bf16[64,1024]{1,0:T(8,128)(2,1)} %get-tuple-element.75), channel_id=1, source_target_pairs={{0,15},{1,14},{2,13},{3,12},{4,11},{5,10},{6,9},{7,8},{8,7},{9,6},... | collective-permute-start | bytes 393224 | tf_op jit(solution)/shard_map/ppermute | solution.py:317
  103.8 3.0 %collective-permute-start.21 = (bf16[64,1024]{1,0:T(8,128)(2,1)}, bf16[64,1024]{1,0:T(8,128)(2,1)S(1)}, u32[]{:S(2)}, u32[]{:S(2)}) collective-permute-start(bf16[64,1024]{1,0:T(8,128)(2,1)} %get-tuple-element.76), channel_id=1, source_target_pairs={{0,8},{1,9},{2,10},{3,11},{4,12},{5,13},{6,14},{7,15},{8,0},{9,1},... | collective-permute-start | bytes 393224 | tf_op jit(solution)/shard_map/ppermute | solution.py:317
  107.2 2.1 %collective-permute-start.23 = (bf16[64,1024]{1,0:T(8,128)(2,1)}, bf16[64,1024]{1,0:T(8,128)(2,1)S(1)}, u32[]{:S(2)}, u32[]{:S(2)}) collective-permute-start(bf16[64,1024]{1,0:T(8,128)(2,1)} %get-tuple-element.78), channel_id=1, source_target_pairs={{0,10},{1,11},{2,8},{3,9},{4,14},{5,15},{6,12},{7,13},{8,2},{9,3},... | collective-permute-start | bytes 393224 | tf_op jit(solution)/shard_map/ppermute | solution.py:317
  112.2 1.2 copy-done.4
  114.1 3.4 %shrink.1 = bf16[64,256]{1,0:T(8,128)(2,1)S(1)} custom-call(s32[19]{0:T(128)S(1)} %dynamic-slice_bitcast_fusion.place, s32[1,256]{1,0:T(1,128)S(1)} %bitcast.9, bf16[64,8192]{1,0:T(8,128)(2,1)S(1)} %bitcast.8, bf16[16,8192]{1,0:T(8,128)(2,1)S(1)} %copy-done.2, bf16[16,8192]{1,0:T(8,128)(2,1)S(1)} %collective-permute-done.refs_1_, ...), custom_call_target="tpu_custom_call" | custom-call | flops 268435456 | bytes 5242880 | tf_op jit(solution)/shard_map/shrink/pallas_call | solution.py:131
  118.2 8.0 %collective-permute-done.21.refs_4_ = bf16[64,1024]{1,0:T(8,128)(2,1)S(1)} collective-permute-done((bf16[64,1024]{1,0:T(8,128)(2,1)}, bf16[64,1024]{1,0:T(8,128)(2,1)S(1)}, u32[]{:S(2)}, u32[]{:S(2)}) %collective-permute-start.21) | collective-permute-done | bytes 131104 | tf_op jit(solution)/shard_map/ppermute | solution.py:317
  126.7 2.2 %collective-permute-done.22.refs_5_ = bf16[64,1024]{1,0:T(8,128)(2,1)S(1)} collective-permute-done((bf16[64,1024]{1,0:T(8,128)(2,1)}, bf16[64,1024]{1,0:T(8,128)(2,1)S(1)}, u32[]{:S(2)}, u32[]{:S(2)}) %collective-permute-start.22) | collective-permute-done | bytes 131104 | tf_op jit(solution)/shard_map/ppermute | solution.py:317
  129.2 2.7 %collective-permute-done.23.refs_6_ = bf16[64,1024]{1,0:T(8,128)(2,1)S(1)} collective-permute-done((bf16[64,1024]{1,0:T(8,128)(2,1)}, bf16[64,1024]{1,0:T(8,128)(2,1)S(1)}, u32[]{:S(2)}, u32[]{:S(2)}) %collective-permute-start.23) | collective-permute-done | bytes 131104 | tf_op jit(solution)/shard_map/ppermute | solution.py:317
  131.9 2.8 %collective-permute-done.24.refs_7_ = bf16[64,1024]{1,0:T(8,128)(2,1)S(1)} collective-permute-done((bf16[64,1024]{1,0:T(8,128)(2,1)}, bf16[64,1024]{1,0:T(8,128)(2,1)S(1)}, u32[]{:S(2)}, u32[]{:S(2)}) %collective-permute-start.24) | collective-permute-done | bytes 131104 | tf_op jit(solution)/shard_map/ppermute | solution.py:317
  134.7 2.5 %collective-permute-start.27 = (bf16[64,1024]{1,0:T(8,128)(2,1)}, bf16[64,1024]{1,0:T(8,128)(2,1)S(1)}, u32[]{:S(2)}, u32[]{:S(2)}) collective-permute-start(bf16[64,1024]{1,0:T(8,128)(2,1)} %get-tuple-element.82), channel_id=1, source_target_pairs={{0,6},{1,7},{2,4},{3,5},{4,2},{5,3},{6,0},{7,1},{8,14},{9,15},{10,... | collective-permute-start | bytes 393224 | tf_op jit(solution)/shard_map/ppermute | solution.py:317
  137.8 1.5 collective-permute-start.30
  139.3 1.2 collective-permute-done.26.refs_9_
  140.5 1.3 collective-permute-start.31
  141.7 2.9 %collective-permute-done.27.refs_10_ = bf16[64,1024]{1,0:T(8,128)(2,1)S(1)} collective-permute-done((bf16[64,1024]{1,0:T(8,128)(2,1)}, bf16[64,1024]{1,0:T(8,128)(2,1)S(1)}, u32[]{:S(2)}, u32[]{:S(2)}) %collective-permute-start.27) | collective-permute-done | bytes 131104 | tf_op jit(solution)/shard_map/ppermute | solution.py:317
  145.0 2.1 %collective-permute-done.28.refs_11_ = bf16[64,1024]{1,0:T(8,128)(2,1)S(1)} collective-permute-done((bf16[64,1024]{1,0:T(8,128)(2,1)}, bf16[64,1024]{1,0:T(8,128)(2,1)S(1)}, u32[]{:S(2)}, u32[]{:S(2)}) %collective-permute-start.28) | collective-permute-done | bytes 131104 | tf_op jit(solution)/shard_map/ppermute | solution.py:317
  147.9 1.9 %collective-permute-start.37 = (bf16[64,256]{1,0:T(8,128)(2,1)S(1)}, bf16[64,256]{1,0:T(8,128)(2,1)S(1)}, u32[]{:S(2)}, u32[]{:S(2)}) collective-permute-start(bf16[64,256]{1,0:T(8,128)(2,1)S(1)} %add_add_fusion.refs_15_), channel_id=1, source_target_pairs={{0,12},{1,13},{2,14},{3,15},{4,0},{5,1},{6,2},{7,3},{8,4},{9,5},{1... | collective-permute-start | bytes 98312 | tf_op jit(solution)/shard_map/ppermute | solution.py:334
  149.7 5.8 %copy-done = bf16[8192,1024]{1,0:T(8,128)(2,1)S(1)} copy-done((bf16[8192,1024]{1,0:T(8,128)(2,1)S(1)}, bf16[8192,1024]{1,0:T(8,128)(2,1)}, u32[]{:S(2)}) %copy-start) | copy-done | bytes 16777240
  156.5 15.7 %project.1 = (f32[256,1024]{1,0:T(8,128)S(1)}, f32[256,1024]{1,0:T(8,128)S(1)}) custom-call(s32[19]{0:T(128)S(1)} %dynamic-slice_bitcast_fusion.place, bf16[8192,1024]{1,0:T(8,128)(2,1)S(1)} %copy-done, bf16[8192,1024]{1,0:T(8,128)(2,1)} %up_weight_ref.1, bf16[16,8192]{1,0:T(8,128)(2,1)S(1)} %copy-done.3, bf16[16,8192]{1,0:T(8,128)(2,1)S(1)} %collective-permute-done.refs_1_, ...), custom_call_target="tpu_custom_call" | custom-call | flops 8589934592 | bytes 37748736 | tf_op jit(solution)/shard_map/project/pallas_call | solution.py:184
  172.4 5.1 %combine.1 = bf16[256,1024]{1,0:T(8,128)(2,1)} custom-call(s32[1]{0:T(128)} %bitcast.me, s32[256,128]{1,0:T(8,128)S(1)} %broadcast_in_dim.2.users_ref, f32[256,1024]{1,0:T(8,128)S(1)} %get-tuple-element.70.gate_ref, f32[256,1024]{1,0:T(8,128)S(1)} %get-tuple-element.71.up_ref, bf16[64,16384]{1,0:T(8,128)(2,1)S(1)} %bitcast.7, ...), custom_call_target="tpu_custom_call" | custom-call | flops 536870912 | bytes 2621440 | tf_op jit(solution)/shard_map/combine/pallas_call | solution.py:254
  (79 shorter events, 13.3 us)
Async XLA Ops:
  0.0 9.5 %collective-permute-start.1 = (bf16[16,8192]{1,0:T(8,128)(2,1)}, bf16[16,8192]{1,0:T(8,128)(2,1)S(1)}, u32[]{:S(2)}, u32[]{:S(2)}) collective-permute-start(bf16[16,8192]{1,0:T(8,128)(2,1)} %refs_0_.3), channel_id=1, source_target_pairs={{0,4},{1,5},{4,8},{5,9},{8,12},{9,13},{12,14},{13,15},{14,10},{15,... | collective-permute-start | bytes 786440 | tf_op jit(solution)/shard_map/ppermute | solution.py:30
  3.0 8.0 %collective-permute-start.2 = (bf16[16,8192]{1,0:T(8,128)(2,1)}, bf16[16,8192]{1,0:T(8,128)(2,1)S(1)}, u32[]{:S(2)}, u32[]{:S(2)}) collective-permute-start(bf16[16,8192]{1,0:T(8,128)(2,1)} %refs_0_.3), channel_id=1, source_target_pairs={{0,2},{1,3},{4,0},{5,1},{8,4},{9,5},{12,8},{13,9},{14,12},{15,13},... | collective-permute-start | bytes 786440 | tf_op jit(solution)/shard_map/ppermute | solution.py:30
  11.0 62.8 %collective-permute-start.5 = (bf16[16,8192]{1,0:T(8,128)(2,1)S(1)}, bf16[16,8192]{1,0:T(8,128)(2,1)S(1)}, u32[]{:S(2)}, u32[]{:S(2)}) collective-permute-start(bf16[16,8192]{1,0:T(8,128)(2,1)S(1)} %collective-permute-done.1.refs_2_), channel_id=1, source_target_pairs={{0,4},{1,5},{4,8},{5,9},{8,12},{9,13},{12,14},{13,15},{14,10},{15,... | collective-permute-start | bytes 786440 | tf_op jit(solution)/shard_map/ppermute | solution.py:30
  12.6 61.3 %collective-permute-start.6 = (bf16[16,8192]{1,0:T(8,128)(2,1)S(1)}, bf16[16,8192]{1,0:T(8,128)(2,1)S(1)}, u32[]{:S(2)}, u32[]{:S(2)}) collective-permute-start(bf16[16,8192]{1,0:T(8,128)(2,1)S(1)} %collective-permute-done.2.refs_4_), channel_id=1, source_target_pairs={{0,2},{1,3},{4,0},{5,1},{8,4},{9,5},{12,8},{13,9},{14,12},{15,13},... | collective-permute-start | bytes 786440 | tf_op jit(solution)/shard_map/ppermute | solution.py:30
  74.2 9.6 %collective-permute-start.9 = (bf16[16,8192]{1,0:T(8,128)(2,1)S(1)}, bf16[16,8192]{1,0:T(8,128)(2,1)S(1)}, u32[]{:S(2)}, u32[]{:S(2)}) collective-permute-start(bf16[16,8192]{1,0:T(8,128)(2,1)S(1)} %collective-permute-done.5.refs_6_), channel_id=1, source_target_pairs={{0,4},{1,5},{4,8},{5,9},{8,12},{9,13},{12,14},{13,15},{14,10},{15,... | collective-permute-start | bytes 786440 | tf_op jit(solution)/shard_map/ppermute | solution.py:30
  75.9 7.9 %collective-permute-start = (bf16[16,8192]{1,0:T(8,128)(2,1)}, bf16[16,8192]{1,0:T(8,128)(2,1)S(1)}, u32[]{:S(2)}, u32[]{:S(2)}) collective-permute-start(bf16[16,8192]{1,0:T(8,128)(2,1)} %refs_0_.3), channel_id=1, source_target_pairs={{0,1},{1,0},{2,3},{3,2},{4,5},{5,4},{6,7},{7,6},{8,9},{9,8},{10,11... | collective-permute-start | bytes 786440 | tf_op jit(solution)/shard_map/ppermute | solution.py:33
  75.9 8.5 %collective-permute-start.3 = (bf16[16,8192]{1,0:T(8,128)(2,1)S(1)}, bf16[16,8192]{1,0:T(8,128)(2,1)S(1)}, u32[]{:S(2)}, u32[]{:S(2)}) collective-permute-start(bf16[16,8192]{1,0:T(8,128)(2,1)S(1)} %collective-permute-done.1.refs_2_), channel_id=1, source_target_pairs={{0,1},{1,0},{2,3},{3,2},{4,5},{5,4},{6,7},{7,6},{8,9},{9,8},{10,11... | collective-permute-start | bytes 786440 | tf_op jit(solution)/shard_map/ppermute | solution.py:33
  76.4 8.3 %collective-permute-start.4 = (bf16[16,8192]{1,0:T(8,128)(2,1)S(1)}, bf16[16,8192]{1,0:T(8,128)(2,1)S(1)}, u32[]{:S(2)}, u32[]{:S(2)}) collective-permute-start(bf16[16,8192]{1,0:T(8,128)(2,1)S(1)} %collective-permute-done.2.refs_4_), channel_id=1, source_target_pairs={{0,1},{1,0},{2,3},{3,2},{4,5},{5,4},{6,7},{7,6},{8,9},{9,8},{10,11... | collective-permute-start | bytes 786440 | tf_op jit(solution)/shard_map/ppermute | solution.py:33
  80.3 7.8 %collective-permute-start.17 = (bf16[64,1024]{1,0:T(8,128)(2,1)}, bf16[64,1024]{1,0:T(8,128)(2,1)S(1)}, u32[]{:S(2)}, u32[]{:S(2)}) collective-permute-start(bf16[64,1024]{1,0:T(8,128)(2,1)} %get-tuple-element.72), channel_id=1, source_target_pairs={{0,12},{1,13},{2,14},{3,15},{4,8},{5,9},{6,10},{7,11},{8,4},{9,5},... | collective-permute-start | bytes 393224 | tf_op jit(solution)/shard_map/ppermute | solution.py:317
  83.8 16.3 %collective-permute-start.7 = (bf16[16,8192]{1,0:T(8,128)(2,1)S(1)}, bf16[16,8192]{1,0:T(8,128)(2,1)S(1)}, u32[]{:S(2)}, u32[]{:S(2)}) collective-permute-start(bf16[16,8192]{1,0:T(8,128)(2,1)S(1)} %collective-permute-done.5.refs_6_), channel_id=1, source_target_pairs={{0,1},{1,0},{2,3},{3,2},{4,5},{5,4},{6,7},{7,6},{8,9},{9,8},{10,11... | collective-permute-start | bytes 786440 | tf_op jit(solution)/shard_map/ppermute | solution.py:33
  84.5 9.5 %collective-permute-start.13 = (bf16[16,4096]{1,0:T(8,128)(2,1)S(1)}, bf16[16,4096]{1,0:T(8,128)(2,1)S(1)}, u32[]{:S(2)}, u32[]{:S(2)}) collective-permute-start(bf16[16,4096]{1,0:T(8,128)(2,1)S(1)} %slice.6), channel_id=1, source_target_pairs={{0,4},{1,5},{4,8},{5,9},{8,12},{9,13},{12,14},{13,15},{14,10},{15,... | collective-permute-start | bytes 393224 | tf_op jit(solution)/shard_map/ppermute | solution.py:30
  84.7 9.6 %collective-permute-start.14 = (bf16[16,4096]{1,0:T(8,128)(2,1)S(1)}, bf16[16,4096]{1,0:T(8,128)(2,1)}, u32[]{:S(2)}, u32[]{:S(2)}) collective-permute-start(bf16[16,4096]{1,0:T(8,128)(2,1)S(1)} %slice.7), channel_id=1, source_target_pairs={{0,2},{1,3},{4,0},{5,1},{8,4},{9,5},{12,8},{13,9},{14,12},{15,13},... | collective-permute-start | bytes 393224 | tf_op jit(solution)/shard_map/ppermute | solution.py:30
  88.7 11.9 %collective-permute-start.8 = (bf16[16,8192]{1,0:T(8,128)(2,1)S(1)}, bf16[16,8192]{1,0:T(8,128)(2,1)S(1)}, u32[]{:S(2)}, u32[]{:S(2)}) collective-permute-start(bf16[16,8192]{1,0:T(8,128)(2,1)S(1)} %collective-permute-done.6.refs_8_), channel_id=1, source_target_pairs={{0,1},{1,0},{2,3},{3,2},{4,5},{5,4},{6,7},{7,6},{8,9},{9,8},{10,11... | collective-permute-start | bytes 786440 | tf_op jit(solution)/shard_map/ppermute | solution.py:33
  91.5 8.0 %collective-permute-start.19 = (bf16[64,1024]{1,0:T(8,128)(2,1)}, bf16[64,1024]{1,0:T(8,128)(2,1)S(1)}, u32[]{:S(2)}, u32[]{:S(2)}) collective-permute-start(bf16[64,1024]{1,0:T(8,128)(2,1)} %get-tuple-element.74), channel_id=1, source_target_pairs={{0,14},{1,15},{2,12},{3,13},{4,10},{5,11},{6,8},{7,9},{8,6},{9,7},... | collective-permute-start | bytes 393224 | tf_op jit(solution)/shard_map/ppermute | solution.py:317
  93.9 13.3 %collective-permute-start.11 = (bf16[16,8192]{1,0:T(8,128)(2,1)S(1)}, bf16[16,8192]{1,0:T(8,128)(2,1)S(1)}, u32[]{:S(2)}, u32[]{:S(2)}) collective-permute-start(bf16[16,8192]{1,0:T(8,128)(2,1)S(1)} %collective-permute-done.9.refs_10_), channel_id=1, source_target_pairs={{0,1},{1,0},{2,3},{3,2},{4,5},{5,4},{6,7},{7,6},{8,9},{9,8},{10,11... | collective-permute-start | bytes 786440 | tf_op jit(solution)/shard_map/ppermute | solution.py:33
  94.3 15.0 %collective-permute-start.12 = (bf16[16,8192]{1,0:T(8,128)(2,1)S(1)}, bf16[16,8192]{1,0:T(8,128)(2,1)S(1)}, u32[]{:S(2)}, u32[]{:S(2)}) collective-permute-start(bf16[16,8192]{1,0:T(8,128)(2,1)S(1)} %collective-permute-done.10.refs_12_), channel_id=1, source_target_pairs={{0,1},{1,0},{2,3},{3,2},{4,5},{5,4},{6,7},{7,6},{8,9},{9,8},{10,11... | collective-permute-start | bytes 786440 | tf_op jit(solution)/shard_map/ppermute | solution.py:33
  100.6 16.9 %collective-permute-start.20 = (bf16[64,1024]{1,0:T(8,128)(2,1)}, bf16[64,1024]{1,0:T(8,128)(2,1)S(1)}, u32[]{:S(2)}, u32[]{:S(2)}) collective-permute-start(bf16[64,1024]{1,0:T(8,128)(2,1)} %get-tuple-element.75), channel_id=1, source_target_pairs={{0,15},{1,14},{2,13},{3,12},{4,11},{5,10},{6,9},{7,8},{8,7},{9,6},... | collective-permute-start | bytes 393224 | tf_op jit(solution)/shard_map/ppermute | solution.py:317
  103.8 22.4 %collective-permute-start.21 = (bf16[64,1024]{1,0:T(8,128)(2,1)}, bf16[64,1024]{1,0:T(8,128)(2,1)S(1)}, u32[]{:S(2)}, u32[]{:S(2)}) collective-permute-start(bf16[64,1024]{1,0:T(8,128)(2,1)} %get-tuple-element.76), channel_id=1, source_target_pairs={{0,8},{1,9},{2,10},{3,11},{4,12},{5,13},{6,14},{7,15},{8,0},{9,1},... | collective-permute-start | bytes 393224 | tf_op jit(solution)/shard_map/ppermute | solution.py:317
  106.9 22.1 %collective-permute-start.22 = (bf16[64,1024]{1,0:T(8,128)(2,1)}, bf16[64,1024]{1,0:T(8,128)(2,1)S(1)}, u32[]{:S(2)}, u32[]{:S(2)}) collective-permute-start(bf16[64,1024]{1,0:T(8,128)(2,1)} %get-tuple-element.77), channel_id=1, source_target_pairs={{0,9},{1,8},{2,11},{3,10},{4,13},{5,12},{6,15},{7,14},{8,1},{9,0},... | collective-permute-start | bytes 393224 | tf_op jit(solution)/shard_map/ppermute | solution.py:317
  107.2 24.7 %collective-permute-start.23 = (bf16[64,1024]{1,0:T(8,128)(2,1)}, bf16[64,1024]{1,0:T(8,128)(2,1)S(1)}, u32[]{:S(2)}, u32[]{:S(2)}) collective-permute-start(bf16[64,1024]{1,0:T(8,128)(2,1)} %get-tuple-element.78), channel_id=1, source_target_pairs={{0,10},{1,11},{2,8},{3,9},{4,14},{5,15},{6,12},{7,13},{8,2},{9,3},... | collective-permute-start | bytes 393224 | tf_op jit(solution)/shard_map/ppermute | solution.py:317
  109.3 25.3 %collective-permute-start.24 = (bf16[64,1024]{1,0:T(8,128)(2,1)}, bf16[64,1024]{1,0:T(8,128)(2,1)S(1)}, u32[]{:S(2)}, u32[]{:S(2)}) collective-permute-start(bf16[64,1024]{1,0:T(8,128)(2,1)} %get-tuple-element.79), channel_id=1, source_target_pairs={{0,11},{1,10},{2,9},{3,8},{4,15},{5,14},{6,13},{7,12},{8,3},{9,2},... | collective-permute-start | bytes 393224 | tf_op jit(solution)/shard_map/ppermute | solution.py:317
  117.5 17.2 %collective-permute-start.32 = (bf16[64,256]{1,0:T(8,128)(2,1)S(1)}, bf16[64,256]{1,0:T(8,128)(2,1)S(1)}, u32[]{:S(2)}, u32[]{:S(2)}) collective-permute-start(bf16[64,256]{1,0:T(8,128)(2,1)S(1)} %shrink.1), channel_id=1, source_target_pairs={{0,1},{1,0},{2,3},{3,2},{4,5},{5,4},{6,7},{7,6},{8,9},{9,8},{10,11... | collective-permute-start | bytes 98312 | tf_op jit(solution)/shard_map/ppermute | solution.py:330
  126.2 11.0 %collective-permute-start.33 = (bf16[64,256]{1,0:T(8,128)(2,1)S(1)}, bf16[64,256]{1,0:T(8,128)(2,1)S(1)}, u32[]{:S(2)}, u32[]{:S(2)}) collective-permute-start(bf16[64,256]{1,0:T(8,128)(2,1)S(1)} %shrink.1), channel_id=1, source_target_pairs={{0,2},{1,3},{2,0},{3,1},{4,6},{5,7},{6,4},{7,5},{8,10},{9,11},{10,... | collective-permute-start | bytes 98312 | tf_op jit(solution)/shard_map/ppermute | solution.py:330
  128.9 8.4 %collective-permute-start.34 = (bf16[64,256]{1,0:T(8,128)(2,1)S(1)}, bf16[64,256]{1,0:T(8,128)(2,1)S(1)}, u32[]{:S(2)}, u32[]{:S(2)}) collective-permute-start(bf16[64,256]{1,0:T(8,128)(2,1)S(1)} %shrink.1), channel_id=1, source_target_pairs={{0,3},{1,2},{2,1},{3,0},{4,7},{5,6},{6,5},{7,4},{8,11},{9,10},{10,... | collective-permute-start | bytes 98312 | tf_op jit(solution)/shard_map/ppermute | solution.py:330
  134.7 10.0 %collective-permute-start.27 = (bf16[64,1024]{1,0:T(8,128)(2,1)}, bf16[64,1024]{1,0:T(8,128)(2,1)S(1)}, u32[]{:S(2)}, u32[]{:S(2)}) collective-permute-start(bf16[64,1024]{1,0:T(8,128)(2,1)} %get-tuple-element.82), channel_id=1, source_target_pairs={{0,6},{1,7},{2,4},{3,5},{4,2},{5,3},{6,0},{7,1},{8,14},{9,15},{10,... | collective-permute-start | bytes 393224 | tf_op jit(solution)/shard_map/ppermute | solution.py:317
  137.2 9.9 %collective-permute-start.28 = (bf16[64,1024]{1,0:T(8,128)(2,1)}, bf16[64,1024]{1,0:T(8,128)(2,1)S(1)}, u32[]{:S(2)}, u32[]{:S(2)}) collective-permute-start(bf16[64,1024]{1,0:T(8,128)(2,1)} %get-tuple-element.83), channel_id=1, source_target_pairs={{0,7},{1,6},{2,5},{3,4},{4,3},{5,2},{6,1},{7,0},{8,15},{9,14},{10,... | collective-permute-start | bytes 393224 | tf_op jit(solution)/shard_map/ppermute | solution.py:317
  137.4 10.5 %collective-permute-start.29 = (bf16[64,1024]{1,0:T(8,128)(2,1)}, bf16[64,1024]{1,0:T(8,128)(2,1)S(1)}, u32[]{:S(2)}, u32[]{:S(2)}) collective-permute-start(bf16[64,1024]{1,0:T(8,128)(2,1)} %get-tuple-element.84), channel_id=1, source_target_pairs={{0,1},{1,0},{2,3},{3,2},{4,5},{5,4},{6,7},{7,6},{8,9},{9,8},{10,11... | collective-permute-start | bytes 393224 | tf_op jit(solution)/shard_map/ppermute | solution.py:317
  137.8 34.5 %collective-permute-start.30 = (bf16[64,1024]{1,0:T(8,128)(2,1)}, bf16[64,1024]{1,0:T(8,128)(2,1)S(1)}, u32[]{:S(2)}, u32[]{:S(2)}) collective-permute-start(bf16[64,1024]{1,0:T(8,128)(2,1)} %get-tuple-element.85), channel_id=1, source_target_pairs={{0,2},{1,3},{2,0},{3,1},{4,6},{5,7},{6,4},{7,5},{8,10},{9,11},{10,... | collective-permute-start | bytes 393224 | tf_op jit(solution)/shard_map/ppermute | solution.py:317
  140.5 31.8 %collective-permute-start.31 = (bf16[64,1024]{1,0:T(8,128)(2,1)}, bf16[64,1024]{1,0:T(8,128)(2,1)S(1)}, u32[]{:S(2)}, u32[]{:S(2)}) collective-permute-start(bf16[64,1024]{1,0:T(8,128)(2,1)} %get-tuple-element.86), channel_id=1, source_target_pairs={{0,3},{1,2},{2,1},{3,0},{4,7},{5,6},{6,5},{7,4},{8,11},{9,10},{10,... | collective-permute-start | bytes 393224 | tf_op jit(solution)/shard_map/ppermute | solution.py:317
  144.7 27.6 %collective-permute-start.35 = (bf16[64,256]{1,0:T(8,128)(2,1)S(1)}, bf16[64,256]{1,0:T(8,128)(2,1)S(1)}, u32[]{:S(2)}, u32[]{:S(2)}) collective-permute-start(bf16[64,256]{1,0:T(8,128)(2,1)S(1)} %add_add_fusion.refs_15_), channel_id=1, source_target_pairs={{0,4},{1,5},{2,6},{3,7},{4,8},{5,9},{6,10},{7,11},{8,12},{9,13},{1... | collective-permute-start | bytes 98312 | tf_op jit(solution)/shard_map/ppermute | solution.py:334
  147.1 25.2 %collective-permute-start.36 = (bf16[64,256]{1,0:T(8,128)(2,1)S(1)}, bf16[64,256]{1,0:T(8,128)(2,1)S(1)}, u32[]{:S(2)}, u32[]{:S(2)}) collective-permute-start(bf16[64,256]{1,0:T(8,128)(2,1)S(1)} %add_add_fusion.refs_15_), channel_id=1, source_target_pairs={{0,8},{1,9},{2,10},{3,11},{4,12},{5,13},{6,14},{7,15},{8,0},{9,1},... | collective-permute-start | bytes 98312 | tf_op jit(solution)/shard_map/ppermute | solution.py:334
  147.9 24.4 %collective-permute-start.37 = (bf16[64,256]{1,0:T(8,128)(2,1)S(1)}, bf16[64,256]{1,0:T(8,128)(2,1)S(1)}, u32[]{:S(2)}, u32[]{:S(2)}) collective-permute-start(bf16[64,256]{1,0:T(8,128)(2,1)S(1)} %add_add_fusion.refs_15_), channel_id=1, source_target_pairs={{0,12},{1,13},{2,14},{3,15},{4,0},{5,1},{6,2},{7,3},{8,4},{9,5},{1... | collective-permute-start | bytes 98312 | tf_op jit(solution)/shard_map/ppermute | solution.py:334
  (19 other events, 164.1 us)

commit v5 on v3

--- a/solution.py
+++ b/solution.py
@@ -16,7 +16,7 @@
     return list(range(0, chips, 2)) + list(range(chips - 1, 0, -2))
 
 
-def ring_gather(block, axis, extra, prepare):
+def ring_gather(block, axis, beside):
     size = lax.axis_size(axis)
     chips = size // CORES
     ring = chip_ring(chips)
@@ -32,34 +32,44 @@
     def other_core(value):
         return lax.ppermute(value, axis, [(d, d ^ 1) for d in range(size)])
 
-    pieces = []
-    where = [[] for _ in range(size)]
-
-    def arrived(value, column, distance):
-        pieces.append((value, column))
-        pieces.append((other_core(value), column))
-        for device in range(size):
-            chip = ring[(ring.index(device // CORES) + distance) % chips]
-            core = device % CORES
-            where[device] += [chip * CORES + core, chip * CORES + 1 - core]
-
-    arrived(block, 0, 0)
+    pieces = [(block, 0)]
+    where = [[device] for device in range(size)]
+
+    def arrived(values, columns, distances):
+        for value, column, distance in zip(values, columns, distances):
+            pieces.append((value, column))
+            for device in range(size):
+                chip = ring[(ring.index(device // CORES) + distance) % chips]
+                where[device].append(chip * CORES + device % CORES)
+
+    def crossed(values, columns, distances):
+        for value, column, distance in zip(values, columns, distances):
+            pieces.append((value, column))
+            for device in range(size):
+                chip = ring[(ring.index(device // CORES) + distance) % chips]
+                where[device].append(chip * CORES + 1 - device % CORES)
+
+    waiting = ((block,), (0,), (0,))
     right = left = block
     for step in range(1, chips // 2):
-        if step == 2:
-            extra, right, left = lax.optimization_barrier((extra, right, left))
-            extra = prepare(extra)
-        if step == 3:
-            extra, right, left = lax.optimization_barrier((extra, right, left))
-        right = moved(right, 1)
-        left = moved(left, -1)
-        arrived(right, 0, -step)
-        arrived(left, 0, step)
+        over = [other_core(value) for value in waiting[0]]
+        right, left = moved(right, 1), moved(left, -1)
+        right, left, *over = lax.optimization_barrier((right, left, *over))
+        right, left = beside(step, (right, left))
+        crossed(over, *waiting[1:])
+        waiting = ((right, left), (0, 0), (-step, step))
+        arrived(*waiting)
     half = block.shape[1] // 2
     far = chips // 2
-    arrived(moved(right[:, :half], 1), 0, far)
-    arrived(moved(left[:, half:], -1), half, far)
-    return pieces, where, extra
+    over = [other_core(value) for value in waiting[0]]
+    ends = moved(right[:, :half], 1), moved(left[:, half:], -1)
+    ends = beside(far, lax.optimization_barrier((*ends, *over)))
+    ends, over = ends[:2], ends[2:]
+    crossed(over, *waiting[1:])
+    waiting = (ends, (0, half), (far, far))
+    arrived(*waiting)
+    crossed([other_core(value) for value in ends], *waiting[1:])
+    return pieces, where
 
 
 def assemble(spots, columns, piece_refs, tokens_vmem, sems):
@@ -98,7 +108,11 @@
     )(weights)
 
 
-HBM_SPEC = pl.BlockSpec(memory_space=pltpu.HBM)
+def in_hbm(values):
+    return [pltpu.with_memory_space_constraint(value, pltpu.HBM) for value in values]
+
+
+ANY_SPEC = pl.BlockSpec(memory_space=pl.ANY)
 
 
 def shrink_kernel(columns, pieces, rank, place, users_ref, down_ref, *refs):
@@ -130,7 +144,7 @@
                 pl.BlockSpec((1, rows), lambda i, s: (0, 0)),
                 pl.BlockSpec((ranks, width), lambda i, s: (0, 0)),
             ]
-            + [HBM_SPEC] * len(pieces),
+            + [ANY_SPEC] * len(pieces),
             out_specs=pl.BlockSpec((rank, rows), lambda i, s: (0, 0)),
             scratch_shapes=[
                 pltpu.VMEM((rows, width), jnp.bfloat16),
@@ -138,12 +152,12 @@
             ],
         ),
         out_shape=jax.ShapeDtypeStruct((rank, rows), jnp.bfloat16),
-        compiler_params=pltpu.CompilerParams(vmem_limit_bytes=40 * MIB),
+        compiler_params=pltpu.CompilerParams(vmem_limit_bytes=rows * width * 2 + 8 * MIB),
         cost_estimate=pl.CostEstimate(
             flops=2 * rows * width * ranks, bytes_accessed=2 * (rows + ranks) * width, transcendentals=0
         ),
         name="shrink",
-    )(place, row_adapter.reshape(1, rows), down, *pieces)
+    )(place, row_adapter.reshape(1, rows), *in_hbm([down, *pieces]))
 
 
 def project_kernel(columns, pieces, place, gate_weight_ref, up_weight_ref, *refs):
@@ -173,13 +187,13 @@
     depth = min(1024, width)
     weight_spec = pl.BlockSpec((depth, units), lambda k, s: (k, 0))
     out_spec = pl.BlockSpec((rows, units), lambda k, s: (0, 0))
-    out = jax.ShapeDtypeStruct((rows, units), jnp.float32)
+    out = pltpu.HBM((rows, units), jnp.float32)
     return pl.pallas_call(
         functools.partial(project_kernel, columns, len(pieces)),
         grid_spec=pltpu.PrefetchScalarGridSpec(
             num_scalar_prefetch=1,
             grid=(width // depth,),
-            in_specs=[weight_spec, weight_spec] + [HBM_SPEC] * len(pieces),
+            in_specs=[weight_spec, weight_spec] + [ANY_SPEC] * len(pieces),
             out_specs=[out_spec, out_spec],
             scratch_shapes=[
                 pltpu.VMEM((rows, width), jnp.bfloat16),
@@ -187,64 +201,73 @@
             ],
         ),
         out_shape=[out, out],
-        compiler_params=pltpu.CompilerParams(vmem_limit_bytes=48 * MIB),
+        compiler_params=pltpu.CompilerParams(vmem_limit_bytes=rows * width * 2 + 20 * MIB),
         cost_estimate=pl.CostEstimate(
             flops=4 * rows * width * units,
             bytes_accessed=2 * (rows + 2 * units) * width,
             transcendentals=rows * units,
         ),
         name="project",
-    )(place, gate_weight, up_weight, *pieces)
-
-
-def combine_kernel(pieces, users_ref, gate_ref, up_ref, maps_ref, *refs):
+    )(place, *in_hbm([gate_weight, up_weight, *pieces]))
+
+
+def spread_kernel(pieces, users_ref, *refs):
     piece_refs = refs[:pieces]
-    out_ref, shrunk_vmem = refs[pieces:]
-    rank, rows = piece_refs[0].shape
-
-    @pl.when(pl.program_id(0) == 0)
-    def _():
-        total = piece_refs[0][...].astype(jnp.float32)
-        for ref in piece_refs[1:]:
-            total += ref[...].astype(jnp.float32)
-        pair = jnp.transpose(jnp.concatenate([total, total], axis=0))
-        users = users_ref[...]
-        column = lax.broadcasted_iota(jnp.int32, pair.shape, 1)
-        for start in range(0, shrunk_vmem.shape[1], 2 * rank):
-            mine = users == (start + column) // rank
-            shrunk_vmem[:, start : start + 2 * rank] = jnp.where(mine, pair, 0.0).astype(jnp.bfloat16)
-
-    delta = jnp.dot(shrunk_vmem[...], maps_ref[...], preferred_element_type=jnp.float32)
+    out_ref = refs[pieces]
+    rank = piece_refs[0].shape[0]
+    total = piece_refs[0][...].astype(jnp.float32)
+    for ref in piece_refs[1:]:
+        total += ref[...].astype(jnp.float32)
+    pair = jnp.transpose(jnp.concatenate([total, total], axis=0))
+    users = users_ref[...]
+    column = lax.broadcasted_iota(jnp.int32, pair.shape, 1)
+    for start in range(0, out_ref.shape[1], 2 * rank):
+        mine = users == (start + column) // rank
+        out_ref[:, start : start + 2 * rank] = jnp.where(mine, pair, 0.0).astype(out_ref.dtype)
+
+
+def spread(row_adapter, pieces, ranks_all):
+    rank, rows = pieces[0].shape
+    users = jnp.broadcast_to(row_adapter[:, None], (rows, 2 * rank))
+    return pl.pallas_call(
+        functools.partial(spread_kernel, len(pieces)),
+        out_shape=pltpu.HBM((rows, ranks_all), jnp.bfloat16),
+        compiler_params=pltpu.CompilerParams(vmem_limit_bytes=rows * ranks_all * 2 + 12 * MIB),
+        cost_estimate=pl.CostEstimate(
+            flops=rows * ranks_all, bytes_accessed=2 * rows * ranks_all, transcendentals=0
+        ),
+        name="spread",
+    )(users, *pieces)
+
+
+def combine_kernel(shrunk_ref, gate_ref, up_ref, maps_ref, out_ref):
+    delta = jnp.dot(shrunk_ref[...], maps_ref[...], preferred_element_type=jnp.float32)
     delta = (ADAPTER_SCALE * delta).astype(jnp.bfloat16).astype(jnp.float32)
     out_ref[...] = (gate_ref[...] * (up_ref[...] + delta)).astype(out_ref.dtype)
 
 
-def combine(row_adapter, pieces, gate, up, maps):
+def combine(shrunk, gate, up, maps):
     rows, units = gate.shape
     ranks_all = maps.shape[0]
-    rank = pieces[0].shape[0]
-    tile = min(512, units)
-    users = jnp.broadcast_to(row_adapter[:, None], (rows, 2 * rank))
+    tile = min(256, units)
     column_spec = pl.BlockSpec((rows, tile), lambda n: (0, n))
     return pl.pallas_call(
-        functools.partial(combine_kernel, len(pieces)),
+        combine_kernel,
         grid=(units // tile,),
         in_specs=[
-            pl.BlockSpec((rows, 2 * rank), lambda n: (0, 0)),
+            pl.BlockSpec((rows, ranks_all), lambda n: (0, 0)),
             column_spec,
             column_spec,
             pl.BlockSpec((ranks_all, tile), lambda n: (0, n)),
-        ]
-        + [pl.BlockSpec((rank, rows), lambda n: (0, 0))] * len(pieces),
+        ],
         out_specs=column_spec,
-        scratch_shapes=[pltpu.VMEM((rows, ranks_all), jnp.bfloat16)],
         out_shape=jax.ShapeDtypeStruct((rows, units), jnp.bfloat16),
-        compiler_params=pltpu.CompilerParams(vmem_limit_bytes=48 * MIB),
+        compiler_params=pltpu.CompilerParams(vmem_limit_bytes=rows * ranks_all * 4 + 16 * MIB),
         cost_estimate=pl.CostEstimate(
             flops=2 * rows * ranks_all * units, bytes_accessed=10 * rows * units, transcendentals=0
         ),
         name="combine",
-    )(users, gate, up, maps, *pieces)
+    )(*in_hbm([shrunk, gate, up]), maps)
 
 
 def per_device(
@@ -264,17 +287,26 @@
     ranks = resident * rank
     rows = row_adapter.shape[0]
 
-    found, where, own_maps = ring_gather(
-        tokens, axis, adapter_up_weight.reshape(ranks, -1), lambda weights: split_columns(weights, size)
-    )
+    own_maps = adapter_up_weight.reshape(ranks, -1)
+    steps = size // CORES // 2
+    maps = None
+
+    def beside(step, values):
+        nonlocal own_maps, maps
+        if step not in (1, 2, steps):
+            return values
+        own_maps, *values = lax.optimization_barrier((own_maps, *values))
+        if step == 1:
+            own_maps = split_columns(own_maps, size)
+        if step == steps:
+            maps = lax.all_to_all(own_maps, axis, split_axis=0, concat_axis=0, tiled=True)
+        return values
+
+    found, where = ring_gather(tokens, axis, beside)
     pieces = [piece for piece, _ in found]
     columns = [column for _, column in found]
     table = jnp.array([row + [device] for device, row in enumerate(where)], jnp.int32)
     place = lax.dynamic_index_in_dim(table, me, 0, keepdims=False)
-
-    own_maps, pieces[-2], pieces[-4] = lax.optimization_barrier((own_maps, pieces[-2], pieces[-4]))
-    maps = lax.all_to_all(own_maps, axis, split_axis=0, concat_axis=0, tiled=True)
-    maps = maps.reshape(size * ranks, -1)
 
     shrunk = shrink(place, columns, pieces, row_adapter, adapter_down_weight.reshape(ranks, width), rank)
     near = min(4, size)
@@ -287,7 +319,8 @@
             lax.ppermute(plane, axis, [(d, (d + shift * near) % size) for d in range(size)])
         )
     gate, up = project(place, columns, pieces, gate_weight, up_weight, rows)
-    return combine(row_adapter, shrunk_pieces, gate, up, maps)
+    spread_shrunk = spread(row_adapter, shrunk_pieces, size * ranks)
+    return combine(spread_shrunk, gate, up, maps.reshape(size * ranks, -1))
 
 
 def solution(mesh):

time: 101 us -> 98.4 us (0.974)
  local copies, waits for them, and re-layouts: 20.5 us -> 2.28 us
  waiting for transfers between devices: 23.9 us -> 38.6 us
  Pallas kernels: 29 us -> 35 us
  starting transfers between devices: 26.4 us -> 22 us
    unnamed x70 -> x36, local copies, waits for them, and re-layouts: 19.7 us -> 1.48 us
    ppermute x3, waiting for transfers between devices: 0.01 us -> 9.33 us  [per_device(): lax.ppermute(plane, axis, [(d, (d + shift * near) % size) for d in range(...]
    ppermute x8, waiting for transfers between devices: 19.1 us -> 22.4 us  [moved(): return lax.ppermute(value, axis, pairs)]
    pallas_call x1 -> x2, Pallas kernels: 2.13 us -> 5.21 us  [the longest x1 4.23 us: combine(): pl.pallas_call(combine_kernel, grid=(units // tile,), in_specs=[pl.BlockS...]
    ppermute x3, starting transfers between devices: 7.77 us -> 5.16 us  [per_device(): lax.ppermute(plane, axis, [(d, (d + shift * near) % size) for d in range(...]
    ppermute x3, waiting for transfers between devices: 4.02 us -> 6.25 us  [per_device(): lax.ppermute(shrunk, axis, [(d, d ^ flip) for d in range(size)])]
    pallas_call x1, Pallas kernels: 3.43 us -> 5.33 us  [shrink(): pl.pallas_call(functools.partial(shrink_kernel, columns, len(pieces), ran...]
    pallas_call x1, Pallas kernels: 19.6 us -> 20.7 us  [project(): pl.pallas_call(functools.partial(project_kernel, columns, len(pieces)), g...]
  transfers between devices with their start and end apart: 24 -> 24, of which waited for: 12 -> 13; matrix products, arithmetic and copies ran while one was open for 1% -> 1% of each run, Pallas kernels for 27% -> 31%
where the time goes in v5:
time: 98.4 us; the launch traced here: 98.1 us
  waiting for transfers between devices  38.6 us (39%)
  Pallas kernels  35 us (36%)
  starting transfers between devices  22 us (22%)
  local copies, waits for them, and re-layouts  2.28 us (2%)
    ppermute x8, waiting for transfers between devices, moved(): return lax.ppermute(value, axis, pairs)  22.4 us
    pallas_call x1, Pallas kernels, project(): pl.pallas_call(functools.partial(project_kernel, columns, len(pieces)), g...  20.7 us
    ppermute x3, waiting for transfers between devices, per_device(): lax.ppermute(plane, axis, [(d, (d + shift * near) % size) for d in range(...  9.33 us
    ppermute x8, starting transfers between devices, moved(): return lax.ppermute(value, axis, pairs)  9.26 us
    ppermute x3, waiting for transfers between devices, per_device(): lax.ppermute(shrunk, axis, [(d, d ^ flip) for d in range(size)])  6.25 us
    pallas_call x1, Pallas kernels, shrink(): pl.pallas_call(functools.partial(shrink_kernel, columns, len(pieces), ran...  5.33 us
    ppermute x3, starting transfers between devices, per_device(): lax.ppermute(plane, axis, [(d, (d + shift * near) % size) for d in range(...  5.16 us
    pallas_call x1, Pallas kernels, combine(): pl.pallas_call(combine_kernel, grid=(units // tile,), in_specs=[pl.BlockS...  4.23 us
  transfers between devices with their start and end apart: 24, of which 13 were waited for; matrix products, arithmetic and copies ran while one was open for 1% of the time, Pallas kernels for 31%

profile of v5, /device:TPU:0, one launch (start us, length us, event | category | flops | bytes accessed | tf_op | source)
XLA Modules:
  0.0 98.1 jit_solution(11296651356855209161)
XLA Ops:
  0.0 3.0 %collective-permute-start = (bf16[16,8192]{1,0:T(8,128)(2,1)}, bf16[16,8192]{1,0:T(8,128)(2,1)S(1)}, u32[]{:S(2)}, u32[]{:S(2)}) collective-permute-start(bf16[16,8192]{1,0:T(8,128)(2,1)} %refs_0_.3), channel_id=1, source_target_pairs={{0,4},{1,5},{4,8},{5,9},{8,12},{9,13},{12,14},{13,15},{14,10},{15,... | collective-permute-start | bytes 786440 | tf_op jit(solution)/shard_map/ppermute | solution.py:30
  3.0 6.4 %collective-permute-done.refs_2_ = bf16[16,8192]{1,0:T(8,128)(2,1)S(1)} collective-permute-done((bf16[16,8192]{1,0:T(8,128)(2,1)}, bf16[16,8192]{1,0:T(8,128)(2,1)S(1)}, u32[]{:S(2)}, u32[]{:S(2)}) %collective-permute-start) | collective-permute-done | bytes 262176 | tf_op jit(solution)/shard_map/ppermute | solution.py:30
  9.5 1.5 %collective-permute-done.1.refs_3_ = bf16[16,8192]{1,0:T(8,128)(2,1)S(1)} collective-permute-done((bf16[16,8192]{1,0:T(8,128)(2,1)}, bf16[16,8192]{1,0:T(8,128)(2,1)S(1)}, u32[]{:S(2)}, u32[]{:S(2)}) %collective-permute-start.1) | collective-permute-done | bytes 262176 | tf_op jit(solution)/shard_map/ppermute | solution.py:30
  11.0 1.6 %collective-permute-start.3 = (bf16[16,8192]{1,0:T(8,128)(2,1)S(1)}, bf16[16,8192]{1,0:T(8,128)(2,1)S(1)}, u32[]{:S(2)}, u32[]{:S(2)}) collective-permute-start(bf16[16,8192]{1,0:T(8,128)(2,1)S(1)} %collective-permute-done.refs_2_), channel_id=1, source_target_pairs={{0,4},{1,5},{4,8},{5,9},{8,12},{9,13},{12,14},{13,15},{14,10},{15,... | collective-permute-start | bytes 786440 | tf_op jit(solution)/shard_map/ppermute | solution.py:30
  12.6 0.4 collective-permute-start.4
  13.1 0.5 collective-permute-start.6
  13.6 3.8 %split_columns.1 = bf16[16,64,1024]{2,1,0:T(8,128)(2,1)} custom-call(bf16[64,16384]{1,0:T(8,128)(2,1)} %bitcast.8), custom_call_target="tpu_custom_call" | custom-call | tf_op jit(solution)/shard_map/split_columns/pallas_call | solution.py:101
  17.4 0.5 collective-permute-done.3.refs_6_
  17.9 1.3 %collective-permute-done.4.refs_7_ = bf16[16,8192]{1,0:T(8,128)(2,1)S(1)} collective-permute-done((bf16[16,8192]{1,0:T(8,128)(2,1)S(1)}, bf16[16,8192]{1,0:T(8,128)(2,1)S(1)}, u32[]{:S(2)}, u32[]{:S(2)}) %collective-permute-start.4) | collective-permute-done | bytes 262176 | tf_op jit(solution)/shard_map/ppermute | solution.py:30
  19.3 1.6 %collective-permute-start.7 = (bf16[16,8192]{1,0:T(8,128)(2,1)S(1)}, bf16[16,8192]{1,0:T(8,128)(2,1)S(1)}, u32[]{:S(2)}, u32[]{:S(2)}) collective-permute-start(bf16[16,8192]{1,0:T(8,128)(2,1)S(1)} %collective-permute-done.3.refs_6_), channel_id=1, source_target_pairs={{0,4},{1,5},{4,8},{5,9},{8,12},{9,13},{12,14},{13,15},{14,10},{15,... | collective-permute-start | bytes 786440 | tf_op jit(solution)/shard_map/ppermute | solution.py:30
  20.9 0.4 collective-permute-start.8
  21.4 6.6 %collective-permute-done.7.refs_10_ = bf16[16,8192]{1,0:T(8,128)(2,1)S(1)} collective-permute-done((bf16[16,8192]{1,0:T(8,128)(2,1)S(1)}, bf16[16,8192]{1,0:T(8,128)(2,1)S(1)}, u32[]{:S(2)}, u32[]{:S(2)}) %collective-permute-start.7) | collective-permute-done | bytes 262176 | tf_op jit(solution)/shard_map/ppermute | solution.py:30
  28.0 1.3 %collective-permute-done.8.refs_11_ = bf16[16,8192]{1,0:T(8,128)(2,1)S(1)} collective-permute-done((bf16[16,8192]{1,0:T(8,128)(2,1)S(1)}, bf16[16,8192]{1,0:T(8,128)(2,1)S(1)}, u32[]{:S(2)}, u32[]{:S(2)}) %collective-permute-start.8) | collective-permute-done | bytes 262176 | tf_op jit(solution)/shard_map/ppermute | solution.py:30
  29.4 0.5 collective-permute-start.14
  30.0 1.6 %collective-permute-start.11 = (bf16[16,4096]{1,0:T(8,128)(2,1)S(1)}, bf16[16,4096]{1,0:T(8,128)(2,1)S(1)}, u32[]{:S(2)}, u32[]{:S(2)}) collective-permute-start(bf16[16,4096]{1,0:T(8,128)(2,1)S(1)} %slice.6), channel_id=1, source_target_pairs={{0,4},{1,5},{4,8},{5,9},{8,12},{9,13},{12,14},{13,15},{14,10},{15,... | collective-permute-start | bytes 393224 | tf_op jit(solution)/shard_map/ppermute | solution.py:30
  31.5 0.5 collective-permute-start.12
  32.0 3.5 %collective-permute-done.11.refs_14_ = bf16[16,4096]{1,0:T(8,128)(2,1)S(1)} collective-permute-done((bf16[16,4096]{1,0:T(8,128)(2,1)S(1)}, bf16[16,4096]{1,0:T(8,128)(2,1)S(1)}, u32[]{:S(2)}, u32[]{:S(2)}) %collective-permute-start.11) | collective-permute-done | bytes 131104 | tf_op jit(solution)/shard_map/ppermute | solution.py:30
  35.5 1.2 %collective-permute-done.12.refs_15_ = bf16[16,4096]{1,0:T(8,128)(2,1)S(1)} collective-permute-done((bf16[16,4096]{1,0:T(8,128)(2,1)S(1)}, bf16[16,4096]{1,0:T(8,128)(2,1)S(1)}, u32[]{:S(2)}, u32[]{:S(2)}) %collective-permute-start.12) | collective-permute-done | bytes 131104 | tf_op jit(solution)/shard_map/ppermute | solution.py:30
  36.8 0.6 copy-done.15
  37.6 3.7 %all-to-all-start = ((bf16[16,64,1024]{2,1,0:T(8,128)(2,1)}), bf16[16,64,1024]{2,1,0:T(8,128)(2,1)S(1)}, u32[]{:S(2)}, u32[]{:S(2)}) async-start(bf16[16,64,1024]{2,1,0:T(8,128)(2,1)} %split_columns.1), calls=%async_computation | async-start | bytes 4194304 | tf_op jit(solution)/shard_map/all_to_all | solution.py:302
  41.9 0.7 dynamic-slice_bitcast_fusion.place
  42.7 0.4 collective-permute-done.16.refs_17_
  43.8 5.3 %shrink.1 = bf16[64,256]{1,0:T(8,128)(2,1)S(1)} custom-call(s32[19]{0:T(128)S(1)} %dynamic-slice_bitcast_fusion.place, s32[1,256]{1,0:T(1,128)S(1)} %bitcast.7, bf16[64,8192]{1,0:T(8,128)(2,1)} %bitcast.9, bf16[16,8192]{1,0:T(8,128)(2,1)} %refs_0_.3, bf16[16,8192]{1,0:T(8,128)(2,1)} %copy-done.5, bf16[16,8192]{1,0:T(8,128)(2,1)} %copy-done.3, ...), custom_call_target="tpu_custom_call" | custom-call | flops 268435456 | bytes 5242880 | tf_op jit(solution)/shard_map/shrink/pallas_call | solution.py:138
  49.5 1.7 %collective-permute-start.18 = (bf16[64,256]{1,0:T(8,128)(2,1)S(1)}, bf16[64,256]{1,0:T(8,128)(2,1)S(1)}, u32[]{:S(2)}, u32[]{:S(2)}) collective-permute-start(bf16[64,256]{1,0:T(8,128)(2,1)S(1)} %shrink.1), channel_id=1, source_target_pairs={{0,2},{1,3},{2,0},{3,1},{4,6},{5,7},{6,4},{7,5},{8,10},{9,11},{10,... | collective-permute-start | bytes 98312 | tf_op jit(solution)/shard_map/ppermute | solution.py:315
  51.2 3.9 %collective-permute-done.18 = bf16[64,256]{1,0:T(8,128)(2,1)S(1)} collective-permute-done((bf16[64,256]{1,0:T(8,128)(2,1)S(1)}, bf16[64,256]{1,0:T(8,128)(2,1)S(1)}, u32[]{:S(2)}, u32[]{:S(2)}) %collective-permute-start.18) | collective-permute-done | bytes 32800 | tf_op jit(solution)/shard_map/ppermute | solution.py:315
  55.1 2.4 %collective-permute-done.19 = bf16[64,256]{1,0:T(8,128)(2,1)S(1)} collective-permute-done((bf16[64,256]{1,0:T(8,128)(2,1)S(1)}, bf16[64,256]{1,0:T(8,128)(2,1)S(1)}, u32[]{:S(2)}, u32[]{:S(2)}) %collective-permute-start.19) | collective-permute-done | bytes 32800 | tf_op jit(solution)/shard_map/ppermute | solution.py:315
  57.7 3.3 %collective-permute-start.21 = (bf16[64,256]{1,0:T(8,128)(2,1)S(1)}, bf16[64,256]{1,0:T(8,128)(2,1)S(1)}, u32[]{:S(2)}, u32[]{:S(2)}) collective-permute-start(bf16[64,256]{1,0:T(8,128)(2,1)S(1)} %add_add_fusion.refs_0_), channel_id=1, source_target_pairs={{0,8},{1,9},{2,10},{3,11},{4,12},{5,13},{6,14},{7,15},{8,0},{9,1},... | collective-permute-start | bytes 98312 | tf_op jit(solution)/shard_map/ppermute | solution.py:319
  61.0 1.6 %collective-permute-start.22 = (bf16[64,256]{1,0:T(8,128)(2,1)S(1)}, bf16[64,256]{1,0:T(8,128)(2,1)S(1)}, u32[]{:S(2)}, u32[]{:S(2)}) collective-permute-start(bf16[64,256]{1,0:T(8,128)(2,1)S(1)} %add_add_fusion.refs_0_), channel_id=1, source_target_pairs={{0,12},{1,13},{2,14},{3,15},{4,0},{5,1},{6,2},{7,3},{8,4},{9,5},{1... | collective-permute-start | bytes 98312 | tf_op jit(solution)/shard_map/ppermute | solution.py:319
  62.7 20.7 %project.1 = (f32[256,1024]{1,0:T(8,128)}, f32[256,1024]{1,0:T(8,128)}) custom-call(s32[19]{0:T(128)S(1)} %dynamic-slice_bitcast_fusion.place, bf16[8192,1024]{1,0:T(8,128)(2,1)} %gate_weight_ref.1, bf16[8192,1024]{1,0:T(8,128)(2,1)} %up_weight_ref.1, bf16[16,8192]{1,0:T(8,128)(2,1)} %refs_0_.3, bf16[16,8192]{1,0:T(8,128)(2,1)} %copy-done.5, ...), custom_call_target="tpu_custom_call" | custom-call | flops 8589934592 | bytes 37748736 | tf_op jit(solution)/shard_map/project/pallas_call | solution.py:191
  83.4 9.3 %collective-permute-done.21.refs_2_ = bf16[64,256]{1,0:T(8,128)(2,1)S(1)} collective-permute-done((bf16[64,256]{1,0:T(8,128)(2,1)S(1)}, bf16[64,256]{1,0:T(8,128)(2,1)S(1)}, u32[]{:S(2)}, u32[]{:S(2)}) %collective-permute-start.21) | collective-permute-done | bytes 32800 | tf_op jit(solution)/shard_map/ppermute | solution.py:319
  92.8 1.0 spread.1.shrunk_ref
  93.8 4.2 %combine.1 = bf16[256,1024]{1,0:T(8,128)(2,1)} custom-call(bf16[256,1024]{1,0:T(8,128)(2,1)} %spread.1.shrunk_ref, f32[256,1024]{1,0:T(8,128)} %get-tuple-element.58.gate_ref, f32[256,1024]{1,0:T(8,128)} %get-tuple-element.59.up_ref, bf16[1024,1024]{1,0:T(8,128)(2,1)S(1)} %bitcast.6), custom_call_target="tpu_custom_call" | custom-call | flops 536870912 | bytes 2621440 | tf_op jit(solution)/shard_map/combine/pallas_call | solution.py:254
  (62 shorter events, 2.4 us)
Async XLA Ops:
  0.0 9.5 %collective-permute-start = (bf16[16,8192]{1,0:T(8,128)(2,1)}, bf16[16,8192]{1,0:T(8,128)(2,1)S(1)}, u32[]{:S(2)}, u32[]{:S(2)}) collective-permute-start(bf16[16,8192]{1,0:T(8,128)(2,1)} %refs_0_.3), channel_id=1, source_target_pairs={{0,4},{1,5},{4,8},{5,9},{8,12},{9,13},{12,14},{13,15},{14,10},{15,... | collective-permute-start | bytes 786440 | tf_op jit(solution)/shard_map/ppermute | solution.py:30
  3.0 8.0 %collective-permute-start.1 = (bf16[16,8192]{1,0:T(8,128)(2,1)}, bf16[16,8192]{1,0:T(8,128)(2,1)S(1)}, u32[]{:S(2)}, u32[]{:S(2)}) collective-permute-start(bf16[16,8192]{1,0:T(8,128)(2,1)} %refs_0_.3), channel_id=1, source_target_pairs={{0,2},{1,3},{4,0},{5,1},{8,4},{9,5},{12,8},{13,9},{14,12},{15,13},... | collective-permute-start | bytes 786440 | tf_op jit(solution)/shard_map/ppermute | solution.py:30
  3.0 8.0 %collective-permute-start.2 = (bf16[16,8192]{1,0:T(8,128)(2,1)}, bf16[16,8192]{1,0:T(8,128)(2,1)S(1)}, u32[]{:S(2)}, u32[]{:S(2)}) collective-permute-start(bf16[16,8192]{1,0:T(8,128)(2,1)} %refs_0_.3), channel_id=1, source_target_pairs={{0,1},{1,0},{2,3},{3,2},{4,5},{5,4},{6,7},{7,6},{8,9},{9,8},{10,11... | collective-permute-start | bytes 786440 | tf_op jit(solution)/shard_map/ppermute | solution.py:33
  11.0 6.9 %collective-permute-start.3 = (bf16[16,8192]{1,0:T(8,128)(2,1)S(1)}, bf16[16,8192]{1,0:T(8,128)(2,1)S(1)}, u32[]{:S(2)}, u32[]{:S(2)}) collective-permute-start(bf16[16,8192]{1,0:T(8,128)(2,1)S(1)} %collective-permute-done.refs_2_), channel_id=1, source_target_pairs={{0,4},{1,5},{4,8},{5,9},{8,12},{9,13},{12,14},{13,15},{14,10},{15,... | collective-permute-start | bytes 786440 | tf_op jit(solution)/shard_map/ppermute | solution.py:30
  12.6 6.6 %collective-permute-start.4 = (bf16[16,8192]{1,0:T(8,128)(2,1)S(1)}, bf16[16,8192]{1,0:T(8,128)(2,1)S(1)}, u32[]{:S(2)}, u32[]{:S(2)}) collective-permute-start(bf16[16,8192]{1,0:T(8,128)(2,1)S(1)} %collective-permute-done.1.refs_3_), channel_id=1, source_target_pairs={{0,2},{1,3},{4,0},{5,1},{8,4},{9,5},{12,8},{13,9},{14,12},{15,13},... | collective-permute-start | bytes 786440 | tf_op jit(solution)/shard_map/ppermute | solution.py:30
  13.1 6.1 %collective-permute-start.5 = (bf16[16,8192]{1,0:T(8,128)(2,1)S(1)}, bf16[16,8192]{1,0:T(8,128)(2,1)S(1)}, u32[]{:S(2)}, u32[]{:S(2)}) collective-permute-start(bf16[16,8192]{1,0:T(8,128)(2,1)S(1)} %collective-permute-done.refs_2_), channel_id=1, source_target_pairs={{0,1},{1,0},{2,3},{3,2},{4,5},{5,4},{6,7},{7,6},{8,9},{9,8},{10,11... | collective-permute-start | bytes 786440 | tf_op jit(solution)/shard_map/ppermute | solution.py:33
  13.1 6.1 %collective-permute-start.6 = (bf16[16,8192]{1,0:T(8,128)(2,1)S(1)}, bf16[16,8192]{1,0:T(8,128)(2,1)S(1)}, u32[]{:S(2)}, u32[]{:S(2)}) collective-permute-start(bf16[16,8192]{1,0:T(8,128)(2,1)S(1)} %collective-permute-done.1.refs_3_), channel_id=1, source_target_pairs={{0,1},{1,0},{2,3},{3,2},{4,5},{5,4},{6,7},{7,6},{8,9},{9,8},{10,11... | collective-permute-start | bytes 786440 | tf_op jit(solution)/shard_map/ppermute | solution.py:33
  17.9 12.0 %copy-start.6 = (bf16[16,8192]{1,0:T(8,128)(2,1)}, bf16[16,8192]{1,0:T(8,128)(2,1)S(1)}, u32[]{:S(2)}) copy-start(bf16[16,8192]{1,0:T(8,128)(2,1)S(1)} %collective-permute-done.3.refs_6_) | copy-start | bytes 786436
  19.2 17.5 %copy-start.7 = (bf16[16,8192]{1,0:T(8,128)(2,1)}, bf16[16,8192]{1,0:T(8,128)(2,1)S(1)}, u32[]{:S(2)}) copy-start(bf16[16,8192]{1,0:T(8,128)(2,1)S(1)} %collective-permute-done.4.refs_7_) | copy-start | bytes 786436
  19.2 17.5 %copy-start.8 = (bf16[16,8192]{1,0:T(8,128)(2,1)}, bf16[16,8192]{1,0:T(8,128)(2,1)S(1)}, u32[]{:S(2)}) copy-start(bf16[16,8192]{1,0:T(8,128)(2,1)S(1)} %collective-permute-done.5.refs_4_) | copy-start | bytes 786436
  19.2 17.5 %copy-start.9 = (bf16[16,8192]{1,0:T(8,128)(2,1)}, bf16[16,8192]{1,0:T(8,128)(2,1)S(1)}, u32[]{:S(2)}) copy-start(bf16[16,8192]{1,0:T(8,128)(2,1)S(1)} %collective-permute-done.6.refs_5_) | copy-start | bytes 786436
  19.2 2.2 %collective-permute-start.10 = (bf16[16,8192]{1,0:T(8,128)(2,1)S(1)}, bf16[16,8192]{1,0:T(8,128)(2,1)S(1)}, u32[]{:S(2)}, u32[]{:S(2)}) collective-permute-start(bf16[16,8192]{1,0:T(8,128)(2,1)S(1)} %collective-permute-done.4.refs_7_), channel_id=1, source_target_pairs={{0,1},{1,0},{2,3},{3,2},{4,5},{5,4},{6,7},{7,6},{8,9},{9,8},{10,11... | collective-permute-start | bytes 786440 | tf_op jit(solution)/shard_map/ppermute | solution.py:33
  19.3 8.7 %collective-permute-start.7 = (bf16[16,8192]{1,0:T(8,128)(2,1)S(1)}, bf16[16,8192]{1,0:T(8,128)(2,1)S(1)}, u32[]{:S(2)}, u32[]{:S(2)}) collective-permute-start(bf16[16,8192]{1,0:T(8,128)(2,1)S(1)} %collective-permute-done.3.refs_6_), channel_id=1, source_target_pairs={{0,4},{1,5},{4,8},{5,9},{8,12},{9,13},{12,14},{13,15},{14,10},{15,... | collective-permute-start | bytes 786440 | tf_op jit(solution)/shard_map/ppermute | solution.py:30
  20.9 8.4 %collective-permute-start.8 = (bf16[16,8192]{1,0:T(8,128)(2,1)S(1)}, bf16[16,8192]{1,0:T(8,128)(2,1)S(1)}, u32[]{:S(2)}, u32[]{:S(2)}) collective-permute-start(bf16[16,8192]{1,0:T(8,128)(2,1)S(1)} %collective-permute-done.4.refs_7_), channel_id=1, source_target_pairs={{0,2},{1,3},{4,0},{5,1},{8,4},{9,5},{12,8},{13,9},{14,12},{15,13},... | collective-permute-start | bytes 786440 | tf_op jit(solution)/shard_map/ppermute | solution.py:30
  21.4 7.9 %collective-permute-start.9 = (bf16[16,8192]{1,0:T(8,128)(2,1)S(1)}, bf16[16,8192]{1,0:T(8,128)(2,1)S(1)}, u32[]{:S(2)}, u32[]{:S(2)}) collective-permute-start(bf16[16,8192]{1,0:T(8,128)(2,1)S(1)} %collective-permute-done.3.refs_6_), channel_id=1, source_target_pairs={{0,1},{1,0},{2,3},{3,2},{4,5},{5,4},{6,7},{7,6},{8,9},{9,8},{10,11... | collective-permute-start | bytes 786440 | tf_op jit(solution)/shard_map/ppermute | solution.py:33
  21.4 16.1 %copy-start.10 = (bf16[16,8192]{1,0:T(8,128)(2,1)}, bf16[16,8192]{1,0:T(8,128)(2,1)S(1)}, u32[]{:S(2)}) copy-start(bf16[16,8192]{1,0:T(8,128)(2,1)S(1)} %collective-permute-done.10.refs_9_) | copy-start | bytes 786436
  28.0 9.5 %copy-start.1 = (bf16[16,8192]{1,0:T(8,128)(2,1)}, bf16[16,8192]{1,0:T(8,128)(2,1)S(1)}, u32[]{:S(2)}) copy-start(bf16[16,8192]{1,0:T(8,128)(2,1)S(1)} %collective-permute-done.7.refs_10_) | copy-start | bytes 786436
  29.3 8.2 %copy-start.2 = (bf16[16,8192]{1,0:T(8,128)(2,1)}, bf16[16,8192]{1,0:T(8,128)(2,1)S(1)}, u32[]{:S(2)}) copy-start(bf16[16,8192]{1,0:T(8,128)(2,1)S(1)} %collective-permute-done.8.refs_11_) | copy-start | bytes 786436
  29.3 7.4 %collective-permute-start.13 = (bf16[16,8192]{1,0:T(8,128)(2,1)S(1)}, bf16[16,8192]{1,0:T(8,128)(2,1)S(1)}, u32[]{:S(2)}, u32[]{:S(2)}) collective-permute-start(bf16[16,8192]{1,0:T(8,128)(2,1)S(1)} %collective-permute-done.7.refs_10_), channel_id=1, source_target_pairs={{0,1},{1,0},{2,3},{3,2},{4,5},{5,4},{6,7},{7,6},{8,9},{9,8},{10,11... | collective-permute-start | bytes 786440 | tf_op jit(solution)/shard_map/ppermute | solution.py:33
  29.4 7.3 %collective-permute-start.14 = (bf16[16,8192]{1,0:T(8,128)(2,1)S(1)}, bf16[16,8192]{1,0:T(8,128)(2,1)S(1)}, u32[]{:S(2)}, u32[]{:S(2)}) collective-permute-start(bf16[16,8192]{1,0:T(8,128)(2,1)S(1)} %collective-permute-done.8.refs_11_), channel_id=1, source_target_pairs={{0,1},{1,0},{2,3},{3,2},{4,5},{5,4},{6,7},{7,6},{8,9},{9,8},{10,11... | collective-permute-start | bytes 786440 | tf_op jit(solution)/shard_map/ppermute | solution.py:33
  29.9 13.9 %copy-start = (s32[256]{0:T(256)S(1)}, s32[256]{0:T(256)}, u32[]{:S(2)}) copy-start(s32[256]{0:T(256)} %param.14) | copy-start | bytes 3076
  30.0 5.5 %collective-permute-start.11 = (bf16[16,4096]{1,0:T(8,128)(2,1)S(1)}, bf16[16,4096]{1,0:T(8,128)(2,1)S(1)}, u32[]{:S(2)}, u32[]{:S(2)}) collective-permute-start(bf16[16,4096]{1,0:T(8,128)(2,1)S(1)} %slice.6), channel_id=1, source_target_pairs={{0,4},{1,5},{4,8},{5,9},{8,12},{9,13},{12,14},{13,15},{14,10},{15,... | collective-permute-start | bytes 393224 | tf_op jit(solution)/shard_map/ppermute | solution.py:30
  31.5 5.2 %collective-permute-start.12 = (bf16[16,4096]{1,0:T(8,128)(2,1)S(1)}, bf16[16,4096]{1,0:T(8,128)(2,1)S(1)}, u32[]{:S(2)}, u32[]{:S(2)}) collective-permute-start(bf16[16,4096]{1,0:T(8,128)(2,1)S(1)} %slice.7), channel_id=1, source_target_pairs={{0,2},{1,3},{4,0},{5,1},{8,4},{9,5},{12,8},{13,9},{14,12},{15,13},... | collective-permute-start | bytes 393224 | tf_op jit(solution)/shard_map/ppermute | solution.py:30
  37.6 56.3 %all-to-all-start = ((bf16[16,64,1024]{2,1,0:T(8,128)(2,1)}), bf16[16,64,1024]{2,1,0:T(8,128)(2,1)S(1)}, u32[]{:S(2)}, u32[]{:S(2)}) async-start(bf16[16,64,1024]{2,1,0:T(8,128)(2,1)} %split_columns.1), calls=%async_computation | async-start | bytes 4194304 | tf_op jit(solution)/shard_map/all_to_all | solution.py:302
  41.3 1.4 %collective-permute-start.15 = (bf16[16,4096]{1,0:T(8,128)(2,1)S(1)}, bf16[16,4096]{1,0:T(8,128)(2,1)S(1)}, u32[]{:S(2)}, u32[]{:S(2)}) collective-permute-start(bf16[16,4096]{1,0:T(8,128)(2,1)S(1)} %collective-permute-done.11.refs_14_), channel_id=1, source_target_pairs={{0,1},{1,0},{2,3},{3,2},{4,5},{5,4},{6,7},{7,6},{8,9},{9,8},{10,11... | collective-permute-start | bytes 393224 | tf_op jit(solution)/shard_map/ppermute | solution.py:33
  41.6 1.6 %collective-permute-start.16 = (bf16[16,4096]{1,0:T(8,128)(2,1)}, bf16[16,4096]{1,0:T(8,128)(2,1)S(1)}, u32[]{:S(2)}, u32[]{:S(2)}) collective-permute-start(bf16[16,4096]{1,0:T(8,128)(2,1)} %copy-done.15), channel_id=1, source_target_pairs={{0,1},{1,0},{2,3},{3,2},{4,5},{5,4},{6,7},{7,6},{8,9},{9,8},{10,11... | collective-permute-start | bytes 393224 | tf_op jit(solution)/shard_map/ppermute | solution.py:33
  49.1 2.1 %collective-permute-start.17 = (bf16[64,256]{1,0:T(8,128)(2,1)S(1)}, bf16[64,256]{1,0:T(8,128)(2,1)S(1)}, u32[]{:S(2)}, u32[]{:S(2)}) collective-permute-start(bf16[64,256]{1,0:T(8,128)(2,1)S(1)} %shrink.1), channel_id=1, source_target_pairs={{0,1},{1,0},{2,3},{3,2},{4,5},{5,4},{6,7},{7,6},{8,9},{9,8},{10,11... | collective-permute-start | bytes 98312 | tf_op jit(solution)/shard_map/ppermute | solution.py:315
  49.5 5.7 %collective-permute-start.18 = (bf16[64,256]{1,0:T(8,128)(2,1)S(1)}, bf16[64,256]{1,0:T(8,128)(2,1)S(1)}, u32[]{:S(2)}, u32[]{:S(2)}) collective-permute-start(bf16[64,256]{1,0:T(8,128)(2,1)S(1)} %shrink.1), channel_id=1, source_target_pairs={{0,2},{1,3},{2,0},{3,1},{4,6},{5,7},{6,4},{7,5},{8,10},{9,11},{10,... | collective-permute-start | bytes 98312 | tf_op jit(solution)/shard_map/ppermute | solution.py:315
  51.2 6.3 %collective-permute-start.19 = (bf16[64,256]{1,0:T(8,128)(2,1)S(1)}, bf16[64,256]{1,0:T(8,128)(2,1)S(1)}, u32[]{:S(2)}, u32[]{:S(2)}) collective-permute-start(bf16[64,256]{1,0:T(8,128)(2,1)S(1)} %shrink.1), channel_id=1, source_target_pairs={{0,3},{1,2},{2,1},{3,0},{4,7},{5,6},{6,5},{7,4},{8,11},{9,10},{10,... | collective-permute-start | bytes 98312 | tf_op jit(solution)/shard_map/ppermute | solution.py:315
  57.5 25.9 %collective-permute-start.20 = (bf16[64,256]{1,0:T(8,128)(2,1)S(1)}, bf16[64,256]{1,0:T(8,128)(2,1)S(1)}, u32[]{:S(2)}, u32[]{:S(2)}) collective-permute-start(bf16[64,256]{1,0:T(8,128)(2,1)S(1)} %add_add_fusion.refs_0_), channel_id=1, source_target_pairs={{0,4},{1,5},{2,6},{3,7},{4,8},{5,9},{6,10},{7,11},{8,12},{9,13},{1... | collective-permute-start | bytes 98312 | tf_op jit(solution)/shard_map/ppermute | solution.py:319
  57.7 35.0 %collective-permute-start.21 = (bf16[64,256]{1,0:T(8,128)(2,1)S(1)}, bf16[64,256]{1,0:T(8,128)(2,1)S(1)}, u32[]{:S(2)}, u32[]{:S(2)}) collective-permute-start(bf16[64,256]{1,0:T(8,128)(2,1)S(1)} %add_add_fusion.refs_0_), channel_id=1, source_target_pairs={{0,8},{1,9},{2,10},{3,11},{4,12},{5,13},{6,14},{7,15},{8,0},{9,1},... | collective-permute-start | bytes 98312 | tf_op jit(solution)/shard_map/ppermute | solution.py:319
  61.0 31.7 %collective-permute-start.22 = (bf16[64,256]{1,0:T(8,128)(2,1)S(1)}, bf16[64,256]{1,0:T(8,128)(2,1)S(1)}, u32[]{:S(2)}, u32[]{:S(2)}) collective-permute-start(bf16[64,256]{1,0:T(8,128)(2,1)S(1)} %add_add_fusion.refs_0_), channel_id=1, source_target_pairs={{0,12},{1,13},{2,14},{3,15},{4,0},{5,1},{6,2},{7,3},{8,4},{9,5},{1... | collective-permute-start | bytes 98312 | tf_op jit(solution)/shard_map/ppermute | solution.py:319
  (10 other events, 40.0 us)

commit v6 on v3

--- a/solution.py
+++ b/solution.py
@@ -16,7 +16,7 @@
     return list(range(0, chips, 2)) + list(range(chips - 1, 0, -2))
 
 
-def ring_gather(block, axis, extra, prepare):
+def ring_gather(block, axis, beside):
     size = lax.axis_size(axis)
     chips = size // CORES
     ring = chip_ring(chips)
@@ -29,37 +29,28 @@
         ]
         return lax.ppermute(value, axis, pairs)
 
-    def other_core(value):
-        return lax.ppermute(value, axis, [(d, d ^ 1) for d in range(size)])
-
-    pieces = []
-    where = [[] for _ in range(size)]
-
-    def arrived(value, column, distance):
-        pieces.append((value, column))
-        pieces.append((other_core(value), column))
-        for device in range(size):
-            chip = ring[(ring.index(device // CORES) + distance) % chips]
-            core = device % CORES
-            where[device] += [chip * CORES + core, chip * CORES + 1 - core]
-
-    arrived(block, 0, 0)
+    pieces = [(block, 0, 0)]
     right = left = block
     for step in range(1, chips // 2):
-        if step == 2:
-            extra, right, left = lax.optimization_barrier((extra, right, left))
-            extra = prepare(extra)
-        if step == 3:
-            extra, right, left = lax.optimization_barrier((extra, right, left))
-        right = moved(right, 1)
-        left = moved(left, -1)
-        arrived(right, 0, -step)
-        arrived(left, 0, step)
+        right, left = beside(step, (moved(right, 1), moved(left, -1)))
+        pieces += [(right, 0, -step), (left, 0, step)]
     half = block.shape[1] // 2
     far = chips // 2
-    arrived(moved(right[:, :half], 1), 0, far)
-    arrived(moved(left[:, half:], -1), half, far)
-    return pieces, where, extra
+    right, left = beside(far, (moved(right[:, :half], 1), moved(left[:, half:], -1)))
+    pieces += [(right, 0, far), (left, half, far)]
+
+    flips = [(d, d ^ 1) for d in range(size)]
+    found = [(value, column) for value, column, _ in pieces]
+    found += [(lax.ppermute(value, axis, flips), column) for value, column, _ in pieces]
+    where = [
+        [
+            ring[(ring.index(device // CORES) + distance) % chips] * CORES + core
+            for core in (device % CORES, 1 - device % CORES)
+            for _, _, distance in pieces
+        ]
+        for device in range(size)
+    ]
+    return found, where
 
 
 def assemble(spots, columns, piece_refs, tokens_vmem, sems):
@@ -98,7 +89,11 @@
     )(weights)
 
 
-HBM_SPEC = pl.BlockSpec(memory_space=pltpu.HBM)
+def in_hbm(values):
+    return [pltpu.with_memory_space_constraint(value, pltpu.HBM) for value in values]
+
+
+ANY_SPEC = pl.BlockSpec(memory_space=pl.ANY)
 
 
 def shrink_kernel(columns, pieces, rank, place, users_ref, down_ref, *refs):
@@ -130,7 +125,7 @@
                 pl.BlockSpec((1, rows), lambda i, s: (0, 0)),
                 pl.BlockSpec((ranks, width), lambda i, s: (0, 0)),
             ]
-            + [HBM_SPEC] * len(pieces),
+            + [ANY_SPEC] * len(pieces),
             out_specs=pl.BlockSpec((rank, rows), lambda i, s: (0, 0)),
             scratch_shapes=[
                 pltpu.VMEM((rows, width), jnp.bfloat16),
@@ -138,12 +133,12 @@
             ],
         ),
         out_shape=jax.ShapeDtypeStruct((rank, rows), jnp.bfloat16),
-        compiler_params=pltpu.CompilerParams(vmem_limit_bytes=40 * MIB),
+        compiler_params=pltpu.CompilerParams(vmem_limit_bytes=rows * width * 2 + 8 * MIB),
         cost_estimate=pl.CostEstimate(
             flops=2 * rows * width * ranks, bytes_accessed=2 * (rows + ranks) * width, transcendentals=0
         ),
         name="shrink",
-    )(place, row_adapter.reshape(1, rows), down, *pieces)
+    )(place, row_adapter.reshape(1, rows), *in_hbm([down, *pieces]))
 
 
 def project_kernel(columns, pieces, place, gate_weight_ref, up_weight_ref, *refs):
@@ -173,13 +168,13 @@
     depth = min(1024, width)
     weight_spec = pl.BlockSpec((depth, units), lambda k, s: (k, 0))
     out_spec = pl.BlockSpec((rows, units), lambda k, s: (0, 0))
-    out = jax.ShapeDtypeStruct((rows, units), jnp.float32)
+    out = pltpu.HBM((rows, units), jnp.float32)
     return pl.pallas_call(
         functools.partial(project_kernel, columns, len(pieces)),
         grid_spec=pltpu.PrefetchScalarGridSpec(
             num_scalar_prefetch=1,
             grid=(width // depth,),
-            in_specs=[weight_spec, weight_spec] + [HBM_SPEC] * len(pieces),
+            in_specs=[weight_spec, weight_spec] + [ANY_SPEC] * len(pieces),
             out_specs=[out_spec, out_spec],
             scratch_shapes=[
                 pltpu.VMEM((rows, width), jnp.bfloat16),
@@ -187,20 +182,20 @@
             ],
         ),
         out_shape=[out, out],
-        compiler_params=pltpu.CompilerParams(vmem_limit_bytes=48 * MIB),
+        compiler_params=pltpu.CompilerParams(vmem_limit_bytes=rows * width * 2 + 20 * MIB),
         cost_estimate=pl.CostEstimate(
             flops=4 * rows * width * units,
             bytes_accessed=2 * (rows + 2 * units) * width,
             transcendentals=rows * units,
         ),
         name="project",
-    )(place, gate_weight, up_weight, *pieces)
+    )(place, *in_hbm([gate_weight, up_weight, *pieces]))
 
 
 def combine_kernel(pieces, users_ref, gate_ref, up_ref, maps_ref, *refs):
     piece_refs = refs[:pieces]
     out_ref, shrunk_vmem = refs[pieces:]
-    rank, rows = piece_refs[0].shape
+    rank = piece_refs[0].shape[0]
 
     @pl.when(pl.program_id(0) == 0)
     def _():
@@ -239,12 +234,12 @@
         out_specs=column_spec,
         scratch_shapes=[pltpu.VMEM((rows, ranks_all), jnp.bfloat16)],
         out_shape=jax.ShapeDtypeStruct((rows, units), jnp.bfloat16),
-        compiler_params=pltpu.CompilerParams(vmem_limit_bytes=48 * MIB),
+        compiler_params=pltpu.CompilerParams(vmem_limit_bytes=rows * ranks_all * 4 + 16 * MIB),
         cost_estimate=pl.CostEstimate(
             flops=2 * rows * ranks_all * units, bytes_accessed=10 * rows * units, transcendentals=0
         ),
         name="combine",
-    )(users, gate, up, maps, *pieces)
+    )(*in_hbm([users, gate, up]), maps, *in_hbm(pieces))
 
 
 def per_device(
@@ -264,17 +259,26 @@
     ranks = resident * rank
     rows = row_adapter.shape[0]
 
-    found, where, own_maps = ring_gather(
-        tokens, axis, adapter_up_weight.reshape(ranks, -1), lambda weights: split_columns(weights, size)
-    )
+    own_maps = adapter_up_weight.reshape(ranks, -1)
+    steps = size // CORES // 2
+    maps = None
+
+    def beside(step, values):
+        nonlocal own_maps, maps
+        if step not in (1, 2, steps):
+            return values
+        own_maps, *values = lax.optimization_barrier((own_maps, *values))
+        if step == 1:
+            own_maps = split_columns(own_maps, size)
+        if step == steps:
+            maps = lax.all_to_all(own_maps, axis, split_axis=0, concat_axis=0, tiled=True)
+        return values
+
+    found, where = ring_gather(tokens, axis, beside)
     pieces = [piece for piece, _ in found]
     columns = [column for _, column in found]
     table = jnp.array([row + [device] for device, row in enumerate(where)], jnp.int32)
     place = lax.dynamic_index_in_dim(table, me, 0, keepdims=False)
-
-    own_maps, pieces[-2], pieces[-4] = lax.optimization_barrier((own_maps, pieces[-2], pieces[-4]))
-    maps = lax.all_to_all(own_maps, axis, split_axis=0, concat_axis=0, tiled=True)
-    maps = maps.reshape(size * ranks, -1)
 
     shrunk = shrink(place, columns, pieces, row_adapter, adapter_down_weight.reshape(ranks, width), rank)
     near = min(4, size)
@@ -287,7 +291,7 @@
             lax.ppermute(plane, axis, [(d, (d + shift * near) % size) for d in range(size)])
         )
     gate, up = project(place, columns, pieces, gate_weight, up_weight, rows)
-    return combine(row_adapter, shrunk_pieces, gate, up, maps)
+    return combine(row_adapter, shrunk_pieces, gate, up, maps.reshape(size * ranks, -1))
 
 
 def solution(mesh):

time: 101 us -> 93.3 us (0.924)
  local copies, waits for them, and re-layouts: 20.5 us -> 3.36 us
  waiting for transfers between devices: 23.9 us -> 33.9 us
  Pallas kernels: 29 us -> 33.1 us
  starting transfers between devices: 26.4 us -> 22.4 us
    unnamed x70 -> x42, local copies, waits for them, and re-layouts: 19.7 us -> 1.9 us
    ppermute x3, waiting for transfers between devices: 0.01 us -> 8.25 us  [per_device(): lax.ppermute(plane, axis, [(d, (d + shift * near) % size) for d in range(...]
    ppermute x3, starting transfers between devices: 7.77 us -> 4.64 us  [per_device(): lax.ppermute(plane, axis, [(d, (d + shift * near) % size) for d in range(...]
    pallas_call x1, Pallas kernels: 3.43 us -> 5.33 us  [shrink(): pl.pallas_call(functools.partial(shrink_kernel, columns, len(pieces), ran...]
    pallas_call x1, Pallas kernels: 19.6 us -> 20.9 us  [project(): pl.pallas_call(functools.partial(project_kernel, columns, len(pieces)), g...]
    all_to_all x1, starting transfers between devices: 4.81 us -> 3.72 us  [beside(): lax.all_to_all(own_maps, axis, split_axis=0, concat_axis=0, tiled=True)]
    ppermute x8, waiting for transfers between devices: 19.1 us -> 20.1 us  [moved(): return lax.ppermute(value, axis, pairs)]
    pallas_call x1, Pallas kernels: 2.13 us -> 3.15 us  [combine(): pl.pallas_call(functools.partial(combine_kernel, len(pieces)), grid=(unit...]
  transfers between devices with their start and end apart: 24 -> 24, of which waited for: 12 -> 15; matrix products, arithmetic and copies ran while one was open for 1% -> 1% of each run, Pallas kernels for 27% -> 32%
where the time goes in v6:
time: 93.3 us; the launch traced here: 93 us
  waiting for transfers between devices  33.9 us (36%)
  Pallas kernels  33.1 us (35%)
  starting transfers between devices  22.4 us (24%)
  local copies, waits for them, and re-layouts  3.36 us (4%)
    pallas_call x1, Pallas kernels, project(): pl.pallas_call(functools.partial(project_kernel, columns, len(pieces)), g...  20.9 us
    ppermute x8, waiting for transfers between devices, moved(): return lax.ppermute(value, axis, pairs)  20.1 us
    ppermute x8, starting transfers between devices, moved(): return lax.ppermute(value, axis, pairs)  9.21 us
    ppermute x3, waiting for transfers between devices, per_device(): lax.ppermute(plane, axis, [(d, (d + shift * near) % size) for d in range(...  8.25 us
    pallas_call x1, Pallas kernels, shrink(): pl.pallas_call(functools.partial(shrink_kernel, columns, len(pieces), ran...  5.33 us
    ppermute x3, starting transfers between devices, per_device(): lax.ppermute(plane, axis, [(d, (d + shift * near) % size) for d in range(...  4.64 us
    ppermute x3, waiting for transfers between devices, per_device(): lax.ppermute(shrunk, axis, [(d, d ^ flip) for d in range(size)])  4.3 us
    pallas_call x1, Pallas kernels, split_columns(): pl.pallas_call(split_kernel, grid=(parts // group,), in_specs=[pl.BlockSp...  3.79 us
  transfers between devices with their start and end apart: 24, of which 15 were waited for; matrix products, arithmetic and copies ran while one was open for 1% of the time, Pallas kernels for 32%

profile of v6, /device:TPU:0, one launch (start us, length us, event | category | flops | bytes accessed | tf_op | source)
XLA Modules:
  0.0 93.0 jit_solution(15572589222958801366)
XLA Ops:
  0.0 3.0 %collective-permute-start = (bf16[16,8192]{1,0:T(8,128)(2,1)}, bf16[16,8192]{1,0:T(8,128)(2,1)S(1)}, u32[]{:S(2)}, u32[]{:S(2)}) collective-permute-start(bf16[16,8192]{1,0:T(8,128)(2,1)} %refs_0_.3), channel_id=1, source_target_pairs={{0,4},{1,5},{4,8},{5,9},{8,12},{9,13},{12,14},{13,15},{14,10},{15,... | collective-permute-start | bytes 786440 | tf_op jit(solution)/shard_map/ppermute | solution.py:30
  3.0 6.5 %collective-permute-done.refs_1_ = bf16[16,8192]{1,0:T(8,128)(2,1)S(1)} collective-permute-done((bf16[16,8192]{1,0:T(8,128)(2,1)}, bf16[16,8192]{1,0:T(8,128)(2,1)S(1)}, u32[]{:S(2)}, u32[]{:S(2)}) %collective-permute-start) | collective-permute-done | bytes 262176 | tf_op jit(solution)/shard_map/ppermute | solution.py:30
  9.5 1.5 %collective-permute-done.1.refs_2_ = bf16[16,8192]{1,0:T(8,128)(2,1)S(1)} collective-permute-done((bf16[16,8192]{1,0:T(8,128)(2,1)}, bf16[16,8192]{1,0:T(8,128)(2,1)S(1)}, u32[]{:S(2)}, u32[]{:S(2)}) %collective-permute-start.1) | collective-permute-done | bytes 262176 | tf_op jit(solution)/shard_map/ppermute | solution.py:30
  11.0 1.6 %collective-permute-start.2 = (bf16[16,8192]{1,0:T(8,128)(2,1)S(1)}, bf16[16,8192]{1,0:T(8,128)(2,1)S(1)}, u32[]{:S(2)}, u32[]{:S(2)}) collective-permute-start(bf16[16,8192]{1,0:T(8,128)(2,1)S(1)} %collective-permute-done.refs_1_), channel_id=1, source_target_pairs={{0,4},{1,5},{4,8},{5,9},{8,12},{9,13},{12,14},{13,15},{14,10},{15,... | collective-permute-start | bytes 786440 | tf_op jit(solution)/shard_map/ppermute | solution.py:30
  12.6 0.4 collective-permute-start.3
  13.0 3.8 %split_columns.1 = bf16[16,64,1024]{2,1,0:T(8,128)(2,1)} custom-call(bf16[64,16384]{1,0:T(8,128)(2,1)} %bitcast.8), custom_call_target="tpu_custom_call" | custom-call | tf_op jit(solution)/shard_map/split_columns/pallas_call | solution.py:82
  16.8 1.0 %collective-permute-done.2.refs_3_ = bf16[16,8192]{1,0:T(8,128)(2,1)S(1)} collective-permute-done((bf16[16,8192]{1,0:T(8,128)(2,1)S(1)}, bf16[16,8192]{1,0:T(8,128)(2,1)S(1)}, u32[]{:S(2)}, u32[]{:S(2)}) %collective-permute-start.2) | collective-permute-done | bytes 262176 | tf_op jit(solution)/shard_map/ppermute | solution.py:30
  17.9 1.3 %collective-permute-done.3.refs_4_ = bf16[16,8192]{1,0:T(8,128)(2,1)S(1)} collective-permute-done((bf16[16,8192]{1,0:T(8,128)(2,1)S(1)}, bf16[16,8192]{1,0:T(8,128)(2,1)S(1)}, u32[]{:S(2)}, u32[]{:S(2)}) %collective-permute-start.3) | collective-permute-done | bytes 262176 | tf_op jit(solution)/shard_map/ppermute | solution.py:30
  19.2 1.6 %collective-permute-start.4 = (bf16[16,8192]{1,0:T(8,128)(2,1)S(1)}, bf16[16,8192]{1,0:T(8,128)(2,1)S(1)}, u32[]{:S(2)}, u32[]{:S(2)}) collective-permute-start(bf16[16,8192]{1,0:T(8,128)(2,1)S(1)} %collective-permute-done.2.refs_3_), channel_id=1, source_target_pairs={{0,4},{1,5},{4,8},{5,9},{8,12},{9,13},{12,14},{13,15},{14,10},{15,... | collective-permute-start | bytes 786440 | tf_op jit(solution)/shard_map/ppermute | solution.py:30
  20.7 0.4 collective-permute-start.5
  21.2 5.3 %collective-permute-done.4.refs_5_ = bf16[16,8192]{1,0:T(8,128)(2,1)S(1)} collective-permute-done((bf16[16,8192]{1,0:T(8,128)(2,1)S(1)}, bf16[16,8192]{1,0:T(8,128)(2,1)S(1)}, u32[]{:S(2)}, u32[]{:S(2)}) %collective-permute-start.4) | collective-permute-done | bytes 262176 | tf_op jit(solution)/shard_map/ppermute | solution.py:30
  26.5 1.6 %collective-permute-start.6 = (bf16[16,4096]{1,0:T(8,128)(2,1)S(1)}, bf16[16,4096]{1,0:T(8,128)(2,1)S(1)}, u32[]{:S(2)}, u32[]{:S(2)}) collective-permute-start(bf16[16,4096]{1,0:T(8,128)(2,1)S(1)} %slice.8), channel_id=1, source_target_pairs={{0,4},{1,5},{4,8},{5,9},{8,12},{9,13},{12,14},{13,15},{14,10},{15,... | collective-permute-start | bytes 393224 | tf_op jit(solution)/shard_map/ppermute | solution.py:30
  28.2 0.5 collective-permute-start.7
  28.7 2.8 %collective-permute-done.6.refs_7_ = bf16[16,4096]{1,0:T(8,128)(2,1)S(1)} collective-permute-done((bf16[16,4096]{1,0:T(8,128)(2,1)S(1)}, bf16[16,4096]{1,0:T(8,128)(2,1)S(1)}, u32[]{:S(2)}, u32[]{:S(2)}) %collective-permute-start.6) | collective-permute-done | bytes 131104 | tf_op jit(solution)/shard_map/ppermute | solution.py:30
  31.5 1.7 %collective-permute-done.7.refs_8_ = bf16[16,4096]{1,0:T(8,128)(2,1)S(1)} collective-permute-done((bf16[16,4096]{1,0:T(8,128)(2,1)S(1)}, bf16[16,4096]{1,0:T(8,128)(2,1)S(1)}, u32[]{:S(2)}, u32[]{:S(2)}) %collective-permute-start.7) | collective-permute-done | bytes 131104 | tf_op jit(solution)/shard_map/ppermute | solution.py:30
  33.2 0.7 copy-done.15
  33.9 3.7 %all-to-all-start = ((bf16[16,64,1024]{2,1,0:T(8,128)(2,1)}), bf16[16,64,1024]{2,1,0:T(8,128)(2,1)S(1)}, u32[]{:S(2)}, u32[]{:S(2)}) async-start(bf16[16,64,1024]{2,1,0:T(8,128)(2,1)} %split_columns.1), calls=%async_computation | async-start | bytes 4194304 | tf_op jit(solution)/shard_map/all_to_all | solution.py:274
  40.3 0.4 collective-permute-start.15
  41.0 0.4 collective-permute-start.16
  41.7 0.7 dynamic-slice_bitcast_fusion.place
  42.7 0.4 copy-done.16
  43.5 5.3 %shrink.1 = bf16[64,256]{1,0:T(8,128)(2,1)S(1)} custom-call(s32[19]{0:T(128)S(1)} %dynamic-slice_bitcast_fusion.place, s32[1,256]{1,0:T(1,128)S(1)} %bitcast.7, bf16[64,8192]{1,0:T(8,128)(2,1)} %bitcast.9, bf16[16,8192]{1,0:T(8,128)(2,1)} %refs_0_.3, bf16[16,8192]{1,0:T(8,128)(2,1)} %copy-done.4, bf16[16,8192]{1,0:T(8,128)(2,1)} %copy-done.5, ...), custom_call_target="tpu_custom_call" | custom-call | flops 268435456 | bytes 5242880 | tf_op jit(solution)/shard_map/shrink/pallas_call | solution.py:119
  48.8 0.4 collective-permute-start.17
  49.2 1.7 %collective-permute-start.18 = (bf16[64,256]{1,0:T(8,128)(2,1)S(1)}, bf16[64,256]{1,0:T(8,128)(2,1)S(1)}, u32[]{:S(2)}, u32[]{:S(2)}) collective-permute-start(bf16[64,256]{1,0:T(8,128)(2,1)S(1)} %shrink.1), channel_id=1, source_target_pairs={{0,2},{1,3},{2,0},{3,1},{4,6},{5,7},{6,4},{7,5},{8,10},{9,11},{10,... | collective-permute-start | bytes 98312 | tf_op jit(solution)/shard_map/ppermute | solution.py:287
  50.9 3.7 %collective-permute-done.18 = bf16[64,256]{1,0:T(8,128)(2,1)S(1)} collective-permute-done((bf16[64,256]{1,0:T(8,128)(2,1)S(1)}, bf16[64,256]{1,0:T(8,128)(2,1)S(1)}, u32[]{:S(2)}, u32[]{:S(2)}) %collective-permute-start.18) | collective-permute-done | bytes 32800 | tf_op jit(solution)/shard_map/ppermute | solution.py:287
  54.7 0.6 collective-permute-done.19
  55.3 0.8 collective-permute-start.20
  56.0 3.9 %collective-permute-start.21 = (bf16[64,256]{1,0:T(8,128)(2,1)S(1)}, bf16[64,256]{1,0:T(8,128)(2,1)S(1)}, u32[]{:S(2)}, u32[]{:S(2)}) collective-permute-start(bf16[64,256]{1,0:T(8,128)(2,1)S(1)} %add_add_fusion.refs_0_), channel_id=1, source_target_pairs={{0,8},{1,9},{2,10},{3,11},{4,12},{5,13},{6,14},{7,15},{8,0},{9,1},... | collective-permute-start | bytes 98312 | tf_op jit(solution)/shard_map/ppermute | solution.py:291
  59.9 20.9 %project.1 = (f32[256,1024]{1,0:T(8,128)}, f32[256,1024]{1,0:T(8,128)}) custom-call(s32[19]{0:T(128)S(1)} %dynamic-slice_bitcast_fusion.place, bf16[8192,1024]{1,0:T(8,128)(2,1)} %gate_weight_ref.1, bf16[8192,1024]{1,0:T(8,128)(2,1)} %up_weight_ref.1, bf16[16,8192]{1,0:T(8,128)(2,1)} %refs_0_.3, bf16[16,8192]{1,0:T(8,128)(2,1)} %copy-done.4, ...), custom_call_target="tpu_custom_call" | custom-call | flops 8589934592 | bytes 37748736 | tf_op jit(solution)/shard_map/project/pallas_call | solution.py:172
  80.8 8.2 %collective-permute-done.21.refs_2_ = bf16[64,256]{1,0:T(8,128)(2,1)S(1)} collective-permute-done((bf16[64,256]{1,0:T(8,128)(2,1)S(1)}, bf16[64,256]{1,0:T(8,128)(2,1)S(1)}, u32[]{:S(2)}, u32[]{:S(2)}) %collective-permute-start.21) | collective-permute-done | bytes 32800 | tf_op jit(solution)/shard_map/ppermute | solution.py:291
  89.1 0.8 broadcast_in_dim.2.users_ref
  89.8 3.1 %combine.1 = bf16[256,1024]{1,0:T(8,128)(2,1)} custom-call(s32[256,128]{1,0:T(8,128)} %broadcast_in_dim.2.users_ref, f32[256,1024]{1,0:T(8,128)} %get-tuple-element.24.gate_ref, f32[256,1024]{1,0:T(8,128)} %get-tuple-element.25.up_ref, bf16[1024,1024]{1,0:T(8,128)(2,1)S(1)} %bitcast.6, bf16[64,256]{1,0:T(8,128)(2,1)} %copy-done.17, ...), custom_call_target="tpu_custom_call" | custom-call | flops 536870912 | bytes 2621440 | tf_op jit(solution)/shard_map/combine/pallas_call | solution.py:224
  (67 shorter events, 4.0 us)
Async XLA Ops:
  0.0 9.5 %collective-permute-start = (bf16[16,8192]{1,0:T(8,128)(2,1)}, bf16[16,8192]{1,0:T(8,128)(2,1)S(1)}, u32[]{:S(2)}, u32[]{:S(2)}) collective-permute-start(bf16[16,8192]{1,0:T(8,128)(2,1)} %refs_0_.3), channel_id=1, source_target_pairs={{0,4},{1,5},{4,8},{5,9},{8,12},{9,13},{12,14},{13,15},{14,10},{15,... | collective-permute-start | bytes 786440 | tf_op jit(solution)/shard_map/ppermute | solution.py:30
  3.0 8.0 %collective-permute-start.1 = (bf16[16,8192]{1,0:T(8,128)(2,1)}, bf16[16,8192]{1,0:T(8,128)(2,1)S(1)}, u32[]{:S(2)}, u32[]{:S(2)}) collective-permute-start(bf16[16,8192]{1,0:T(8,128)(2,1)} %refs_0_.3), channel_id=1, source_target_pairs={{0,2},{1,3},{4,0},{5,1},{8,4},{9,5},{12,8},{13,9},{14,12},{15,13},... | collective-permute-start | bytes 786440 | tf_op jit(solution)/shard_map/ppermute | solution.py:30
  9.5 28.7 %copy-start.4 = (bf16[16,8192]{1,0:T(8,128)(2,1)}, bf16[16,8192]{1,0:T(8,128)(2,1)S(1)}, u32[]{:S(2)}) copy-start(bf16[16,8192]{1,0:T(8,128)(2,1)S(1)} %collective-permute-done.refs_1_) | copy-start | bytes 786436
  11.0 27.0 %copy-start.5 = (bf16[16,8192]{1,0:T(8,128)(2,1)}, bf16[16,8192]{1,0:T(8,128)(2,1)S(1)}, u32[]{:S(2)}) copy-start(bf16[16,8192]{1,0:T(8,128)(2,1)S(1)} %collective-permute-done.1.refs_2_) | copy-start | bytes 786436
  11.0 6.9 %collective-permute-start.2 = (bf16[16,8192]{1,0:T(8,128)(2,1)S(1)}, bf16[16,8192]{1,0:T(8,128)(2,1)S(1)}, u32[]{:S(2)}, u32[]{:S(2)}) collective-permute-start(bf16[16,8192]{1,0:T(8,128)(2,1)S(1)} %collective-permute-done.refs_1_), channel_id=1, source_target_pairs={{0,4},{1,5},{4,8},{5,9},{8,12},{9,13},{12,14},{13,15},{14,10},{15,... | collective-permute-start | bytes 786440 | tf_op jit(solution)/shard_map/ppermute | solution.py:30
  12.6 6.6 %collective-permute-start.3 = (bf16[16,8192]{1,0:T(8,128)(2,1)S(1)}, bf16[16,8192]{1,0:T(8,128)(2,1)S(1)}, u32[]{:S(2)}, u32[]{:S(2)}) collective-permute-start(bf16[16,8192]{1,0:T(8,128)(2,1)S(1)} %collective-permute-done.1.refs_2_), channel_id=1, source_target_pairs={{0,2},{1,3},{4,0},{5,1},{8,4},{9,5},{12,8},{13,9},{14,12},{15,13},... | collective-permute-start | bytes 786440 | tf_op jit(solution)/shard_map/ppermute | solution.py:30
  17.9 10.3 %copy-start.6 = (bf16[16,8192]{1,0:T(8,128)(2,1)}, bf16[16,8192]{1,0:T(8,128)(2,1)S(1)}, u32[]{:S(2)}) copy-start(bf16[16,8192]{1,0:T(8,128)(2,1)S(1)} %collective-permute-done.2.refs_3_) | copy-start | bytes 786436
  19.2 14.1 %copy-start.7 = (bf16[16,8192]{1,0:T(8,128)(2,1)}, bf16[16,8192]{1,0:T(8,128)(2,1)S(1)}, u32[]{:S(2)}) copy-start(bf16[16,8192]{1,0:T(8,128)(2,1)S(1)} %collective-permute-done.3.refs_4_) | copy-start | bytes 786436
  19.2 7.3 %collective-permute-start.4 = (bf16[16,8192]{1,0:T(8,128)(2,1)S(1)}, bf16[16,8192]{1,0:T(8,128)(2,1)S(1)}, u32[]{:S(2)}, u32[]{:S(2)}) collective-permute-start(bf16[16,8192]{1,0:T(8,128)(2,1)S(1)} %collective-permute-done.2.refs_3_), channel_id=1, source_target_pairs={{0,4},{1,5},{4,8},{5,9},{8,12},{9,13},{12,14},{13,15},{14,10},{15,... | collective-permute-start | bytes 786440 | tf_op jit(solution)/shard_map/ppermute | solution.py:30
  20.7 7.4 %collective-permute-start.5 = (bf16[16,8192]{1,0:T(8,128)(2,1)S(1)}, bf16[16,8192]{1,0:T(8,128)(2,1)S(1)}, u32[]{:S(2)}, u32[]{:S(2)}) collective-permute-start(bf16[16,8192]{1,0:T(8,128)(2,1)S(1)} %collective-permute-done.3.refs_4_), channel_id=1, source_target_pairs={{0,2},{1,3},{4,0},{5,1},{8,4},{9,5},{12,8},{13,9},{14,12},{15,13},... | collective-permute-start | bytes 786440 | tf_op jit(solution)/shard_map/ppermute | solution.py:30
  26.5 12.7 %copy-start.1 = (bf16[16,8192]{1,0:T(8,128)(2,1)}, bf16[16,8192]{1,0:T(8,128)(2,1)S(1)}, u32[]{:S(2)}) copy-start(bf16[16,8192]{1,0:T(8,128)(2,1)S(1)} %collective-permute-done.4.refs_5_) | copy-start | bytes 786436
  26.5 5.0 %collective-permute-start.6 = (bf16[16,4096]{1,0:T(8,128)(2,1)S(1)}, bf16[16,4096]{1,0:T(8,128)(2,1)S(1)}, u32[]{:S(2)}, u32[]{:S(2)}) collective-permute-start(bf16[16,4096]{1,0:T(8,128)(2,1)S(1)} %slice.8), channel_id=1, source_target_pairs={{0,4},{1,5},{4,8},{5,9},{8,12},{9,13},{12,14},{13,15},{14,10},{15,... | collective-permute-start | bytes 393224 | tf_op jit(solution)/shard_map/ppermute | solution.py:30
  28.2 11.4 %copy-start.2 = (bf16[16,8192]{1,0:T(8,128)(2,1)}, bf16[16,8192]{1,0:T(8,128)(2,1)S(1)}, u32[]{:S(2)}) copy-start(bf16[16,8192]{1,0:T(8,128)(2,1)S(1)} %collective-permute-done.5.refs_6_) | copy-start | bytes 786436
  28.2 15.3 %copy-start = (s32[256]{0:T(256)S(1)}, s32[256]{0:T(256)}, u32[]{:S(2)}) copy-start(s32[256]{0:T(256)} %param.14) | copy-start | bytes 3076
  28.2 5.0 %collective-permute-start.7 = (bf16[16,4096]{1,0:T(8,128)(2,1)S(1)}, bf16[16,4096]{1,0:T(8,128)(2,1)S(1)}, u32[]{:S(2)}, u32[]{:S(2)}) collective-permute-start(bf16[16,4096]{1,0:T(8,128)(2,1)S(1)} %slice.9), channel_id=1, source_target_pairs={{0,2},{1,3},{4,0},{5,1},{8,4},{9,5},{12,8},{13,9},{14,12},{15,13},... | collective-permute-start | bytes 393224 | tf_op jit(solution)/shard_map/ppermute | solution.py:30
  33.9 55.2 %all-to-all-start = ((bf16[16,64,1024]{2,1,0:T(8,128)(2,1)}), bf16[16,64,1024]{2,1,0:T(8,128)(2,1)S(1)}, u32[]{:S(2)}, u32[]{:S(2)}) async-start(bf16[16,64,1024]{2,1,0:T(8,128)(2,1)} %split_columns.1), calls=%async_computation | async-start | bytes 4194304 | tf_op jit(solution)/shard_map/all_to_all | solution.py:274
  37.6 1.6 %collective-permute-start.8 = (bf16[16,8192]{1,0:T(8,128)(2,1)S(1)}, bf16[16,8192]{1,0:T(8,128)(2,1)S(1)}, u32[]{:S(2)}, u32[]{:S(2)}) collective-permute-start(bf16[16,8192]{1,0:T(8,128)(2,1)S(1)} %copy-done.3), channel_id=1, source_target_pairs={{0,1},{1,0},{2,3},{3,2},{4,5},{5,4},{6,7},{7,6},{8,9},{9,8},{10,11... | collective-permute-start | bytes 786440 | tf_op jit(solution)/shard_map/ppermute | solution.py:44
  38.0 1.6 %collective-permute-start.10 = (bf16[16,8192]{1,0:T(8,128)(2,1)S(1)}, bf16[16,8192]{1,0:T(8,128)(2,1)S(1)}, u32[]{:S(2)}, u32[]{:S(2)}) collective-permute-start(bf16[16,8192]{1,0:T(8,128)(2,1)S(1)} %collective-permute-done.1.refs_2_), channel_id=1, source_target_pairs={{0,1},{1,0},{2,3},{3,2},{4,5},{5,4},{6,7},{7,6},{8,9},{9,8},{10,11... | collective-permute-start | bytes 786440 | tf_op jit(solution)/shard_map/ppermute | solution.py:44
  38.2 2.1 %collective-permute-start.9 = (bf16[16,8192]{1,0:T(8,128)(2,1)S(1)}, bf16[16,8192]{1,0:T(8,128)(2,1)S(1)}, u32[]{:S(2)}, u32[]{:S(2)}) collective-permute-start(bf16[16,8192]{1,0:T(8,128)(2,1)S(1)} %collective-permute-done.refs_1_), channel_id=1, source_target_pairs={{0,1},{1,0},{2,3},{3,2},{4,5},{5,4},{6,7},{7,6},{8,9},{9,8},{10,11... | collective-permute-start | bytes 786440 | tf_op jit(solution)/shard_map/ppermute | solution.py:44
  38.5 2.4 %collective-permute-start.11 = (bf16[16,8192]{1,0:T(8,128)(2,1)}, bf16[16,8192]{1,0:T(8,128)(2,1)S(1)}, u32[]{:S(2)}, u32[]{:S(2)}) collective-permute-start(bf16[16,8192]{1,0:T(8,128)(2,1)} %copy-done.6), channel_id=1, source_target_pairs={{0,1},{1,0},{2,3},{3,2},{4,5},{5,4},{6,7},{7,6},{8,9},{9,8},{10,11... | collective-permute-start | bytes 786440 | tf_op jit(solution)/shard_map/ppermute | solution.py:44
  38.7 3.7 %collective-permute-start.12 = (bf16[16,8192]{1,0:T(8,128)(2,1)}, bf16[16,8192]{1,0:T(8,128)(2,1)}, u32[]{:S(2)}, u32[]{:S(2)}) collective-permute-start(bf16[16,8192]{1,0:T(8,128)(2,1)} %copy-done.7), channel_id=1, source_target_pairs={{0,1},{1,0},{2,3},{3,2},{4,5},{5,4},{6,7},{7,6},{8,9},{9,8},{10,11... | collective-permute-start | bytes 786440 | tf_op jit(solution)/shard_map/ppermute | solution.py:44
  39.2 3.4 %collective-permute-start.13 = (bf16[16,8192]{1,0:T(8,128)(2,1)S(1)}, bf16[16,8192]{1,0:T(8,128)(2,1)S(1)}, u32[]{:S(2)}, u32[]{:S(2)}) collective-permute-start(bf16[16,8192]{1,0:T(8,128)(2,1)S(1)} %collective-permute-done.4.refs_5_), channel_id=1, source_target_pairs={{0,1},{1,0},{2,3},{3,2},{4,5},{5,4},{6,7},{7,6},{8,9},{9,8},{10,11... | collective-permute-start | bytes 786440 | tf_op jit(solution)/shard_map/ppermute | solution.py:44
  39.6 3.1 %collective-permute-start.14 = (bf16[16,8192]{1,0:T(8,128)(2,1)S(1)}, bf16[16,8192]{1,0:T(8,128)(2,1)S(1)}, u32[]{:S(2)}, u32[]{:S(2)}) collective-permute-start(bf16[16,8192]{1,0:T(8,128)(2,1)S(1)} %collective-permute-done.5.refs_6_), channel_id=1, source_target_pairs={{0,1},{1,0},{2,3},{3,2},{4,5},{5,4},{6,7},{7,6},{8,9},{9,8},{10,11... | collective-permute-start | bytes 786440 | tf_op jit(solution)/shard_map/ppermute | solution.py:44
  40.3 2.1 %collective-permute-start.15 = (bf16[16,4096]{1,0:T(8,128)(2,1)S(1)}, bf16[16,4096]{1,0:T(8,128)(2,1)S(1)}, u32[]{:S(2)}, u32[]{:S(2)}) collective-permute-start(bf16[16,4096]{1,0:T(8,128)(2,1)S(1)} %collective-permute-done.6.refs_7_), channel_id=1, source_target_pairs={{0,1},{1,0},{2,3},{3,2},{4,5},{5,4},{6,7},{7,6},{8,9},{9,8},{10,11... | collective-permute-start | bytes 393224 | tf_op jit(solution)/shard_map/ppermute | solution.py:44
  41.0 1.7 %collective-permute-start.16 = (bf16[16,4096]{1,0:T(8,128)(2,1)}, bf16[16,4096]{1,0:T(8,128)(2,1)}, u32[]{:S(2)}, u32[]{:S(2)}) collective-permute-start(bf16[16,4096]{1,0:T(8,128)(2,1)} %copy-done.15), channel_id=1, source_target_pairs={{0,1},{1,0},{2,3},{3,2},{4,5},{5,4},{6,7},{7,6},{8,9},{9,8},{10,11... | collective-permute-start | bytes 393224 | tf_op jit(solution)/shard_map/ppermute | solution.py:44
  48.8 2.1 %collective-permute-start.17 = (bf16[64,256]{1,0:T(8,128)(2,1)S(1)}, bf16[64,256]{1,0:T(8,128)(2,1)S(1)}, u32[]{:S(2)}, u32[]{:S(2)}) collective-permute-start(bf16[64,256]{1,0:T(8,128)(2,1)S(1)} %shrink.1), channel_id=1, source_target_pairs={{0,1},{1,0},{2,3},{3,2},{4,5},{5,4},{6,7},{7,6},{8,9},{9,8},{10,11... | collective-permute-start | bytes 98312 | tf_op jit(solution)/shard_map/ppermute | solution.py:287
  49.2 5.4 %collective-permute-start.18 = (bf16[64,256]{1,0:T(8,128)(2,1)S(1)}, bf16[64,256]{1,0:T(8,128)(2,1)S(1)}, u32[]{:S(2)}, u32[]{:S(2)}) collective-permute-start(bf16[64,256]{1,0:T(8,128)(2,1)S(1)} %shrink.1), channel_id=1, source_target_pairs={{0,2},{1,3},{2,0},{3,1},{4,6},{5,7},{6,4},{7,5},{8,10},{9,11},{10,... | collective-permute-start | bytes 98312 | tf_op jit(solution)/shard_map/ppermute | solution.py:287
  50.9 4.3 %collective-permute-start.19 = (bf16[64,256]{1,0:T(8,128)(2,1)S(1)}, bf16[64,256]{1,0:T(8,128)(2,1)S(1)}, u32[]{:S(2)}, u32[]{:S(2)}) collective-permute-start(bf16[64,256]{1,0:T(8,128)(2,1)S(1)} %shrink.1), channel_id=1, source_target_pairs={{0,3},{1,2},{2,1},{3,0},{4,7},{5,6},{6,5},{7,4},{8,11},{9,10},{10,... | collective-permute-start | bytes 98312 | tf_op jit(solution)/shard_map/ppermute | solution.py:287
  55.3 25.5 %copy-start.17 = (bf16[64,256]{1,0:T(8,128)(2,1)}, bf16[64,256]{1,0:T(8,128)(2,1)S(1)}, u32[]{:S(2)}) copy-start(bf16[64,256]{1,0:T(8,128)(2,1)S(1)} %add_add_fusion.refs_0_) | copy-start | bytes 98308
  55.3 25.5 %collective-permute-start.20 = (bf16[64,256]{1,0:T(8,128)(2,1)S(1)}, bf16[64,256]{1,0:T(8,128)(2,1)S(1)}, u32[]{:S(2)}, u32[]{:S(2)}) collective-permute-start(bf16[64,256]{1,0:T(8,128)(2,1)S(1)} %add_add_fusion.refs_0_), channel_id=1, source_target_pairs={{0,4},{1,5},{2,6},{3,7},{4,8},{5,9},{6,10},{7,11},{8,12},{9,13},{1... | collective-permute-start | bytes 98312 | tf_op jit(solution)/shard_map/ppermute | solution.py:291
  56.0 33.0 %collective-permute-start.21 = (bf16[64,256]{1,0:T(8,128)(2,1)S(1)}, bf16[64,256]{1,0:T(8,128)(2,1)S(1)}, u32[]{:S(2)}, u32[]{:S(2)}) collective-permute-start(bf16[64,256]{1,0:T(8,128)(2,1)S(1)} %add_add_fusion.refs_0_), channel_id=1, source_target_pairs={{0,8},{1,9},{2,10},{3,11},{4,12},{5,13},{6,14},{7,15},{8,0},{9,1},... | collective-permute-start | bytes 98312 | tf_op jit(solution)/shard_map/ppermute | solution.py:291
  59.9 29.2 %collective-permute-start.22 = (bf16[64,256]{1,0:T(8,128)(2,1)S(1)}, bf16[64,256]{1,0:T(8,128)(2,1)S(1)}, u32[]{:S(2)}, u32[]{:S(2)}) collective-permute-start(bf16[64,256]{1,0:T(8,128)(2,1)S(1)} %add_add_fusion.refs_0_), channel_id=1, source_target_pairs={{0,12},{1,13},{2,14},{3,15},{4,0},{5,1},{6,2},{7,3},{8,4},{9,5},{1... | collective-permute-start | bytes 98312 | tf_op jit(solution)/shard_map/ppermute | solution.py:291
  (13 other events, 35.1 us)

commit v7 on v6

--- a/solution.py
+++ b/solution.py
@@ -29,15 +29,18 @@
         ]
         return lax.ppermute(value, axis, pairs)
 
-    pieces = [(block, 0, 0)]
-    right = left = block
-    for step in range(1, chips // 2):
-        right, left = beside(step, (moved(right, 1), moved(left, -1)))
-        pieces += [(right, 0, -step), (left, 0, step)]
     half = block.shape[1] // 2
     far = chips // 2
-    right, left = beside(far, (moved(right[:, :half], 1), moved(left[:, half:], -1)))
-    pieces += [(right, 0, far), (left, half, far)]
+    halves = block[:, :half], block[:, half:]
+    columns = (0, half), (half, 0)
+    held = [halves, halves[::-1]]
+    pieces = [(block, 0, 0)]
+    for step in range(1, far + 1):
+        for chain in range(1 if step == far else 2):
+            right, left = held[chain]
+            held[chain] = beside(chain, step, (moved(right, 1), moved(left, -1)))
+            for value, column, distance in zip(held[chain], columns[chain], (-step, step)):
+                pieces.append((value, column, distance))
 
     flips = [(d, d ^ 1) for d in range(size)]
     found = [(value, column) for value, column, _ in pieces]
@@ -263,14 +266,14 @@
     steps = size // CORES // 2
     maps = None
 
-    def beside(step, values):
+    def beside(chain, step, values):
         nonlocal own_maps, maps
-        if step not in (1, 2, steps):
+        if (chain, step) not in ((0, 1), (0, 2), (1, steps - 1)):
             return values
         own_maps, *values = lax.optimization_barrier((own_maps, *values))
-        if step == 1:
+        if (chain, step) == (0, 1):
             own_maps = split_columns(own_maps, size)
-        if step == steps:
+        if chain == 1:
             maps = lax.all_to_all(own_maps, axis, split_axis=0, concat_axis=0, tiled=True)
         return values
 

time: 93.3 us -> 128 us (1.37)
  starting transfers between devices: 22.4 us -> 44.4 us
  waiting for transfers between devices: 33.9 us -> 46.7 us
    ppermute x8 -> x14, waiting for transfers between devices: 20.1 us -> 43.3 us  [moved(): return lax.ppermute(value, axis, pairs)]
    ppermute x8 -> x14, starting transfers between devices: 9.21 us -> 28 us  [moved(): return lax.ppermute(value, axis, pairs)]
    ppermute x3, waiting for transfers between devices: 8.25 us -> 0.01 us  [per_device(): lax.ppermute(plane, axis, [(d, (d + shift * near) % size) for d in range(...]
    ppermute x3, waiting for transfers between devices: 4.3 us -> 2.43 us  [per_device(): lax.ppermute(shrunk, axis, [(d, d ^ flip) for d in range(size)])]
    all_to_all x1, starting transfers between devices: 3.72 us -> 5.52 us  [beside(): lax.all_to_all(own_maps, axis, split_axis=0, concat_axis=0, tiled=True)]
    ppermute x9 -> x15, starting transfers between devices: 2.75 us -> 3.59 us  [ring_gather(): lax.ppermute(value, axis, flips)]
  transfers between devices with their start and end apart: 24 -> 36, of which waited for: 15 -> 9; matrix products, arithmetic and copies ran while one was open for 1% -> 1% of each run, Pallas kernels for 32% -> 24%
where the time goes in v7:
time: 128 us
  waiting for transfers between devices  46.7 us (36%)
  starting transfers between devices  44.4 us (35%)
  Pallas kernels  33.5 us (26%)
  local copies, waits for them, and re-layouts  3.19 us (2%)
    ppermute x14, waiting for transfers between devices, moved(): return lax.ppermute(value, axis, pairs)  43.3 us
    ppermute x14, starting transfers between devices, moved(): return lax.ppermute(value, axis, pairs)  28 us
    pallas_call x1, Pallas kernels, project(): pl.pallas_call(functools.partial(project_kernel, columns, len(pieces)), g...  21 us
    pallas_call x1, Pallas kernels, shrink(): pl.pallas_call(functools.partial(shrink_kernel, columns, len(pieces), ran...  5.53 us
    all_to_all x1, starting transfers between devices, beside(): lax.all_to_all(own_maps, axis, split_axis=0, concat_axis=0, tiled=True)  5.52 us
    ppermute x3, starting transfers between devices, per_device(): lax.ppermute(plane, axis, [(d, (d + shift * near) % size) for d in range(...  5.41 us
    pallas_call x1, Pallas kernels, split_columns(): pl.pallas_call(split_kernel, grid=(parts // group,), in_specs=[pl.BlockSp...  3.79 us
    ppermute x15, starting transfers between devices, ring_gather(): lax.ppermute(value, axis, flips)  3.59 us
  transfers between devices with their start and end apart: 36, of which 9 were waited for; matrix products, arithmetic and copies ran while one was open for 1% of the time, Pallas kernels for 24%

profile of v7, /device:TPU:0, one launch (start us, length us, event | category | flops | bytes accessed | tf_op | source)
XLA Modules:
  0.0 128.1 jit_solution(4515178815013256745)
XLA Ops:
  0.0 1.0 fusion
  1.0 3.1 %collective-permute-start.2 = (bf16[16,4096]{1,0:T(8,128)(2,1)S(1)}, bf16[16,4096]{1,0:T(8,128)(2,1)S(1)}, u32[]{:S(2)}, u32[]{:S(2)}) collective-permute-start(bf16[16,4096]{1,0:T(8,128)(2,1)S(1)} %get-tuple-element.27), channel_id=1, source_target_pairs={{0,4},{1,5},{4,8},{5,9},{8,12},{9,13},{12,14},{13,15},{14,10},{15,... | collective-permute-start | bytes 393224 | tf_op jit(solution)/shard_map/ppermute | solution.py:30
  4.1 2.0 %collective-permute-start = (bf16[16,4096]{1,0:T(8,128)(2,1)S(1)}, bf16[16,4096]{1,0:T(8,128)(2,1)S(1)}, u32[]{:S(2)}, u32[]{:S(2)}) collective-permute-start(bf16[16,4096]{1,0:T(8,128)(2,1)S(1)} %get-tuple-element.28), channel_id=1, source_target_pairs={{0,4},{1,5},{4,8},{5,9},{8,12},{9,13},{12,14},{13,15},{14,10},{15,... | collective-permute-start | bytes 393224 | tf_op jit(solution)/shard_map/ppermute | solution.py:30
  6.1 2.2 %collective-permute-done.2.refs_3_ = bf16[16,4096]{1,0:T(8,128)(2,1)S(1)} collective-permute-done((bf16[16,4096]{1,0:T(8,128)(2,1)S(1)}, bf16[16,4096]{1,0:T(8,128)(2,1)S(1)}, u32[]{:S(2)}, u32[]{:S(2)}) %collective-permute-start.2) | collective-permute-done | bytes 131104 | tf_op jit(solution)/shard_map/ppermute | solution.py:30
  8.3 2.1 %collective-permute-start.6 = (bf16[16,4096]{1,0:T(8,128)(2,1)S(1)}, bf16[16,4096]{1,0:T(8,128)(2,1)S(1)}, u32[]{:S(2)}, u32[]{:S(2)}) collective-permute-start(bf16[16,4096]{1,0:T(8,128)(2,1)S(1)} %collective-permute-done.2.refs_3_), channel_id=1, source_target_pairs={{0,4},{1,5},{4,8},{5,9},{8,12},{9,13},{12,14},{13,15},{14,10},{15,... | collective-permute-start | bytes 393224 | tf_op jit(solution)/shard_map/ppermute | solution.py:30
  10.5 0.7 collective-permute-done.refs_1_
  11.1 1.9 %collective-permute-done.1.refs_2_ = bf16[16,4096]{1,0:T(8,128)(2,1)S(1)} collective-permute-done((bf16[16,4096]{1,0:T(8,128)(2,1)S(1)}, bf16[16,4096]{1,0:T(8,128)(2,1)S(1)}, u32[]{:S(2)}, u32[]{:S(2)}) %collective-permute-start.1) | collective-permute-done | bytes 131104 | tf_op jit(solution)/shard_map/ppermute | solution.py:30
  13.0 1.6 %collective-permute-start.4 = (bf16[16,4096]{1,0:T(8,128)(2,1)S(1)}, bf16[16,4096]{1,0:T(8,128)(2,1)S(1)}, u32[]{:S(2)}, u32[]{:S(2)}) collective-permute-start(bf16[16,4096]{1,0:T(8,128)(2,1)S(1)} %collective-permute-done.refs_1_), channel_id=1, source_target_pairs={{0,4},{1,5},{4,8},{5,9},{8,12},{9,13},{12,14},{13,15},{14,10},{15,... | collective-permute-start | bytes 393224 | tf_op jit(solution)/shard_map/ppermute | solution.py:30
  15.1 1.6 %collective-permute-start.10 = (bf16[16,4096]{1,0:T(8,128)(2,1)S(1)}, bf16[16,4096]{1,0:T(8,128)(2,1)S(1)}, u32[]{:S(2)}, u32[]{:S(2)}) collective-permute-start(bf16[16,4096]{1,0:T(8,128)(2,1)S(1)} %collective-permute-done.6.refs_7_), channel_id=1, source_target_pairs={{0,4},{1,5},{4,8},{5,9},{8,12},{9,13},{12,14},{13,15},{14,10},{15,... | collective-permute-start | bytes 393224 | tf_op jit(solution)/shard_map/ppermute | solution.py:30
  17.1 3.8 %split_columns.1 = bf16[16,64,1024]{2,1,0:T(8,128)(2,1)} custom-call(bf16[64,16384]{1,0:T(8,128)(2,1)} %bitcast.8), custom_call_target="tpu_custom_call" | custom-call | tf_op jit(solution)/shard_map/split_columns/pallas_call | solution.py:85
  20.9 0.7 collective-permute-done.11.refs_12_
  21.6 0.7 copy-done.12
  22.3 5.5 %all-to-all-start = ((bf16[16,64,1024]{2,1,0:T(8,128)(2,1)}), bf16[16,64,1024]{2,1,0:T(8,128)(2,1)S(1)}, u32[]{:S(2)}, u32[]{:S(2)}) async-start(bf16[16,64,1024]{2,1,0:T(8,128)(2,1)} %split_columns.1), calls=%async_computation | async-start | bytes 4194304 | tf_op jit(solution)/shard_map/all_to_all | solution.py:277
  27.8 0.5 collective-permute-start.15
  29.3 1.8 %collective-permute-start.8 = (bf16[16,4096]{1,0:T(8,128)(2,1)S(1)}, bf16[16,4096]{1,0:T(8,128)(2,1)S(1)}, u32[]{:S(2)}, u32[]{:S(2)}) collective-permute-start(bf16[16,4096]{1,0:T(8,128)(2,1)S(1)} %collective-permute-done.4.refs_5_), channel_id=1, source_target_pairs={{0,4},{1,5},{4,8},{5,9},{8,12},{9,13},{12,14},{13,15},{14,10},{15,... | collective-permute-start | bytes 393224 | tf_op jit(solution)/shard_map/ppermute | solution.py:30
  31.2 0.6 collective-permute-start.9
  32.5 33.0 %collective-permute-done.8.refs_9_ = bf16[16,4096]{1,0:T(8,128)(2,1)S(1)} collective-permute-done((bf16[16,4096]{1,0:T(8,128)(2,1)S(1)}, bf16[16,4096]{1,0:T(8,128)(2,1)S(1)}, u32[]{:S(2)}, u32[]{:S(2)}) %collective-permute-start.8) | collective-permute-done | bytes 131104 | tf_op jit(solution)/shard_map/ppermute | solution.py:30
  65.5 0.5 collective-permute-start.25
  66.0 14.3 %collective-permute-start.12 = (bf16[16,4096]{1,0:T(8,128)(2,1)S(1)}, bf16[16,4096]{1,0:T(8,128)(2,1)S(1)}, u32[]{:S(2)}, u32[]{:S(2)}) collective-permute-start(bf16[16,4096]{1,0:T(8,128)(2,1)S(1)} %collective-permute-done.8.refs_9_), channel_id=1, source_target_pairs={{0,4},{1,5},{4,8},{5,9},{8,12},{9,13},{12,14},{13,15},{14,10},{15,... | collective-permute-start | bytes 393224 | tf_op jit(solution)/shard_map/ppermute | solution.py:30
  81.2 2.4 %collective-permute-done.12.refs_13_ = bf16[16,4096]{1,0:T(8,128)(2,1)S(1)} collective-permute-done((bf16[16,4096]{1,0:T(8,128)(2,1)S(1)}, bf16[16,4096]{1,0:T(8,128)(2,1)S(1)}, u32[]{:S(2)}, u32[]{:S(2)}) %collective-permute-start.12) | collective-permute-done | bytes 131104 | tf_op jit(solution)/shard_map/ppermute | solution.py:30
  83.7 2.3 %collective-permute-done.13.refs_14_ = bf16[16,4096]{1,0:T(8,128)(2,1)} collective-permute-done((bf16[16,4096]{1,0:T(8,128)(2,1)S(1)}, bf16[16,4096]{1,0:T(8,128)(2,1)}, u32[]{:S(2)}, u32[]{:S(2)}) %collective-permute-start.13) | collective-permute-done | bytes 131104 | tf_op jit(solution)/shard_map/ppermute | solution.py:30
  86.0 0.7 dynamic-slice_bitcast_fusion.place
  86.7 1.0 collective-permute-done.28.refs_29_
  87.8 5.5 %shrink.1 = bf16[64,256]{1,0:T(8,128)(2,1)S(1)} custom-call(s32[31]{0:T(128)S(1)} %dynamic-slice_bitcast_fusion.place, s32[1,256]{1,0:T(1,128)S(1)} %bitcast.7, bf16[64,8192]{1,0:T(8,128)(2,1)} %bitcast.9, bf16[16,8192]{1,0:T(8,128)(2,1)} %refs_0_.3, bf16[16,4096]{1,0:T(8,128)(2,1)} %copy-done.5, bf16[16,4096]{1,0:T(8,128)(2,1)} %copy-done.6, ...), custom_call_target="tpu_custom_call" | custom-call | flops 268435456 | bytes 5242880 | tf_op jit(solution)/shard_map/shrink/pallas_call | solution.py:122
  94.0 1.3 collective-permute-start.31
  95.2 2.4 %collective-permute-done.30 = bf16[64,256]{1,0:T(8,128)(2,1)S(1)} collective-permute-done((bf16[64,256]{1,0:T(8,128)(2,1)S(1)}, bf16[64,256]{1,0:T(8,128)(2,1)S(1)}, u32[]{:S(2)}, u32[]{:S(2)}) %collective-permute-start.30) | collective-permute-done | bytes 32800 | tf_op jit(solution)/shard_map/ppermute | solution.py:290
  97.7 1.7 %collective-permute-start.32 = (bf16[64,256]{1,0:T(8,128)(2,1)S(1)}, bf16[64,256]{1,0:T(8,128)(2,1)S(1)}, u32[]{:S(2)}, u32[]{:S(2)}) collective-permute-start(bf16[64,256]{1,0:T(8,128)(2,1)S(1)} %add_add_fusion.refs_0_), channel_id=1, source_target_pairs={{0,4},{1,5},{2,6},{3,7},{4,8},{5,9},{6,10},{7,11},{8,12},{9,13},{1... | collective-permute-start | bytes 98312 | tf_op jit(solution)/shard_map/ppermute | solution.py:294
  99.4 1.1 collective-permute-start.33
  100.5 2.6 %collective-permute-start.34 = (bf16[64,256]{1,0:T(8,128)(2,1)S(1)}, bf16[64,256]{1,0:T(8,128)(2,1)S(1)}, u32[]{:S(2)}, u32[]{:S(2)}) collective-permute-start(bf16[64,256]{1,0:T(8,128)(2,1)S(1)} %add_add_fusion.refs_0_), channel_id=1, source_target_pairs={{0,12},{1,13},{2,14},{3,15},{4,0},{5,1},{6,2},{7,3},{8,4},{9,5},{1... | collective-permute-start | bytes 98312 | tf_op jit(solution)/shard_map/ppermute | solution.py:294
  103.1 21.0 %project.1 = (f32[256,1024]{1,0:T(8,128)}, f32[256,1024]{1,0:T(8,128)}) custom-call(s32[31]{0:T(128)S(1)} %dynamic-slice_bitcast_fusion.place, bf16[8192,1024]{1,0:T(8,128)(2,1)} %gate_weight_ref.1, bf16[8192,1024]{1,0:T(8,128)(2,1)} %up_weight_ref.1, bf16[16,8192]{1,0:T(8,128)(2,1)} %refs_0_.3, bf16[16,4096]{1,0:T(8,128)(2,1)} %copy-done.5, ...), custom_call_target="tpu_custom_call" | custom-call | flops 8589934592 | bytes 37748736 | tf_op jit(solution)/shard_map/project/pallas_call | solution.py:175
  124.2 0.7 broadcast_in_dim.2.users_ref
  124.9 3.1 %combine.1 = bf16[256,1024]{1,0:T(8,128)(2,1)} custom-call(s32[256,128]{1,0:T(8,128)} %broadcast_in_dim.2.users_ref, f32[256,1024]{1,0:T(8,128)} %get-tuple-element.24.gate_ref, f32[256,1024]{1,0:T(8,128)} %get-tuple-element.25.up_ref, bf16[1024,1024]{1,0:T(8,128)(2,1)S(1)} %bitcast.6, bf16[64,256]{1,0:T(8,128)(2,1)} %copy-done.27, ...), custom_call_target="tpu_custom_call" | custom-call | flops 536870912 | bytes 2621440 | tf_op jit(solution)/shard_map/combine/pallas_call | solution.py:227
  (110 shorter events, 4.4 us)
Async XLA Ops:
  1.0 7.3 %collective-permute-start.2 = (bf16[16,4096]{1,0:T(8,128)(2,1)S(1)}, bf16[16,4096]{1,0:T(8,128)(2,1)S(1)}, u32[]{:S(2)}, u32[]{:S(2)}) collective-permute-start(bf16[16,4096]{1,0:T(8,128)(2,1)S(1)} %get-tuple-element.27), channel_id=1, source_target_pairs={{0,4},{1,5},{4,8},{5,9},{8,12},{9,13},{12,14},{13,15},{14,10},{15,... | collective-permute-start | bytes 393224 | tf_op jit(solution)/shard_map/ppermute | solution.py:30
  4.1 6.4 %collective-permute-start.3 = (bf16[16,4096]{1,0:T(8,128)(2,1)S(1)}, bf16[16,4096]{1,0:T(8,128)(2,1)S(1)}, u32[]{:S(2)}, u32[]{:S(2)}) collective-permute-start(bf16[16,4096]{1,0:T(8,128)(2,1)S(1)} %get-tuple-element.28), channel_id=1, source_target_pairs={{0,2},{1,3},{4,0},{5,1},{8,4},{9,5},{12,8},{13,9},{14,12},{15,13},... | collective-permute-start | bytes 393224 | tf_op jit(solution)/shard_map/ppermute | solution.py:30
  4.1 7.1 %collective-permute-start = (bf16[16,4096]{1,0:T(8,128)(2,1)S(1)}, bf16[16,4096]{1,0:T(8,128)(2,1)S(1)}, u32[]{:S(2)}, u32[]{:S(2)}) collective-permute-start(bf16[16,4096]{1,0:T(8,128)(2,1)S(1)} %get-tuple-element.28), channel_id=1, source_target_pairs={{0,4},{1,5},{4,8},{5,9},{8,12},{9,13},{12,14},{13,15},{14,10},{15,... | collective-permute-start | bytes 393224 | tf_op jit(solution)/shard_map/ppermute | solution.py:30
  6.1 6.9 %collective-permute-start.1 = (bf16[16,4096]{1,0:T(8,128)(2,1)S(1)}, bf16[16,4096]{1,0:T(8,128)(2,1)S(1)}, u32[]{:S(2)}, u32[]{:S(2)}) collective-permute-start(bf16[16,4096]{1,0:T(8,128)(2,1)S(1)} %get-tuple-element.27), channel_id=1, source_target_pairs={{0,2},{1,3},{4,0},{5,1},{8,4},{9,5},{12,8},{13,9},{14,12},{15,13},... | collective-permute-start | bytes 393224 | tf_op jit(solution)/shard_map/ppermute | solution.py:30
  8.3 6.7 %collective-permute-start.6 = (bf16[16,4096]{1,0:T(8,128)(2,1)S(1)}, bf16[16,4096]{1,0:T(8,128)(2,1)S(1)}, u32[]{:S(2)}, u32[]{:S(2)}) collective-permute-start(bf16[16,4096]{1,0:T(8,128)(2,1)S(1)} %collective-permute-done.2.refs_3_), channel_id=1, source_target_pairs={{0,4},{1,5},{4,8},{5,9},{8,12},{9,13},{12,14},{13,15},{14,10},{15,... | collective-permute-start | bytes 393224 | tf_op jit(solution)/shard_map/ppermute | solution.py:30
  10.5 6.2 %collective-permute-start.7 = (bf16[16,4096]{1,0:T(8,128)(2,1)S(1)}, bf16[16,4096]{1,0:T(8,128)(2,1)S(1)}, u32[]{:S(2)}, u32[]{:S(2)}) collective-permute-start(bf16[16,4096]{1,0:T(8,128)(2,1)S(1)} %collective-permute-done.3.refs_4_), channel_id=1, source_target_pairs={{0,2},{1,3},{4,0},{5,1},{8,4},{9,5},{12,8},{13,9},{14,12},{15,13},... | collective-permute-start | bytes 393224 | tf_op jit(solution)/shard_map/ppermute | solution.py:30
  13.0 7.9 %collective-permute-start.4 = (bf16[16,4096]{1,0:T(8,128)(2,1)S(1)}, bf16[16,4096]{1,0:T(8,128)(2,1)S(1)}, u32[]{:S(2)}, u32[]{:S(2)}) collective-permute-start(bf16[16,4096]{1,0:T(8,128)(2,1)S(1)} %collective-permute-done.refs_1_), channel_id=1, source_target_pairs={{0,4},{1,5},{4,8},{5,9},{8,12},{9,13},{12,14},{13,15},{14,10},{15,... | collective-permute-start | bytes 393224 | tf_op jit(solution)/shard_map/ppermute | solution.py:30
  14.6 6.3 %collective-permute-start.5 = (bf16[16,4096]{1,0:T(8,128)(2,1)S(1)}, bf16[16,4096]{1,0:T(8,128)(2,1)S(1)}, u32[]{:S(2)}, u32[]{:S(2)}) collective-permute-start(bf16[16,4096]{1,0:T(8,128)(2,1)S(1)} %collective-permute-done.1.refs_2_), channel_id=1, source_target_pairs={{0,2},{1,3},{4,0},{5,1},{8,4},{9,5},{12,8},{13,9},{14,12},{15,13},... | collective-permute-start | bytes 393224 | tf_op jit(solution)/shard_map/ppermute | solution.py:30
  15.1 5.9 %collective-permute-start.10 = (bf16[16,4096]{1,0:T(8,128)(2,1)S(1)}, bf16[16,4096]{1,0:T(8,128)(2,1)S(1)}, u32[]{:S(2)}, u32[]{:S(2)}) collective-permute-start(bf16[16,4096]{1,0:T(8,128)(2,1)S(1)} %collective-permute-done.6.refs_7_), channel_id=1, source_target_pairs={{0,4},{1,5},{4,8},{5,9},{8,12},{9,13},{12,14},{13,15},{14,10},{15,... | collective-permute-start | bytes 393224 | tf_op jit(solution)/shard_map/ppermute | solution.py:30
  16.6 5.0 %collective-permute-start.11 = (bf16[16,4096]{1,0:T(8,128)(2,1)S(1)}, bf16[16,4096]{1,0:T(8,128)(2,1)S(1)}, u32[]{:S(2)}, u32[]{:S(2)}) collective-permute-start(bf16[16,4096]{1,0:T(8,128)(2,1)S(1)} %collective-permute-done.7.refs_8_), channel_id=1, source_target_pairs={{0,2},{1,3},{4,0},{5,1},{8,4},{9,5},{12,8},{13,9},{14,12},{15,13},... | collective-permute-start | bytes 393224 | tf_op jit(solution)/shard_map/ppermute | solution.py:30
  22.3 101.9 %all-to-all-start = ((bf16[16,64,1024]{2,1,0:T(8,128)(2,1)}), bf16[16,64,1024]{2,1,0:T(8,128)(2,1)S(1)}, u32[]{:S(2)}, u32[]{:S(2)}) async-start(bf16[16,64,1024]{2,1,0:T(8,128)(2,1)} %split_columns.1), calls=%async_computation | async-start | bytes 4194304 | tf_op jit(solution)/shard_map/all_to_all | solution.py:277
  28.3 4.0 %collective-permute-start.14 = (bf16[16,8192]{1,0:T(8,128)(2,1)S(1)}, bf16[16,8192]{1,0:T(8,128)(2,1)S(1)}, u32[]{:S(2)}, u32[]{:S(2)}) collective-permute-start(bf16[16,8192]{1,0:T(8,128)(2,1)S(1)} %copy-done.1), channel_id=1, source_target_pairs={{0,1},{1,0},{2,3},{3,2},{4,5},{5,4},{6,7},{7,6},{8,9},{9,8},{10,11... | collective-permute-start | bytes 786440 | tf_op jit(solution)/shard_map/ppermute | solution.py:47
  28.8 2.9 %collective-permute-start.17 = (bf16[16,4096]{1,0:T(8,128)(2,1)S(1)}, bf16[16,4096]{1,0:T(8,128)(2,1)S(1)}, u32[]{:S(2)}, u32[]{:S(2)}) collective-permute-start(bf16[16,4096]{1,0:T(8,128)(2,1)S(1)} %collective-permute-done.2.refs_3_), channel_id=1, source_target_pairs={{0,1},{1,0},{2,3},{3,2},{4,5},{5,4},{6,7},{7,6},{8,9},{9,8},{10,11... | collective-permute-start | bytes 393224 | tf_op jit(solution)/shard_map/ppermute | solution.py:47
  28.9 2.9 %collective-permute-start.18 = (bf16[16,4096]{1,0:T(8,128)(2,1)S(1)}, bf16[16,4096]{1,0:T(8,128)(2,1)S(1)}, u32[]{:S(2)}, u32[]{:S(2)}) collective-permute-start(bf16[16,4096]{1,0:T(8,128)(2,1)S(1)} %collective-permute-done.3.refs_4_), channel_id=1, source_target_pairs={{0,1},{1,0},{2,3},{3,2},{4,5},{5,4},{6,7},{7,6},{8,9},{9,8},{10,11... | collective-permute-start | bytes 393224 | tf_op jit(solution)/shard_map/ppermute | solution.py:47
  29.3 36.2 %collective-permute-start.8 = (bf16[16,4096]{1,0:T(8,128)(2,1)S(1)}, bf16[16,4096]{1,0:T(8,128)(2,1)S(1)}, u32[]{:S(2)}, u32[]{:S(2)}) collective-permute-start(bf16[16,4096]{1,0:T(8,128)(2,1)S(1)} %collective-permute-done.4.refs_5_), channel_id=1, source_target_pairs={{0,4},{1,5},{4,8},{5,9},{8,12},{9,13},{12,14},{13,15},{14,10},{15,... | collective-permute-start | bytes 393224 | tf_op jit(solution)/shard_map/ppermute | solution.py:30
  31.2 34.4 %collective-permute-start.9 = (bf16[16,4096]{1,0:T(8,128)(2,1)}, bf16[16,4096]{1,0:T(8,128)(2,1)S(1)}, u32[]{:S(2)}, u32[]{:S(2)}) collective-permute-start(bf16[16,4096]{1,0:T(8,128)(2,1)} %copy-done.10), channel_id=1, source_target_pairs={{0,2},{1,3},{4,0},{5,1},{8,4},{9,5},{12,8},{13,9},{14,12},{15,13},... | collective-permute-start | bytes 393224 | tf_op jit(solution)/shard_map/ppermute | solution.py:30
  31.7 34.3 %collective-permute-start.19 = (bf16[16,4096]{1,0:T(8,128)(2,1)S(1)}, bf16[16,4096]{1,0:T(8,128)(2,1)S(1)}, u32[]{:S(2)}, u32[]{:S(2)}) collective-permute-start(bf16[16,4096]{1,0:T(8,128)(2,1)S(1)} %collective-permute-done.4.refs_5_), channel_id=1, source_target_pairs={{0,1},{1,0},{2,3},{3,2},{4,5},{5,4},{6,7},{7,6},{8,9},{9,8},{10,11... | collective-permute-start | bytes 393224 | tf_op jit(solution)/shard_map/ppermute | solution.py:47
  31.8 48.5 %collective-permute-start.20 = (bf16[16,4096]{1,0:T(8,128)(2,1)}, bf16[16,4096]{1,0:T(8,128)(2,1)S(1)}, u32[]{:S(2)}, u32[]{:S(2)}) collective-permute-start(bf16[16,4096]{1,0:T(8,128)(2,1)} %copy-done.10), channel_id=1, source_target_pairs={{0,1},{1,0},{2,3},{3,2},{4,5},{5,4},{6,7},{7,6},{8,9},{9,8},{10,11... | collective-permute-start | bytes 393224 | tf_op jit(solution)/shard_map/ppermute | solution.py:47
  32.3 48.0 %collective-permute-start.21 = (bf16[16,4096]{1,0:T(8,128)(2,1)S(1)}, bf16[16,4096]{1,0:T(8,128)(2,1)S(1)}, u32[]{:S(2)}, u32[]{:S(2)}) collective-permute-start(bf16[16,4096]{1,0:T(8,128)(2,1)S(1)} %collective-permute-done.6.refs_7_), channel_id=1, source_target_pairs={{0,1},{1,0},{2,3},{3,2},{4,5},{5,4},{6,7},{7,6},{8,9},{9,8},{10,11... | collective-permute-start | bytes 393224 | tf_op jit(solution)/shard_map/ppermute | solution.py:47
  65.5 15.1 %collective-permute-start.22 = (bf16[16,4096]{1,0:T(8,128)(2,1)S(1)}, bf16[16,4096]{1,0:T(8,128)(2,1)S(1)}, u32[]{:S(2)}, u32[]{:S(2)}) collective-permute-start(bf16[16,4096]{1,0:T(8,128)(2,1)S(1)} %collective-permute-done.7.refs_8_), channel_id=1, source_target_pairs={{0,1},{1,0},{2,3},{3,2},{4,5},{5,4},{6,7},{7,6},{8,9},{9,8},{10,11... | collective-permute-start | bytes 393224 | tf_op jit(solution)/shard_map/ppermute | solution.py:47
  65.5 15.5 %collective-permute-start.25 = (bf16[16,4096]{1,0:T(8,128)(2,1)}, bf16[16,4096]{1,0:T(8,128)(2,1)S(1)}, u32[]{:S(2)}, u32[]{:S(2)}) collective-permute-start(bf16[16,4096]{1,0:T(8,128)(2,1)} %copy-done.11), channel_id=1, source_target_pairs={{0,1},{1,0},{2,3},{3,2},{4,5},{5,4},{6,7},{7,6},{8,9},{9,8},{10,11... | collective-permute-start | bytes 393224 | tf_op jit(solution)/shard_map/ppermute | solution.py:47
  66.0 17.6 %collective-permute-start.12 = (bf16[16,4096]{1,0:T(8,128)(2,1)S(1)}, bf16[16,4096]{1,0:T(8,128)(2,1)S(1)}, u32[]{:S(2)}, u32[]{:S(2)}) collective-permute-start(bf16[16,4096]{1,0:T(8,128)(2,1)S(1)} %collective-permute-done.8.refs_9_), channel_id=1, source_target_pairs={{0,4},{1,5},{4,8},{5,9},{8,12},{9,13},{12,14},{13,15},{14,10},{15,... | collective-permute-start | bytes 393224 | tf_op jit(solution)/shard_map/ppermute | solution.py:30
  80.3 5.7 %collective-permute-start.13 = (bf16[16,4096]{1,0:T(8,128)(2,1)S(1)}, bf16[16,4096]{1,0:T(8,128)(2,1)}, u32[]{:S(2)}, u32[]{:S(2)}) collective-permute-start(bf16[16,4096]{1,0:T(8,128)(2,1)S(1)} %collective-permute-done.9.refs_10_), channel_id=1, source_target_pairs={{0,2},{1,3},{4,0},{5,1},{8,4},{9,5},{12,8},{13,9},{14,12},{15,13},... | collective-permute-start | bytes 393224 | tf_op jit(solution)/shard_map/ppermute | solution.py:30
  80.3 6.3 %collective-permute-start.26 = (bf16[16,4096]{1,0:T(8,128)(2,1)}, bf16[16,4096]{1,0:T(8,128)(2,1)S(1)}, u32[]{:S(2)}, u32[]{:S(2)}) collective-permute-start(bf16[16,4096]{1,0:T(8,128)(2,1)} %copy-done.12), channel_id=1, source_target_pairs={{0,1},{1,0},{2,3},{3,2},{4,5},{5,4},{6,7},{7,6},{8,9},{9,8},{10,11... | collective-permute-start | bytes 393224 | tf_op jit(solution)/shard_map/ppermute | solution.py:47
  80.6 6.1 %collective-permute-start.23 = (bf16[16,4096]{1,0:T(8,128)(2,1)S(1)}, bf16[16,4096]{1,0:T(8,128)(2,1)S(1)}, u32[]{:S(2)}, u32[]{:S(2)}) collective-permute-start(bf16[16,4096]{1,0:T(8,128)(2,1)S(1)} %collective-permute-done.8.refs_9_), channel_id=1, source_target_pairs={{0,1},{1,0},{2,3},{3,2},{4,5},{5,4},{6,7},{7,6},{8,9},{9,8},{10,11... | collective-permute-start | bytes 393224 | tf_op jit(solution)/shard_map/ppermute | solution.py:47
  81.0 5.7 %collective-permute-start.24 = (bf16[16,4096]{1,0:T(8,128)(2,1)S(1)}, bf16[16,4096]{1,0:T(8,128)(2,1)}, u32[]{:S(2)}, u32[]{:S(2)}) collective-permute-start(bf16[16,4096]{1,0:T(8,128)(2,1)S(1)} %collective-permute-done.9.refs_10_), channel_id=1, source_target_pairs={{0,1},{1,0},{2,3},{3,2},{4,5},{5,4},{6,7},{7,6},{8,9},{9,8},{10,11... | collective-permute-start | bytes 393224 | tf_op jit(solution)/shard_map/ppermute | solution.py:47
  83.7 3.0 %collective-permute-start.27 = (bf16[16,4096]{1,0:T(8,128)(2,1)S(1)}, bf16[16,4096]{1,0:T(8,128)(2,1)}, u32[]{:S(2)}, u32[]{:S(2)}) collective-permute-start(bf16[16,4096]{1,0:T(8,128)(2,1)S(1)} %collective-permute-done.12.refs_13_), channel_id=1, source_target_pairs={{0,1},{1,0},{2,3},{3,2},{4,5},{5,4},{6,7},{7,6},{8,9},{9,8},{10,11... | collective-permute-start | bytes 393224 | tf_op jit(solution)/shard_map/ppermute | solution.py:47
  93.5 4.1 %collective-permute-start.30 = (bf16[64,256]{1,0:T(8,128)(2,1)S(1)}, bf16[64,256]{1,0:T(8,128)(2,1)S(1)}, u32[]{:S(2)}, u32[]{:S(2)}) collective-permute-start(bf16[64,256]{1,0:T(8,128)(2,1)S(1)} %shrink.1), channel_id=1, source_target_pairs={{0,2},{1,3},{2,0},{3,1},{4,6},{5,7},{6,4},{7,5},{8,10},{9,11},{10,... | collective-permute-start | bytes 98312 | tf_op jit(solution)/shard_map/ppermute | solution.py:290
  94.0 3.7 %collective-permute-start.31 = (bf16[64,256]{1,0:T(8,128)(2,1)S(1)}, bf16[64,256]{1,0:T(8,128)(2,1)S(1)}, u32[]{:S(2)}, u32[]{:S(2)}) collective-permute-start(bf16[64,256]{1,0:T(8,128)(2,1)S(1)} %shrink.1), channel_id=1, source_target_pairs={{0,3},{1,2},{2,1},{3,0},{4,7},{5,6},{6,5},{7,4},{8,11},{9,10},{10,... | collective-permute-start | bytes 98312 | tf_op jit(solution)/shard_map/ppermute | solution.py:290
  97.7 26.4 %collective-permute-start.32 = (bf16[64,256]{1,0:T(8,128)(2,1)S(1)}, bf16[64,256]{1,0:T(8,128)(2,1)S(1)}, u32[]{:S(2)}, u32[]{:S(2)}) collective-permute-start(bf16[64,256]{1,0:T(8,128)(2,1)S(1)} %add_add_fusion.refs_0_), channel_id=1, source_target_pairs={{0,4},{1,5},{2,6},{3,7},{4,8},{5,9},{6,10},{7,11},{8,12},{9,13},{1... | collective-permute-start | bytes 98312 | tf_op jit(solution)/shard_map/ppermute | solution.py:294
  99.4 24.7 %collective-permute-start.33 = (bf16[64,256]{1,0:T(8,128)(2,1)S(1)}, bf16[64,256]{1,0:T(8,128)(2,1)S(1)}, u32[]{:S(2)}, u32[]{:S(2)}) collective-permute-start(bf16[64,256]{1,0:T(8,128)(2,1)S(1)} %add_add_fusion.refs_0_), channel_id=1, source_target_pairs={{0,8},{1,9},{2,10},{3,11},{4,12},{5,13},{6,14},{7,15},{8,0},{9,1},... | collective-permute-start | bytes 98312 | tf_op jit(solution)/shard_map/ppermute | solution.py:294
  100.5 23.6 %collective-permute-start.34 = (bf16[64,256]{1,0:T(8,128)(2,1)S(1)}, bf16[64,256]{1,0:T(8,128)(2,1)S(1)}, u32[]{:S(2)}, u32[]{:S(2)}) collective-permute-start(bf16[64,256]{1,0:T(8,128)(2,1)S(1)} %add_add_fusion.refs_0_), channel_id=1, source_target_pairs={{0,12},{1,13},{2,14},{3,15},{4,0},{5,1},{6,2},{7,3},{8,4},{9,5},{1... | collective-permute-start | bytes 98312 | tf_op jit(solution)/shard_map/ppermute | solution.py:294
  (35 other events, 616.4 us)

commit v8 on v7

--- a/solution.py
+++ b/solution.py
@@ -44,7 +44,8 @@
 
     flips = [(d, d ^ 1) for d in range(size)]
     found = [(value, column) for value, column, _ in pieces]
-    found += [(lax.ppermute(value, axis, flips), column) for value, column, _ in pieces]
+    ready = lax.optimization_barrier([value for value, _, _ in pieces])
+    found += [(lax.ppermute(value, axis, flips), column) for value, (_, column, _) in zip(ready, pieces)]
     where = [
         [
             ring[(ring.index(device // CORES) + distance) % chips] * CORES + core
@@ -268,12 +269,12 @@
 
     def beside(chain, step, values):
         nonlocal own_maps, maps
-        if (chain, step) not in ((0, 1), (0, 2), (1, steps - 1)):
-            return values
-        own_maps, *values = lax.optimization_barrier((own_maps, *values))
-        if (chain, step) == (0, 1):
-            own_maps = split_columns(own_maps, size)
-        if chain == 1:
+        if step == steps - 1:
+            own_maps, *values = lax.optimization_barrier((own_maps, *values))
+            if chain == 1:
+                own_maps = split_columns(own_maps, size)
+        if step == steps:
+            own_maps, *values = lax.optimization_barrier((own_maps, *values))
             maps = lax.all_to_all(own_maps, axis, split_axis=0, concat_axis=0, tiled=True)
         return values
 

time: 128 us -> 90.1 us (0.70)
  waiting for transfers between devices: 46.7 us -> 17.8 us
  starting transfers between devices: 44.4 us -> 34.1 us
    ppermute x14, waiting for transfers between devices: 43.3 us -> 8.69 us  [moved(): return lax.ppermute(value, axis, pairs)]
    ppermute x14, starting transfers between devices: 28 us -> 15.8 us  [moved(): return lax.ppermute(value, axis, pairs)]
    ppermute x3, waiting for transfers between devices: 0.01 us -> 4.95 us  [per_device(): lax.ppermute(plane, axis, [(d, (d + shift * near) % size) for d in range(...]
    ppermute x3, starting transfers between devices: 5.41 us -> 7.59 us  [per_device(): lax.ppermute(plane, axis, [(d, (d + shift * near) % size) for d in range(...]
    all_to_all x1, starting transfers between devices: 5.52 us -> 4.22 us  [beside(): lax.all_to_all(own_maps, axis, split_axis=0, concat_axis=0, tiled=True)]
  transfers between devices with their start and end apart: 36 -> 36, of which waited for: 9 -> 12; matrix products, arithmetic and copies ran while one was open for 1% -> 1% of each run, Pallas kernels for 24% -> 34%
where the time goes in v8:
time: 90.1 us; the launch traced here: 89.8 us
  starting transfers between devices  34.1 us (38%)
  Pallas kernels  33.5 us (37%)
  waiting for transfers between devices  17.8 us (20%)
  local copies, waits for them, and re-layouts  4.21 us (5%)
    pallas_call x1, Pallas kernels, project(): pl.pallas_call(functools.partial(project_kernel, columns, len(pieces)), g...  21 us
    ppermute x14, starting transfers between devices, moved(): return lax.ppermute(value, axis, pairs)  15.8 us
    ppermute x14, waiting for transfers between devices, moved(): return lax.ppermute(value, axis, pairs)  8.69 us
    ppermute x3, starting transfers between devices, per_device(): lax.ppermute(plane, axis, [(d, (d + shift * near) % size) for d in range(...  7.59 us
    pallas_call x1, Pallas kernels, shrink(): pl.pallas_call(functools.partial(shrink_kernel, columns, len(pieces), ran...  5.48 us
    ppermute x3, waiting for transfers between devices, per_device(): lax.ppermute(plane, axis, [(d, (d + shift * near) % size) for d in range(...  4.95 us
    ppermute x15, starting transfers between devices, ring_gather(): lax.ppermute(value, axis, flips)  4.35 us
    all_to_all x1, starting transfers between devices, beside(): lax.all_to_all(own_maps, axis, split_axis=0, concat_axis=0, tiled=True)  4.22 us
  transfers between devices with their start and end apart: 36, of which 12 were waited for; matrix products, arithmetic and copies ran while one was open for 1% of the time, Pallas kernels for 34%

profile of v8, /device:TPU:0, one launch (start us, length us, event | category | flops | bytes accessed | tf_op | source)
XLA Modules:
  0.0 89.8 jit_solution(3913198283612832543)
XLA Ops:
  0.0 1.0 %fusion = (bf16[16,4096]{1,0:T(8,128)(2,1)S(1)}, bf16[16,4096]{1,0:T(8,128)(2,1)S(1)}) fusion(bf16[16,8192]{1,0:T(8,128)(2,1)} %refs_0_.3), kind=kLoop, calls=%fused_computation.2 | loop fusion | bytes 524288 | tf_op jit(solution)/shard_map/slice | solution.py:34
  1.0 3.1 %collective-permute-start = (bf16[16,4096]{1,0:T(8,128)(2,1)S(1)}, bf16[16,4096]{1,0:T(8,128)(2,1)S(1)}, u32[]{:S(2)}, u32[]{:S(2)}) collective-permute-start(bf16[16,4096]{1,0:T(8,128)(2,1)S(1)} %get-tuple-element.58), channel_id=1, source_target_pairs={{0,4},{1,5},{4,8},{5,9},{8,12},{9,13},{12,14},{13,15},{14,10},{15,... | collective-permute-start | bytes 393224 | tf_op jit(solution)/shard_map/ppermute | solution.py:30
  4.1 2.0 %collective-permute-start.2 = (bf16[16,4096]{1,0:T(8,128)(2,1)S(1)}, bf16[16,4096]{1,0:T(8,128)(2,1)S(1)}, u32[]{:S(2)}, u32[]{:S(2)}) collective-permute-start(bf16[16,4096]{1,0:T(8,128)(2,1)S(1)} %get-tuple-element.57), channel_id=1, source_target_pairs={{0,4},{1,5},{4,8},{5,9},{8,12},{9,13},{12,14},{13,15},{14,10},{15,... | collective-permute-start | bytes 393224 | tf_op jit(solution)/shard_map/ppermute | solution.py:30
  6.1 2.2 %collective-permute-done.refs_1_ = bf16[16,4096]{1,0:T(8,128)(2,1)S(1)} collective-permute-done((bf16[16,4096]{1,0:T(8,128)(2,1)S(1)}, bf16[16,4096]{1,0:T(8,128)(2,1)S(1)}, u32[]{:S(2)}, u32[]{:S(2)}) %collective-permute-start) | collective-permute-done | bytes 131104 | tf_op jit(solution)/shard_map/ppermute | solution.py:30
  8.3 2.1 %collective-permute-start.4 = (bf16[16,4096]{1,0:T(8,128)(2,1)S(1)}, bf16[16,4096]{1,0:T(8,128)(2,1)S(1)}, u32[]{:S(2)}, u32[]{:S(2)}) collective-permute-start(bf16[16,4096]{1,0:T(8,128)(2,1)S(1)} %collective-permute-done.refs_1_), channel_id=1, source_target_pairs={{0,4},{1,5},{4,8},{5,9},{8,12},{9,13},{12,14},{13,15},{14,10},{15,... | collective-permute-start | bytes 393224 | tf_op jit(solution)/shard_map/ppermute | solution.py:30
  10.5 0.7 collective-permute-done.2.refs_3_
  11.1 2.1 %collective-permute-start.6 = (bf16[16,4096]{1,0:T(8,128)(2,1)S(1)}, bf16[16,4096]{1,0:T(8,128)(2,1)S(1)}, u32[]{:S(2)}, u32[]{:S(2)}) collective-permute-start(bf16[16,4096]{1,0:T(8,128)(2,1)S(1)} %collective-permute-done.2.refs_3_), channel_id=1, source_target_pairs={{0,4},{1,5},{4,8},{5,9},{8,12},{9,13},{12,14},{13,15},{14,10},{15,... | collective-permute-start | bytes 393224 | tf_op jit(solution)/shard_map/ppermute | solution.py:30
  13.3 1.2 %collective-permute-done.4.refs_5_ = bf16[16,4096]{1,0:T(8,128)(2,1)S(1)} collective-permute-done((bf16[16,4096]{1,0:T(8,128)(2,1)S(1)}, bf16[16,4096]{1,0:T(8,128)(2,1)S(1)}, u32[]{:S(2)}, u32[]{:S(2)}) %collective-permute-start.4) | collective-permute-done | bytes 131104 | tf_op jit(solution)/shard_map/ppermute | solution.py:30
  14.5 2.2 %collective-permute-start.8 = (bf16[16,4096]{1,0:T(8,128)(2,1)S(1)}, bf16[16,4096]{1,0:T(8,128)(2,1)}, u32[]{:S(2)}, u32[]{:S(2)}) collective-permute-start(bf16[16,4096]{1,0:T(8,128)(2,1)S(1)} %collective-permute-done.4.refs_5_), channel_id=1, source_target_pairs={{0,4},{1,5},{4,8},{5,9},{8,12},{9,13},{12,14},{13,15},{14,10},{15,... | collective-permute-start | bytes 393224 | tf_op jit(solution)/shard_map/ppermute | solution.py:30
  16.8 0.8 collective-permute-done.6.refs_7_
  17.6 2.0 %collective-permute-start.10 = (bf16[16,4096]{1,0:T(8,128)(2,1)S(1)}, bf16[16,4096]{1,0:T(8,128)(2,1)S(1)}, u32[]{:S(2)}, u32[]{:S(2)}) collective-permute-start(bf16[16,4096]{1,0:T(8,128)(2,1)S(1)} %collective-permute-done.6.refs_7_), channel_id=1, source_target_pairs={{0,4},{1,5},{4,8},{5,9},{8,12},{9,13},{12,14},{13,15},{14,10},{15,... | collective-permute-start | bytes 393224 | tf_op jit(solution)/shard_map/ppermute | solution.py:30
  19.7 0.8 collective-permute-done.8.refs_9_
  20.5 1.5 %collective-permute-done.9.refs_10_ = bf16[16,4096]{1,0:T(8,128)(2,1)} collective-permute-done((bf16[16,4096]{1,0:T(8,128)(2,1)S(1)}, bf16[16,4096]{1,0:T(8,128)(2,1)}, u32[]{:S(2)}, u32[]{:S(2)}) %collective-permute-start.9) | collective-permute-done | bytes 131104 | tf_op jit(solution)/shard_map/ppermute | solution.py:30
  21.9 1.6 %collective-permute-start.12 = (bf16[16,4096]{1,0:T(8,128)(2,1)}, bf16[16,4096]{1,0:T(8,128)(2,1)S(1)}, u32[]{:S(2)}, u32[]{:S(2)}) collective-permute-start(bf16[16,4096]{1,0:T(8,128)(2,1)} %collective-permute-done.8.refs_9_), channel_id=1, source_target_pairs={{0,4},{1,5},{4,8},{5,9},{8,12},{9,13},{12,14},{13,15},{14,10},{15,... | collective-permute-start | bytes 393224 | tf_op jit(solution)/shard_map/ppermute | solution.py:30
  23.5 0.4 collective-permute-start.13
  24.0 1.6 %collective-permute-done.11.refs_12_ = bf16[16,4096]{1,0:T(8,128)(2,1)S(1)} collective-permute-done((bf16[16,4096]{1,0:T(8,128)(2,1)}, bf16[16,4096]{1,0:T(8,128)(2,1)S(1)}, u32[]{:S(2)}, u32[]{:S(2)}) %collective-permute-start.11) | collective-permute-done | bytes 131104 | tf_op jit(solution)/shard_map/ppermute | solution.py:30
  25.5 3.9 %split_columns.1 = bf16[16,64,1024]{2,1,0:T(8,128)(2,1)} custom-call(bf16[64,16384]{1,0:T(8,128)(2,1)} %bitcast.8), custom_call_target="tpu_custom_call" | custom-call | tf_op jit(solution)/shard_map/split_columns/pallas_call | solution.py:86
  29.4 0.6 copy-done.12
  30.1 4.2 %all-to-all-start = ((bf16[16,64,1024]{2,1,0:T(8,128)(2,1)}), bf16[16,64,1024]{2,1,0:T(8,128)(2,1)S(1)}, u32[]{:S(2)}, u32[]{:S(2)}) async-start(bf16[16,64,1024]{2,1,0:T(8,128)(2,1)} %split_columns.1), calls=%async_computation | async-start | bytes 4194304 | tf_op jit(solution)/shard_map/all_to_all | solution.py:278
  34.3 0.5 collective-permute-start.15
  39.3 0.7 dynamic-slice_bitcast_fusion.place
  41.1 5.5 %shrink.1 = bf16[64,256]{1,0:T(8,128)(2,1)S(1)} custom-call(s32[31]{0:T(128)S(1)} %dynamic-slice_bitcast_fusion.place, s32[1,256]{1,0:T(1,128)S(1)} %bitcast.7, bf16[64,8192]{1,0:T(8,128)(2,1)} %bitcast.9, bf16[16,8192]{1,0:T(8,128)(2,1)} %refs_0_.3, bf16[16,4096]{1,0:T(8,128)(2,1)} %copy-done.3, bf16[16,4096]{1,0:T(8,128)(2,1)} %copy-done.4, ...), custom_call_target="tpu_custom_call" | custom-call | flops 268435456 | bytes 5242880 | tf_op jit(solution)/shard_map/shrink/pallas_call | solution.py:123
  46.9 1.8 %collective-permute-start.30 = (bf16[64,256]{1,0:T(8,128)(2,1)S(1)}, bf16[64,256]{1,0:T(8,128)(2,1)S(1)}, u32[]{:S(2)}, u32[]{:S(2)}) collective-permute-start(bf16[64,256]{1,0:T(8,128)(2,1)S(1)} %shrink.1), channel_id=1, source_target_pairs={{0,2},{1,3},{2,0},{3,1},{4,6},{5,7},{6,4},{7,5},{8,10},{9,11},{10,... | collective-permute-start | bytes 98312 | tf_op jit(solution)/shard_map/ppermute | solution.py:291
  48.7 2.7 %collective-permute-done.30 = bf16[64,256]{1,0:T(8,128)(2,1)S(1)} collective-permute-done((bf16[64,256]{1,0:T(8,128)(2,1)S(1)}, bf16[64,256]{1,0:T(8,128)(2,1)S(1)}, u32[]{:S(2)}, u32[]{:S(2)}) %collective-permute-start.30) | collective-permute-done | bytes 32800 | tf_op jit(solution)/shard_map/ppermute | solution.py:291
  51.4 0.9 collective-permute-done.31
  52.3 5.2 %collective-permute-start.32 = (bf16[64,256]{1,0:T(8,128)(2,1)S(1)}, bf16[64,256]{1,0:T(8,128)(2,1)S(1)}, u32[]{:S(2)}, u32[]{:S(2)}) collective-permute-start(bf16[64,256]{1,0:T(8,128)(2,1)S(1)} %add_add_fusion.refs_0_), channel_id=1, source_target_pairs={{0,4},{1,5},{2,6},{3,7},{4,8},{5,9},{6,10},{7,11},{8,12},{9,13},{1... | collective-permute-start | bytes 98312 | tf_op jit(solution)/shard_map/ppermute | solution.py:295
  57.4 1.1 %collective-permute-start.33 = (bf16[64,256]{1,0:T(8,128)(2,1)S(1)}, bf16[64,256]{1,0:T(8,128)(2,1)S(1)}, u32[]{:S(2)}, u32[]{:S(2)}) collective-permute-start(bf16[64,256]{1,0:T(8,128)(2,1)S(1)} %add_add_fusion.refs_0_), channel_id=1, source_target_pairs={{0,8},{1,9},{2,10},{3,11},{4,12},{5,13},{6,14},{7,15},{8,0},{9,1},... | collective-permute-start | bytes 98312 | tf_op jit(solution)/shard_map/ppermute | solution.py:295
  58.5 1.3 %collective-permute-start.34 = (bf16[64,256]{1,0:T(8,128)(2,1)S(1)}, bf16[64,256]{1,0:T(8,128)(2,1)S(1)}, u32[]{:S(2)}, u32[]{:S(2)}) collective-permute-start(bf16[64,256]{1,0:T(8,128)(2,1)S(1)} %add_add_fusion.refs_0_), channel_id=1, source_target_pairs={{0,12},{1,13},{2,14},{3,15},{4,0},{5,1},{6,2},{7,3},{8,4},{9,5},{1... | collective-permute-start | bytes 98312 | tf_op jit(solution)/shard_map/ppermute | solution.py:295
  59.9 21.0 %project.1 = (f32[256,1024]{1,0:T(8,128)}, f32[256,1024]{1,0:T(8,128)}) custom-call(s32[31]{0:T(128)S(1)} %dynamic-slice_bitcast_fusion.place, bf16[8192,1024]{1,0:T(8,128)(2,1)} %gate_weight_ref.1, bf16[8192,1024]{1,0:T(8,128)(2,1)} %up_weight_ref.1, bf16[16,8192]{1,0:T(8,128)(2,1)} %refs_0_.3, bf16[16,4096]{1,0:T(8,128)(2,1)} %copy-done.3, ...), custom_call_target="tpu_custom_call" | custom-call | flops 8589934592 | bytes 37748736 | tf_op jit(solution)/shard_map/project/pallas_call | solution.py:176
  80.9 4.9 %collective-permute-done.33.refs_2_ = bf16[64,256]{1,0:T(8,128)(2,1)S(1)} collective-permute-done((bf16[64,256]{1,0:T(8,128)(2,1)S(1)}, bf16[64,256]{1,0:T(8,128)(2,1)S(1)}, u32[]{:S(2)}, u32[]{:S(2)}) %collective-permute-start.33) | collective-permute-done | bytes 32800 | tf_op jit(solution)/shard_map/ppermute | solution.py:295
  85.9 0.7 broadcast_in_dim.2.users_ref
  86.6 3.1 %combine.1 = bf16[256,1024]{1,0:T(8,128)(2,1)} custom-call(s32[256,128]{1,0:T(8,128)} %broadcast_in_dim.2.users_ref, f32[256,1024]{1,0:T(8,128)} %get-tuple-element.54.gate_ref, f32[256,1024]{1,0:T(8,128)} %get-tuple-element.55.up_ref, bf16[1024,1024]{1,0:T(8,128)(2,1)S(1)} %bitcast.6, bf16[64,256]{1,0:T(8,128)(2,1)} %copy-done.26, ...), custom_call_target="tpu_custom_call" | custom-call | flops 536870912 | bytes 2621440 | tf_op jit(solution)/shard_map/combine/pallas_call | solution.py:228
  (108 shorter events, 6.3 us)
Async XLA Ops:
  1.0 7.3 %collective-permute-start = (bf16[16,4096]{1,0:T(8,128)(2,1)S(1)}, bf16[16,4096]{1,0:T(8,128)(2,1)S(1)}, u32[]{:S(2)}, u32[]{:S(2)}) collective-permute-start(bf16[16,4096]{1,0:T(8,128)(2,1)S(1)} %get-tuple-element.58), channel_id=1, source_target_pairs={{0,4},{1,5},{4,8},{5,9},{8,12},{9,13},{12,14},{13,15},{14,10},{15,... | collective-permute-start | bytes 393224 | tf_op jit(solution)/shard_map/ppermute | solution.py:30
  4.1 6.4 %collective-permute-start.1 = (bf16[16,4096]{1,0:T(8,128)(2,1)S(1)}, bf16[16,4096]{1,0:T(8,128)(2,1)S(1)}, u32[]{:S(2)}, u32[]{:S(2)}) collective-permute-start(bf16[16,4096]{1,0:T(8,128)(2,1)S(1)} %get-tuple-element.57), channel_id=1, source_target_pairs={{0,2},{1,3},{4,0},{5,1},{8,4},{9,5},{12,8},{13,9},{14,12},{15,13},... | collective-permute-start | bytes 393224 | tf_op jit(solution)/shard_map/ppermute | solution.py:30
  4.1 7.1 %collective-permute-start.2 = (bf16[16,4096]{1,0:T(8,128)(2,1)S(1)}, bf16[16,4096]{1,0:T(8,128)(2,1)S(1)}, u32[]{:S(2)}, u32[]{:S(2)}) collective-permute-start(bf16[16,4096]{1,0:T(8,128)(2,1)S(1)} %get-tuple-element.57), channel_id=1, source_target_pairs={{0,4},{1,5},{4,8},{5,9},{8,12},{9,13},{12,14},{13,15},{14,10},{15,... | collective-permute-start | bytes 393224 | tf_op jit(solution)/shard_map/ppermute | solution.py:30
  6.1 7.2 %collective-permute-start.3 = (bf16[16,4096]{1,0:T(8,128)(2,1)S(1)}, bf16[16,4096]{1,0:T(8,128)(2,1)S(1)}, u32[]{:S(2)}, u32[]{:S(2)}) collective-permute-start(bf16[16,4096]{1,0:T(8,128)(2,1)S(1)} %get-tuple-element.58), channel_id=1, source_target_pairs={{0,2},{1,3},{4,0},{5,1},{8,4},{9,5},{12,8},{13,9},{14,12},{15,13},... | collective-permute-start | bytes 393224 | tf_op jit(solution)/shard_map/ppermute | solution.py:30
  8.3 6.2 %collective-permute-start.4 = (bf16[16,4096]{1,0:T(8,128)(2,1)S(1)}, bf16[16,4096]{1,0:T(8,128)(2,1)S(1)}, u32[]{:S(2)}, u32[]{:S(2)}) collective-permute-start(bf16[16,4096]{1,0:T(8,128)(2,1)S(1)} %collective-permute-done.refs_1_), channel_id=1, source_target_pairs={{0,4},{1,5},{4,8},{5,9},{8,12},{9,13},{12,14},{13,15},{14,10},{15,... | collective-permute-start | bytes 393224 | tf_op jit(solution)/shard_map/ppermute | solution.py:30
  10.5 6.2 %collective-permute-start.5 = (bf16[16,4096]{1,0:T(8,128)(2,1)S(1)}, bf16[16,4096]{1,0:T(8,128)(2,1)S(1)}, u32[]{:S(2)}, u32[]{:S(2)}) collective-permute-start(bf16[16,4096]{1,0:T(8,128)(2,1)S(1)} %collective-permute-done.1.refs_2_), channel_id=1, source_target_pairs={{0,2},{1,3},{4,0},{5,1},{8,4},{9,5},{12,8},{13,9},{14,12},{15,13},... | collective-permute-start | bytes 393224 | tf_op jit(solution)/shard_map/ppermute | solution.py:30
  11.1 6.5 %collective-permute-start.6 = (bf16[16,4096]{1,0:T(8,128)(2,1)S(1)}, bf16[16,4096]{1,0:T(8,128)(2,1)S(1)}, u32[]{:S(2)}, u32[]{:S(2)}) collective-permute-start(bf16[16,4096]{1,0:T(8,128)(2,1)S(1)} %collective-permute-done.2.refs_3_), channel_id=1, source_target_pairs={{0,4},{1,5},{4,8},{5,9},{8,12},{9,13},{12,14},{13,15},{14,10},{15,... | collective-permute-start | bytes 393224 | tf_op jit(solution)/shard_map/ppermute | solution.py:30
  13.3 6.3 %collective-permute-start.7 = (bf16[16,4096]{1,0:T(8,128)(2,1)S(1)}, bf16[16,4096]{1,0:T(8,128)(2,1)}, u32[]{:S(2)}, u32[]{:S(2)}) collective-permute-start(bf16[16,4096]{1,0:T(8,128)(2,1)S(1)} %collective-permute-done.3.refs_4_), channel_id=1, source_target_pairs={{0,2},{1,3},{4,0},{5,1},{8,4},{9,5},{12,8},{13,9},{14,12},{15,13},... | collective-permute-start | bytes 393224 | tf_op jit(solution)/shard_map/ppermute | solution.py:30
  14.5 6.0 %collective-permute-start.8 = (bf16[16,4096]{1,0:T(8,128)(2,1)S(1)}, bf16[16,4096]{1,0:T(8,128)(2,1)}, u32[]{:S(2)}, u32[]{:S(2)}) collective-permute-start(bf16[16,4096]{1,0:T(8,128)(2,1)S(1)} %collective-permute-done.4.refs_5_), channel_id=1, source_target_pairs={{0,4},{1,5},{4,8},{5,9},{8,12},{9,13},{12,14},{13,15},{14,10},{15,... | collective-permute-start | bytes 393224 | tf_op jit(solution)/shard_map/ppermute | solution.py:30
  16.7 5.3 %collective-permute-start.9 = (bf16[16,4096]{1,0:T(8,128)(2,1)S(1)}, bf16[16,4096]{1,0:T(8,128)(2,1)}, u32[]{:S(2)}, u32[]{:S(2)}) collective-permute-start(bf16[16,4096]{1,0:T(8,128)(2,1)S(1)} %collective-permute-done.5.refs_6_), channel_id=1, source_target_pairs={{0,2},{1,3},{4,0},{5,1},{8,4},{9,5},{12,8},{13,9},{14,12},{15,13},... | collective-permute-start | bytes 393224 | tf_op jit(solution)/shard_map/ppermute | solution.py:30
  17.6 6.3 %collective-permute-start.10 = (bf16[16,4096]{1,0:T(8,128)(2,1)S(1)}, bf16[16,4096]{1,0:T(8,128)(2,1)S(1)}, u32[]{:S(2)}, u32[]{:S(2)}) collective-permute-start(bf16[16,4096]{1,0:T(8,128)(2,1)S(1)} %collective-permute-done.6.refs_7_), channel_id=1, source_target_pairs={{0,4},{1,5},{4,8},{5,9},{8,12},{9,13},{12,14},{13,15},{14,10},{15,... | collective-permute-start | bytes 393224 | tf_op jit(solution)/shard_map/ppermute | solution.py:30
  19.6 5.9 %collective-permute-start.11 = (bf16[16,4096]{1,0:T(8,128)(2,1)}, bf16[16,4096]{1,0:T(8,128)(2,1)S(1)}, u32[]{:S(2)}, u32[]{:S(2)}) collective-permute-start(bf16[16,4096]{1,0:T(8,128)(2,1)} %collective-permute-done.7.refs_8_), channel_id=1, source_target_pairs={{0,2},{1,3},{4,0},{5,1},{8,4},{9,5},{12,8},{13,9},{14,12},{15,13},... | collective-permute-start | bytes 393224 | tf_op jit(solution)/shard_map/ppermute | solution.py:30
  21.9 7.5 %collective-permute-start.12 = (bf16[16,4096]{1,0:T(8,128)(2,1)}, bf16[16,4096]{1,0:T(8,128)(2,1)S(1)}, u32[]{:S(2)}, u32[]{:S(2)}) collective-permute-start(bf16[16,4096]{1,0:T(8,128)(2,1)} %collective-permute-done.8.refs_9_), channel_id=1, source_target_pairs={{0,4},{1,5},{4,8},{5,9},{8,12},{9,13},{12,14},{13,15},{14,10},{15,... | collective-permute-start | bytes 393224 | tf_op jit(solution)/shard_map/ppermute | solution.py:30
  23.5 5.9 %collective-permute-start.13 = (bf16[16,4096]{1,0:T(8,128)(2,1)}, bf16[16,4096]{1,0:T(8,128)(2,1)S(1)}, u32[]{:S(2)}, u32[]{:S(2)}) collective-permute-start(bf16[16,4096]{1,0:T(8,128)(2,1)} %collective-permute-done.9.refs_10_), channel_id=1, source_target_pairs={{0,2},{1,3},{4,0},{5,1},{8,4},{9,5},{12,8},{13,9},{14,12},{15,13},... | collective-permute-start | bytes 393224 | tf_op jit(solution)/shard_map/ppermute | solution.py:30
  30.1 55.8 %all-to-all-start = ((bf16[16,64,1024]{2,1,0:T(8,128)(2,1)}), bf16[16,64,1024]{2,1,0:T(8,128)(2,1)S(1)}, u32[]{:S(2)}, u32[]{:S(2)}) async-start(bf16[16,64,1024]{2,1,0:T(8,128)(2,1)} %split_columns.1), calls=%async_computation | async-start | bytes 4194304 | tf_op jit(solution)/shard_map/all_to_all | solution.py:278
  34.3 1.5 %collective-permute-start.15 = (bf16[16,4096]{1,0:T(8,128)(2,1)S(1)}, bf16[16,4096]{1,0:T(8,128)(2,1)S(1)}, u32[]{:S(2)}, u32[]{:S(2)}) collective-permute-start(bf16[16,4096]{1,0:T(8,128)(2,1)S(1)} %collective-permute-done.refs_1_), channel_id=1, source_target_pairs={{0,1},{1,0},{2,3},{3,2},{4,5},{5,4},{6,7},{7,6},{8,9},{9,8},{10,11... | collective-permute-start | bytes 393224 | tf_op jit(solution)/shard_map/ppermute | solution.py:48
  34.9 1.6 %collective-permute-start.17 = (bf16[16,4096]{1,0:T(8,128)(2,1)S(1)}, bf16[16,4096]{1,0:T(8,128)(2,1)S(1)}, u32[]{:S(2)}, u32[]{:S(2)}) collective-permute-start(bf16[16,4096]{1,0:T(8,128)(2,1)S(1)} %collective-permute-done.2.refs_3_), channel_id=1, source_target_pairs={{0,1},{1,0},{2,3},{3,2},{4,5},{5,4},{6,7},{7,6},{8,9},{9,8},{10,11... | collective-permute-start | bytes 393224 | tf_op jit(solution)/shard_map/ppermute | solution.py:48
  35.4 1.6 %collective-permute-start.19 = (bf16[16,4096]{1,0:T(8,128)(2,1)S(1)}, bf16[16,4096]{1,0:T(8,128)(2,1)S(1)}, u32[]{:S(2)}, u32[]{:S(2)}) collective-permute-start(bf16[16,4096]{1,0:T(8,128)(2,1)S(1)} %collective-permute-done.4.refs_5_), channel_id=1, source_target_pairs={{0,1},{1,0},{2,3},{3,2},{4,5},{5,4},{6,7},{7,6},{8,9},{9,8},{10,11... | collective-permute-start | bytes 393224 | tf_op jit(solution)/shard_map/ppermute | solution.py:48
  36.5 1.6 %collective-permute-start.22 = (bf16[16,4096]{1,0:T(8,128)(2,1)}, bf16[16,4096]{1,0:T(8,128)(2,1)S(1)}, u32[]{:S(2)}, u32[]{:S(2)}) collective-permute-start(bf16[16,4096]{1,0:T(8,128)(2,1)} %collective-permute-done.7.refs_8_), channel_id=1, source_target_pairs={{0,1},{1,0},{2,3},{3,2},{4,5},{5,4},{6,7},{7,6},{8,9},{9,8},{10,11... | collective-permute-start | bytes 393224 | tf_op jit(solution)/shard_map/ppermute | solution.py:48
  36.7 1.6 %collective-permute-start.23 = (bf16[16,4096]{1,0:T(8,128)(2,1)}, bf16[16,4096]{1,0:T(8,128)(2,1)S(1)}, u32[]{:S(2)}, u32[]{:S(2)}) collective-permute-start(bf16[16,4096]{1,0:T(8,128)(2,1)} %collective-permute-done.8.refs_9_), channel_id=1, source_target_pairs={{0,1},{1,0},{2,3},{3,2},{4,5},{5,4},{6,7},{7,6},{8,9},{9,8},{10,11... | collective-permute-start | bytes 393224 | tf_op jit(solution)/shard_map/ppermute | solution.py:48
  37.0 1.6 %collective-permute-start.24 = (bf16[16,4096]{1,0:T(8,128)(2,1)}, bf16[16,4096]{1,0:T(8,128)(2,1)S(1)}, u32[]{:S(2)}, u32[]{:S(2)}) collective-permute-start(bf16[16,4096]{1,0:T(8,128)(2,1)} %collective-permute-done.9.refs_10_), channel_id=1, source_target_pairs={{0,1},{1,0},{2,3},{3,2},{4,5},{5,4},{6,7},{7,6},{8,9},{9,8},{10,11... | collective-permute-start | bytes 393224 | tf_op jit(solution)/shard_map/ppermute | solution.py:48
  37.3 3.2 %collective-permute-start.14 = (bf16[16,8192]{1,0:T(8,128)(2,1)S(1)}, bf16[16,8192]{1,0:T(8,128)(2,1)S(1)}, u32[]{:S(2)}, u32[]{:S(2)}) collective-permute-start(bf16[16,8192]{1,0:T(8,128)(2,1)S(1)} %copy-done.1), channel_id=1, source_target_pairs={{0,1},{1,0},{2,3},{3,2},{4,5},{5,4},{6,7},{7,6},{8,9},{9,8},{10,11... | collective-permute-start | bytes 786440 | tf_op jit(solution)/shard_map/ppermute | solution.py:48
  37.6 2.4 %collective-permute-start.25 = (bf16[16,4096]{1,0:T(8,128)(2,1)S(1)}, bf16[16,4096]{1,0:T(8,128)(2,1)S(1)}, u32[]{:S(2)}, u32[]{:S(2)}) collective-permute-start(bf16[16,4096]{1,0:T(8,128)(2,1)S(1)} %collective-permute-done.10.refs_11_), channel_id=1, source_target_pairs={{0,1},{1,0},{2,3},{3,2},{4,5},{5,4},{6,7},{7,6},{8,9},{9,8},{10,11... | collective-permute-start | bytes 393224 | tf_op jit(solution)/shard_map/ppermute | solution.py:48
  38.0 2.0 %collective-permute-start.26 = (bf16[16,4096]{1,0:T(8,128)(2,1)S(1)}, bf16[16,4096]{1,0:T(8,128)(2,1)S(1)}, u32[]{:S(2)}, u32[]{:S(2)}) collective-permute-start(bf16[16,4096]{1,0:T(8,128)(2,1)S(1)} %collective-permute-done.11.refs_12_), channel_id=1, source_target_pairs={{0,1},{1,0},{2,3},{3,2},{4,5},{5,4},{6,7},{7,6},{8,9},{9,8},{10,11... | collective-permute-start | bytes 393224 | tf_op jit(solution)/shard_map/ppermute | solution.py:48
  38.3 1.8 %collective-permute-start.27 = (bf16[16,4096]{1,0:T(8,128)(2,1)}, bf16[16,4096]{1,0:T(8,128)(2,1)}, u32[]{:S(2)}, u32[]{:S(2)}) collective-permute-start(bf16[16,4096]{1,0:T(8,128)(2,1)} %copy-done.12), channel_id=1, source_target_pairs={{0,1},{1,0},{2,3},{3,2},{4,5},{5,4},{6,7},{7,6},{8,9},{9,8},{10,11... | collective-permute-start | bytes 393224 | tf_op jit(solution)/shard_map/ppermute | solution.py:48
  38.7 1.8 %collective-permute-start.28 = (bf16[16,4096]{1,0:T(8,128)(2,1)}, bf16[16,4096]{1,0:T(8,128)(2,1)}, u32[]{:S(2)}, u32[]{:S(2)}) collective-permute-start(bf16[16,4096]{1,0:T(8,128)(2,1)} %copy-done.13), channel_id=1, source_target_pairs={{0,1},{1,0},{2,3},{3,2},{4,5},{5,4},{6,7},{7,6},{8,9},{9,8},{10,11... | collective-permute-start | bytes 393224 | tf_op jit(solution)/shard_map/ppermute | solution.py:48
  46.6 2.1 %collective-permute-start.29 = (bf16[64,256]{1,0:T(8,128)(2,1)S(1)}, bf16[64,256]{1,0:T(8,128)(2,1)S(1)}, u32[]{:S(2)}, u32[]{:S(2)}) collective-permute-start(bf16[64,256]{1,0:T(8,128)(2,1)S(1)} %shrink.1), channel_id=1, source_target_pairs={{0,1},{1,0},{2,3},{3,2},{4,5},{5,4},{6,7},{7,6},{8,9},{9,8},{10,11... | collective-permute-start | bytes 98312 | tf_op jit(solution)/shard_map/ppermute | solution.py:291
  46.9 4.4 %collective-permute-start.30 = (bf16[64,256]{1,0:T(8,128)(2,1)S(1)}, bf16[64,256]{1,0:T(8,128)(2,1)S(1)}, u32[]{:S(2)}, u32[]{:S(2)}) collective-permute-start(bf16[64,256]{1,0:T(8,128)(2,1)S(1)} %shrink.1), channel_id=1, source_target_pairs={{0,2},{1,3},{2,0},{3,1},{4,6},{5,7},{6,4},{7,5},{8,10},{9,11},{10,... | collective-permute-start | bytes 98312 | tf_op jit(solution)/shard_map/ppermute | solution.py:291
  48.7 3.5 %collective-permute-start.31 = (bf16[64,256]{1,0:T(8,128)(2,1)S(1)}, bf16[64,256]{1,0:T(8,128)(2,1)S(1)}, u32[]{:S(2)}, u32[]{:S(2)}) collective-permute-start(bf16[64,256]{1,0:T(8,128)(2,1)S(1)} %shrink.1), channel_id=1, source_target_pairs={{0,3},{1,2},{2,1},{3,0},{4,7},{5,6},{6,5},{7,4},{8,11},{9,10},{10,... | collective-permute-start | bytes 98312 | tf_op jit(solution)/shard_map/ppermute | solution.py:291
  52.3 28.6 %collective-permute-start.32 = (bf16[64,256]{1,0:T(8,128)(2,1)S(1)}, bf16[64,256]{1,0:T(8,128)(2,1)S(1)}, u32[]{:S(2)}, u32[]{:S(2)}) collective-permute-start(bf16[64,256]{1,0:T(8,128)(2,1)S(1)} %add_add_fusion.refs_0_), channel_id=1, source_target_pairs={{0,4},{1,5},{2,6},{3,7},{4,8},{5,9},{6,10},{7,11},{8,12},{9,13},{1... | collective-permute-start | bytes 98312 | tf_op jit(solution)/shard_map/ppermute | solution.py:295
  57.4 28.4 %collective-permute-start.33 = (bf16[64,256]{1,0:T(8,128)(2,1)S(1)}, bf16[64,256]{1,0:T(8,128)(2,1)S(1)}, u32[]{:S(2)}, u32[]{:S(2)}) collective-permute-start(bf16[64,256]{1,0:T(8,128)(2,1)S(1)} %add_add_fusion.refs_0_), channel_id=1, source_target_pairs={{0,8},{1,9},{2,10},{3,11},{4,12},{5,13},{6,14},{7,15},{8,0},{9,1},... | collective-permute-start | bytes 98312 | tf_op jit(solution)/shard_map/ppermute | solution.py:295
  58.5 27.3 %collective-permute-start.34 = (bf16[64,256]{1,0:T(8,128)(2,1)S(1)}, bf16[64,256]{1,0:T(8,128)(2,1)S(1)}, u32[]{:S(2)}, u32[]{:S(2)}) collective-permute-start(bf16[64,256]{1,0:T(8,128)(2,1)S(1)} %add_add_fusion.refs_0_), channel_id=1, source_target_pairs={{0,12},{1,13},{2,14},{3,15},{4,0},{5,1},{6,2},{7,3},{8,4},{9,5},{1... | collective-permute-start | bytes 98312 | tf_op jit(solution)/shard_map/ppermute | solution.py:295
  (34 other events, 268.8 us)

commit v9 on v8

v9 whole, which is shorter than its diff:
```python
import functools

import jax
import jax.numpy as jnp
from jax import lax
from jax.experimental import pallas as pl
from jax.experimental.pallas import tpu as pltpu
from jax.sharding import PartitionSpec as P

ADAPTER_SCALE = 0.5
ROWS_PER_LIMIT = 64
SLOT_SIZES = (80, 96)
CORES = 2
MIB = 1024 * 1024


def chip_ring(chips):
    return list(range(0, chips, 2)) + list(range(chips - 1, 0, -2))


def ring_gather(block, axis, beside):
    size = lax.axis_size(axis)
    chips = size // CORES
    ring = chip_ring(chips)

    def moved(value, shift):
        pairs = [
            (ring[p] * CORES + k, ring[(p + shift) % chips] * CORES + k)
            for p in range(chips)
            for k in range(CORES)
        ]
        return lax.ppermute(value, axis, pairs)

    half = block.shape[1] // 2
    far = chips // 2
    halves = block[:, :half], block[:, half:]
    columns = (0, half), (half, 0)
    held = [halves, halves[::-1]]
    pieces = [(block, 0, 0)]
    for step in range(1, far + 1):
        for chain in range(1 if step == far else 2):
            right, left = held[chain]
            held[chain] = beside(chain, step, (moved(right, 1), moved(left, -1)))
            for value, column, distance in zip(held[chain], columns[chain], (-step, step)):
                pieces.append((value, column, distance))

    found = [(value, column) for value, column, _ in pieces]
    where = [
        [ring[(ring.index(device // CORES) + distance) % chips] for _, _, distance in pieces]
        for device in range(size)
    ]
    return found, where


ANY_SPEC = pl.BlockSpec(memory_space=pl.ANY)


def in_hbm(values):
    return [pltpu.with_memory_space_constraint(value, pltpu.HBM) for value in values]


def run_copies(copies):
    for copy in copies:
        copy.start()
    for copy in copies:
        copy.wait()


def split_kernel(me, in_ref, keep_ref, send_ref):
    width = keep_ref.shape[2]
    core = me[0] % CORES
    for pair in range(keep_ref.shape[0]):
        even = in_ref[:, 2 * pair * width : (2 * pair + 1) * width]
        odd = in_ref[:, (2 * pair + 1) * width : (2 * pair + 2) * width]
        keep_ref[pair] = jnp.where(core == 0, even, odd)
        send_ref[pair] = jnp.where(core == 0, odd, even)


def split_columns(me, maps, chips):
    ranks, columns = maps.shape
    units = columns // chips // CORES
    group = min(2, chips)
    out_spec = pl.BlockSpec((group, ranks, units), lambda i, s: (i, 0, 0))
    out = jax.ShapeDtypeStruct((chips, ranks, units), maps.dtype)
    return pl.pallas_call(
        split_kernel,
        grid_spec=pltpu.PrefetchScalarGridSpec(
            num_scalar_prefetch=1,
            grid=(chips // group,),
            in_specs=[pl.BlockSpec((ranks, group * CORES * units), lambda i, s: (0, i))],
            out_specs=[out_spec, out_spec],
        ),
        out_shape=[out, out],
        cost_estimate=pl.CostEstimate(flops=0, bytes_accessed=4 * ranks * columns, transcendentals=0),
        name="split_columns",
    )(me, maps)


def shrink_kernel(columns, pieces, place, own_down_ref, other_down_ref, *refs):
    piece_refs = refs[:pieces]
    tokens_ref, shrunk_ref, tokens_vmem, down_vmem, sems = refs[pieces:]
    core = place[pieces] % CORES
    ranks = own_down_ref.shape[0]
    copies = [
        pltpu.make_async_copy(own_down_ref, down_vmem.at[pl.ds(pl.multiple_of(core * ranks, ranks), ranks)], sems.at[0]),
        pltpu.make_async_copy(
            other_down_ref, down_vmem.at[pl.ds(pl.multiple_of((1 - core) * ranks, ranks), ranks)], sems.at[1]
        ),
    ]
    for i, ref in enumerate(piece_refs):
        rows, width = ref.shape
        start = pl.multiple_of(place[i] * rows, rows)
        copies.append(
            pltpu.make_async_copy(
                ref, tokens_vmem.at[pl.ds(start, rows), pl.ds(columns[i], width)], sems.at[2 + i]
            )
        )
    run_copies(copies)
    out_copy = pltpu.make_async_copy(tokens_vmem, tokens_ref, sems.at[2 + pieces])
    out_copy.start()
    shrunk_ref[...] = lax.dot_general(
        tokens_vmem[...], down_vmem[...], (((1,), (1,)), ((), ())), preferred_element_type=jnp.float32
    ).astype(shrunk_ref.dtype)
    out_copy.wait()


def shrink(place, columns, pieces, rows, own_down, other_down):
    ranks, width = own_down.shape
    return pl.pallas_call(
        functools.partial(shrink_kernel, columns, len(pieces)),
        grid_spec=pltpu.PrefetchScalarGridSpec(
            num_scalar_prefetch=1,
            grid=(1,),
            in_specs=[ANY_SPEC] * (2 + len(pieces)),
            out_specs=[ANY_SPEC, pl.BlockSpec((rows, CORES * ranks), lambda i, s: (0, 0))],
            scratch_shapes=[
                pltpu.VMEM((rows, width), jnp.bfloat16),
                pltpu.VMEM((CORES * ranks, width), jnp.bfloat16),
                pltpu.SemaphoreType.DMA((3 + len(pieces),)),
            ],
        ),
        out_shape=[
            pltpu.HBM((rows, width), jnp.bfloat16),
            jax.ShapeDtypeStruct((rows, CORES * ranks), jnp.bfloat16),
        ],
        compiler_params=pltpu.CompilerParams(vmem_limit_bytes=rows * width * 2 + 16 * MIB),
        cost_estimate=pl.CostEstimate(
            flops=4 * rows * width * ranks, bytes_accessed=4 * (rows + ranks) * width, transcendentals=0
        ),
        name="shrink",
    )(place, own_down, other_down, *pieces)


def expand_kernel(block, bounds, rows_ref, own_ref, other_ref, keep_ref, got_ref, out_ref, shrunk_vmem, maps_vmem):
    adapters = bounds.shape[0] - 2
    core = bounds[adapters + 1] % CORES
    ranks = keep_ref.shape[1]

    @pl.when(pl.program_id(0) == 0)
    def _():
        wanted = rows_ref[:, 0:1]
        slots = wanted.shape[0]
        held = lax.broadcasted_iota(jnp.int32, (slots, own_ref.shape[0]), 1)
        row = held // block * (CORES * block) + held % block
        picked = jnp.zeros(shrunk_vmem.shape, jnp.float32)
        for ref, where in ((own_ref, core), (other_ref, 1 - core)):
            hit = (wanted == row + where * block).astype(jnp.float32).astype(jnp.bfloat16)
            picked += jnp.dot(hit, ref[...], preferred_element_type=jnp.float32)
        slot = lax.broadcasted_iota(jnp.int32, picked.shape, 0)
        adapter = lax.broadcasted_iota(jnp.int32, picked.shape, 1) // (picked.shape[1] // adapters)
        mine = jnp.zeros(picked.shape, jnp.int32)
        for a in range(adapters):
            inside = (adapter == a) & (slot >= bounds[a]) & (slot < bounds[a + 1])
            mine += inside.astype(jnp.int32)
        shrunk_vmem[...] = jnp.where(mine > 0, picked, 0.0).astype(jnp.bfloat16)

    for chip in range(keep_ref.shape[0]):
        maps_vmem[pl.ds(pl.multiple_of(core * ranks, ranks), ranks), :] = keep_ref[chip]
        maps_vmem[pl.ds(pl.multiple_of((1 - core) * ranks, ranks), ranks), :] = got_ref[chip]
        product = jnp.dot(shrunk_vmem[...], maps_vmem[...], preferred_element_type=jnp.float32)
        out_ref[chip] = (ADAPTER_SCALE * product).astype(out_ref.dtype)


def expand(bounds, rows_wanted, own_shrunk, other_shrunk, keep, got, slots, block):
    chips, ranks, units = keep.shape
    rows, ranks_all = own_shrunk.shape
    group = min(4, chips)
    maps_spec = pl.BlockSpec((group, ranks, units), lambda i, s: (i, 0, 0))
    shrunk_spec = pl.BlockSpec((rows, ranks_all), lambda i, s: (0, 0))
    return pl.pallas_call(
        functools.partial(expand_kernel, block),
        grid_spec=pltpu.PrefetchScalarGridSpec(
            num_scalar_prefetch=1,
            grid=(chips // group,),
            in_specs=[
                pl.BlockSpec((slots, 128), lambda i, s: (0, 0)),
                shrunk_spec,
                shrunk_spec,
                maps_spec,
                maps_spec,
            ],
            out_specs=pl.BlockSpec((group, slots, units), lambda i, s: (i, 0, 0)),
            scratch_shapes=[
                pltpu.VMEM((slots, ranks_all), jnp.bfloat16),
                pltpu.VMEM((ranks_all, units), jnp.bfloat16),
            ],
        ),
        out_shape=jax.ShapeDtypeStruct((chips, slots, units), jnp.bfloat16),
        compiler_params=pltpu.CompilerParams(vmem_limit_bytes=20 * MIB),
        cost_estimate=pl.CostEstimate(
            flops=2 * slots * ranks_all * chips * units,
            bytes_accessed=2 * (slots + ranks_all) * chips * units,
            transcendentals=0,
        ),
        name="expand",
    )(bounds, rows_wanted, own_shrunk, other_shrunk, keep, got)


def project_kernel(block, me, gate_weight_ref, up_weight_ref, own_ref, other_ref, gate_ref, up_ref, tokens_vmem, sems):
    depth = gate_weight_ref.shape[0]
    core = me[0] % CORES
    k = pl.program_id(0)

    @pl.when(k == 0)
    def _():
        copies = []
        for ref, where in ((own_ref, core), (other_ref, 1 - core)):
            for chip in range(ref.shape[0] // block):
                start = pl.multiple_of((chip * CORES + where) * block, block)
                copies.append(
                    pltpu.make_async_copy(
                        ref.at[pl.ds(chip * block, block)], tokens_vmem.at[pl.ds(start, block)], sems.at[len(copies)]
                    )
                )
        run_copies(copies)
        gate_ref[...] = jnp.zeros_like(gate_ref)
        up_ref[...] = jnp.zeros_like(up_ref)

    tokens = tokens_vmem[:, pl.ds(pl.multiple_of(k * depth, depth), depth)]
    gate_ref[...] += jnp.dot(tokens, gate_weight_ref[...], preferred_element_type=jnp.float32)
    up_ref[...] += jnp.dot(tokens, up_weight_ref[...], preferred_element_type=jnp.float32)

    @pl.when(k == pl.num_programs(0) - 1)
    def _():
        gate = gate_ref[...]
        gate_ref[...] = gate / (1.0 + jnp.exp(-gate))


def project(me, own, other, gate_weight, up_weight, block):
    width, units = gate_weight.shape
    rows = CORES * own.shape[0]
    depth = min(1024, width)
    weight_spec = pl.BlockSpec((depth, units), lambda k, s: (k, 0))
    out_spec = pl.BlockSpec((rows, units), lambda k, s: (0, 0))
    out = pltpu.HBM((rows, units), jnp.float32)
    return pl.pallas_call(
        functools.partial(project_kernel, block),
        grid_spec=pltpu.PrefetchScalarGridSpec(
            num_scalar_prefetch=1,
            grid=(width // depth,),
            in_specs=[weight_spec, weight_spec, ANY_SPEC, ANY_SPEC],
            out_specs=[out_spec, out_spec],
            scratch_shapes=[
                pltpu.VMEM((rows, width), jnp.bfloat16),
                pltpu.SemaphoreType.DMA((rows // block,)),
            ],
        ),
        out_shape=[out, out],
        compiler_params=pltpu.CompilerParams(vmem_limit_bytes=rows * width * 2 + 20 * MIB),
        cost_estimate=pl.CostEstimate(
            flops=4 * rows * width * units,
            bytes_accessed=2 * (rows + 2 * units) * width,
            transcendentals=rows * units,
        ),
        name="project",
    )(me, *in_hbm([gate_weight, up_weight, own, other]))


def combine_kernel(held_ref, gate_ref, up_ref, products_ref, out_ref, pick_vmem):
    @pl.when(pl.program_id(0) == 0)
    def _():
        row = lax.broadcasted_iota(jnp.int32, pick_vmem.shape, 0)
        pick_vmem[...] = (row == held_ref[0:1, :]).astype(jnp.float32).astype(jnp.bfloat16)

    delta = jnp.dot(pick_vmem[...], products_ref[...], preferred_element_type=jnp.float32)
    out_ref[...] = (gate_ref[...] * (up_ref[...] + delta)).astype(out_ref.dtype)


def combine(held, gate, up, products):
    rows, units = gate.shape
    slots_all = products.shape[0]
    tile = min(512, units)
    column_spec = pl.BlockSpec((rows, tile), lambda n: (0, n))
    return pl.pallas_call(
        combine_kernel,
        grid=(units // tile,),
        in_specs=[
            pl.BlockSpec((8, slots_all), lambda n: (0, 0)),
            column_spec,
            column_spec,
            pl.BlockSpec((slots_all, tile), lambda n: (0, n)),
        ],
        out_specs=column_spec,
        scratch_shapes=[pltpu.VMEM((rows, slots_all), jnp.bfloat16)],
        out_shape=jax.ShapeDtypeStruct((rows, units), jnp.bfloat16),
        compiler_params=pltpu.CompilerParams(vmem_limit_bytes=rows * slots_all * 2 + 20 * MIB),
        cost_estimate=pl.CostEstimate(
            flops=2 * rows * slots_all * units, bytes_accessed=10 * rows * units, transcendentals=0
        ),
        name="combine",
    )(*in_hbm([held, gate, up]), products)


def per_device(
    tokens,
    gate_weight,
    up_weight,
    adapter_down_weight,
    adapter_up_weight,
    row_adapter,
    sorted_rows,
    segment_count,
):
    axis = "tensor"
    size = lax.axis_size(axis)
    me = lax.axis_index(axis).astype(jnp.int32)
    chips = size // CORES
    chip = me // CORES
    resident, rank, width = adapter_down_weight.shape
    ranks = resident * rank
    rows = row_adapter.shape[0]
    block = tokens.shape[0]
    me_array = me.reshape(1)
    flips = [(d, d ^ 1) for d in range(size)]

    def other_core(value):
        return lax.ppermute(value, axis, flips)

    most = CORES * resident * ROWS_PER_LIMIT
    adapters = CORES * resident
    ends = jnp.cumsum(segment_count.reshape(chips, adapters), axis=1)
    totals = ends[:, -1]
    starts = jnp.cumsum(totals) - totals
    slot = jnp.arange(most, dtype=jnp.int32)
    position = starts[:, None] + slot[None, :]
    listed = position[:, :, None] == jnp.arange(rows, dtype=jnp.int32)[None, None, :]
    held = jnp.sum(jnp.where(listed, sorted_rows[None, None, :] + 1, 0), axis=2) - 1
    held = jnp.where(slot[None, :] < totals[:, None], held, -1).astype(jnp.int32)
    wanted = lax.dynamic_index_in_dim(held, chip, 0, keepdims=False)
    wanted = jnp.broadcast_to(wanted[:, None], (most, 128))
    own_ends = lax.dynamic_index_in_dim(ends, chip, 0, keepdims=False)
    bounds = jnp.concatenate([jnp.zeros((1,), jnp.int32), own_ends, me_array]).astype(jnp.int32)
    needed = jnp.full((8, 128), jnp.max(totals), jnp.int32)
    groups = lax.axis_size("groups")
    for shift in range(1, groups):
        needed = jnp.maximum(
            needed, lax.ppermute(needed, "groups", [(g, (g + shift) % groups) for g in range(groups)])
        )
    sizes = [slots for slots in SLOT_SIZES if slots < most] + [most]
    choice = jnp.sum((needed[0, 0] > jnp.array(sizes[:-1], jnp.int32)).astype(jnp.int32))

    own_down = adapter_down_weight.reshape(ranks, width)
    other_down = other_core(own_down)
    own_maps = adapter_up_weight.reshape(ranks, -1)
    steps = chips // 2
    keep = got = None

    def beside(chain, step, values):
        nonlocal own_maps, keep, got
        if step == steps - 1:
            own_maps, *values = lax.optimization_barrier((own_maps, *values))
            if chain == 1:
                keep, send = split_columns(me_array, own_maps, chips)
                got = other_core(send)
        return values

    found, where = ring_gather(tokens, axis, beside)
    pieces = [piece for piece, _ in found]
    columns = [column for _, column in found]
    table = jnp.array([row + [device] for device, row in enumerate(where)], jnp.int32)
    place = lax.dynamic_index_in_dim(table, me, 0, keepdims=False)
    own_tokens, own_shrunk = shrink(place, columns, pieces, rows // CORES, own_down, other_down)
    other_shrunk = other_core(own_shrunk)

    same_core = [[c * CORES + k for c in range(chips)] for k in range(CORES)]

    def finish(slots):
        def branch(own_tokens, own_shrunk, other_shrunk, keep, got, wanted, held, bounds, gate_weight, up_weight):
            products = expand(bounds, wanted[:slots], own_shrunk, other_shrunk, keep, got, slots, block)
            products = lax.all_to_all(
                products, axis, split_axis=0, concat_axis=0, axis_index_groups=same_core, tiled=True
            )
            other_tokens = other_core(own_tokens)
            gate, up = project(me_array, own_tokens, other_tokens, gate_weight, up_weight, block)
            held_rows = jnp.broadcast_to(held[:, :slots].reshape(1, chips * slots), (8, chips * slots))
            return combine(held_rows, gate, up, products.reshape(chips * slots, -1))

        return branch

    return lax.switch(
        choice,
        [finish(slots) for slots in sizes],
        own_tokens,
        own_shrunk,
        other_shrunk,
        keep,
        got,
        wanted,
        held,
        bounds,
        gate_weight,
        up_weight,
    )


def solution(mesh):
    placed = (
        P(("groups", "tensor"), None),
        P(None, "tensor"),
        P(None, "tensor"),
        P(("groups", "tensor"), None, None),
        P(("groups", "tensor"), None, None),
        P("groups"),
        P("groups"),
        P("groups"),
    )
    return jax.shard_map(
        per_device, mesh=mesh, in_specs=placed, out_specs=P("groups", "tensor"), check_vma=False
    )
```

time: 90.1 us -> 89.2 us (0.990)
  starting transfers between devices: 34.1 us -> 22.1 us
  other arithmetic: 0.01 us -> 6.12 us
  local copies, waits for them, and re-layouts: 4.21 us -> 7.19 us
  Pallas kernels: 33.5 us -> 34.7 us
    ppermute x21 -> x5, starting transfers between devices: 14 us -> 2.72 us  [the longest x1 2.1 us: per_device(): lax.ppermute(needed, 'groups', [(g, (g + shift) % groups) for g in range(...]
    all_to_all x1, waiting for transfers between devices: 0.01 us -> 9.97 us  [branch(): lax.all_to_all(products, axis, split_axis=0, concat_axis=0, axis_index_gr...]
    ppermute x21 -> x5, waiting for transfers between devices: 9.09 us -> 0.01 us  [the longest x4 0.01 us: other_core(): return lax.ppermute(value, axis, flips)]
    reduce_sum x0 -> x2, other arithmetic: none -> 1.66 us  [the longest x1 1.29 us: per_device(): jnp.sum((needed[0, 0] > jnp.array(sizes[:-1], jnp.int32)).astype(jnp.int32))]
    max x0 -> x1, other arithmetic: none -> 1.3 us  [per_device(): jnp.maximum(needed, lax.ppermute(needed, 'groups', [(g, (g + shift) % gro...]
    cond x0 -> x2, local copies, waits for them, and re-layouts: none -> 1.29 us
    pallas_call x4 -> x5, Pallas kernels: 33.5 us -> 34.7 us  [the longest x1 20.2 us: project(): pl.pallas_call(functools.partial(project_kernel, block), grid_spec=pltpu....]
    unnamed x60 -> x8, local copies, waits for them, and re-layouts: 1.78 us -> 0.8 us
  transfers between devices with their start and end apart: 36 -> 20, of which waited for: 12 -> 7; matrix products, arithmetic and copies ran while one was open for 1% -> 11% of each run, Pallas kernels for 34% -> 37%
where the time goes in v9:
time: 89.2 us; the launch traced here: 88.7 us
  Pallas kernels  34.7 us (39%)
  starting transfers between devices  22.1 us (25%)
  waiting for transfers between devices  17.9 us (20%)
  local copies, waits for them, and re-layouts  7.19 us (8%)
  other arithmetic  6.12 us (7%)
    pallas_call x1, Pallas kernels, project(): pl.pallas_call(functools.partial(project_kernel, block), grid_spec=pltpu....  20.2 us
    ppermute x14, starting transfers between devices, moved(): return lax.ppermute(value, axis, pairs)  15.6 us
    all_to_all x1, waiting for transfers between devices, branch(): lax.all_to_all(products, axis, split_axis=0, concat_axis=0, axis_index_gr...  9.97 us
    ppermute x14, waiting for transfers between devices, moved(): return lax.ppermute(value, axis, pairs)  7.89 us
    pallas_call x1, Pallas kernels, shrink(): pl.pallas_call(functools.partial(shrink_kernel, columns, len(pieces)), gr...  4.7 us
    pallas_call x1, Pallas kernels, expand(): pl.pallas_call(functools.partial(expand_kernel, block), grid_spec=pltpu.P...  3.9 us
    all_to_all x1, starting transfers between devices, branch(): lax.all_to_all(products, axis, split_axis=0, concat_axis=0, axis_index_gr...  3.81 us
    pallas_call x1, Pallas kernels, split_columns(): pl.pallas_call(split_kernel, grid_spec=pltpu.PrefetchScalarGridSpec(num_s...  3.77 us
  transfers between devices with their start and end apart: 20, of which 7 were waited for; matrix products, arithmetic and copies ran while one was open for 11% of the time, Pallas kernels for 37%

profile of v9, /device:TPU:0, one launch (start us, length us, event | category | flops | bytes accessed | tf_op | source)
XLA Modules:
  0.0 88.7 jit_solution(16285101473539578201)
XLA Ops:
  0.0 1.1 %fusion.4 = (bf16[16,4096]{1,0:T(8,128)(2,1)S(1)}, bf16[16,4096]{1,0:T(8,128)(2,1)S(1)}) fusion(bf16[16,8192]{1,0:T(8,128)(2,1)} %refs_0_.1), kind=kLoop, calls=%fused_computation.19 | loop fusion | bytes 524288 | tf_op jit(solution)/shard_map/slice | solution.py:36
  1.1 3.1 %collective-permute-start.5 = (bf16[16,4096]{1,0:T(8,128)(2,1)S(1)}, bf16[16,4096]{1,0:T(8,128)(2,1)S(1)}, u32[]{:S(2)}, u32[]{:S(2)}) collective-permute-start(bf16[16,4096]{1,0:T(8,128)(2,1)S(1)} %get-tuple-element.139), channel_id=1, source_target_pairs={{0,4},{1,5},{4,8},{5,9},{8,12},{9,13},{12,14},{13,15},{14,10},{15,... | collective-permute-start | bytes 393224 | tf_op jit(solution)/shard_map/ppermute | solution.py:32
  4.2 2.0 %collective-permute-start.7 = (bf16[16,4096]{1,0:T(8,128)(2,1)S(1)}, bf16[16,4096]{1,0:T(8,128)(2,1)S(1)}, u32[]{:S(2)}, u32[]{:S(2)}) collective-permute-start(bf16[16,4096]{1,0:T(8,128)(2,1)S(1)} %get-tuple-element.138), channel_id=1, source_target_pairs={{0,4},{1,5},{4,8},{5,9},{8,12},{9,13},{12,14},{13,15},{14,10},{15,... | collective-permute-start | bytes 393224 | tf_op jit(solution)/shard_map/ppermute | solution.py:32
  6.2 0.7 reshape.56
  7.2 0.7 slice_reduce_fusion
  8.4 2.1 %collective-permute-start.9 = (bf16[16,4096]{1,0:T(8,128)(2,1)S(1)}, bf16[16,4096]{1,0:T(8,128)(2,1)S(1)}, u32[]{:S(2)}, u32[]{:S(2)}) collective-permute-start(bf16[16,4096]{1,0:T(8,128)(2,1)S(1)} %collective-permute-done.5.refs_1_), channel_id=1, source_target_pairs={{0,4},{1,5},{4,8},{5,9},{8,12},{9,13},{12,14},{13,15},{14,10},{15,... | collective-permute-start | bytes 393224 | tf_op jit(solution)/shard_map/ppermute | solution.py:32
  10.6 2.0 %collective-permute-start.11 = (bf16[16,4096]{1,0:T(8,128)(2,1)S(1)}, bf16[16,4096]{1,0:T(8,128)(2,1)S(1)}, u32[]{:S(2)}, u32[]{:S(2)}) collective-permute-start(bf16[16,4096]{1,0:T(8,128)(2,1)S(1)} %collective-permute-done.7.refs_3_), channel_id=1, source_target_pairs={{0,4},{1,5},{4,8},{5,9},{8,12},{9,13},{12,14},{13,15},{14,10},{15,... | collective-permute-start | bytes 393224 | tf_op jit(solution)/shard_map/ppermute | solution.py:32
  12.7 2.1 %collective-permute-done.9.refs_5_ = bf16[16,4096]{1,0:T(8,128)(2,1)S(1)} collective-permute-done((bf16[16,4096]{1,0:T(8,128)(2,1)S(1)}, bf16[16,4096]{1,0:T(8,128)(2,1)S(1)}, u32[]{:S(2)}, u32[]{:S(2)}) %collective-permute-start.9) | collective-permute-done | bytes 131104 | tf_op jit(solution)/shard_map/ppermute | solution.py:32
  14.8 2.1 %collective-permute-start.13 = (bf16[16,4096]{1,0:T(8,128)(2,1)S(1)}, bf16[16,4096]{1,0:T(8,128)(2,1)S(1)}, u32[]{:S(2)}, u32[]{:S(2)}) collective-permute-start(bf16[16,4096]{1,0:T(8,128)(2,1)S(1)} %collective-permute-done.9.refs_5_), channel_id=1, source_target_pairs={{0,4},{1,5},{4,8},{5,9},{8,12},{9,13},{12,14},{13,15},{14,10},{15,... | collective-permute-start | bytes 393224 | tf_op jit(solution)/shard_map/ppermute | solution.py:32
  16.9 0.7 collective-permute-done.11.refs_7_
  17.6 2.1 %collective-permute-start.15 = (bf16[16,4096]{1,0:T(8,128)(2,1)S(1)}, bf16[16,4096]{1,0:T(8,128)(2,1)}, u32[]{:S(2)}, u32[]{:S(2)}) collective-permute-start(bf16[16,4096]{1,0:T(8,128)(2,1)S(1)} %collective-permute-done.11.refs_7_), channel_id=1, source_target_pairs={{0,4},{1,5},{4,8},{5,9},{8,12},{9,13},{12,14},{13,15},{14,10},{15,... | collective-permute-start | bytes 393224 | tf_op jit(solution)/shard_map/ppermute | solution.py:32
  19.7 0.7 broadcast_add_fusion
  21.7 2.1 %collective-permute-start.3 = (s32[8,128]{1,0:T(8,128)S(1)}, s32[8,128]{1,0:T(8,128)}, u32[]{:S(2)}, u32[]{:S(2)}) collective-permute-start(s32[8,128]{1,0:T(8,128)S(1)} %broadcast_in_dim.52), channel_id=1, source_target_pairs={{0,16},{16,0},{1,17},{17,1},{2,18},{18,2},{3,19},{19,3},{4,20},{20... | collective-permute-start | bytes 12296 | tf_op jit(solution)/shard_map/ppermute | solution.py:357
  23.8 1.1 %collective-permute-done.16.refs_12_ = bf16[16,4096]{1,0:T(8,128)(2,1)} collective-permute-done((bf16[16,4096]{1,0:T(8,128)(2,1)S(1)}, bf16[16,4096]{1,0:T(8,128)(2,1)}, u32[]{:S(2)}, u32[]{:S(2)}) %collective-permute-start.16) | collective-permute-done | bytes 131104 | tf_op jit(solution)/shard_map/ppermute | solution.py:32
  24.8 3.8 %split_columns.1 = (bf16[8,64,1024]{2,1,0:T(8,128)(2,1)}, bf16[8,64,1024]{2,1,0:T(8,128)(2,1)}) custom-call(s32[1]{0:T(128)} %bitcast.8.me, bf16[64,16384]{1,0:T(8,128)(2,1)} %bitcast.21), custom_call_target="tpu_custom_call" | custom-call | bytes 4194304 | tf_op jit(solution)/shard_map/split_columns/pallas_call | solution.py:85
  29.0 0.7 add_select_fusion
  29.7 0.7 fusion.place
  30.4 0.8 pad_add_fusion
  31.1 1.6 %collective-permute-start.17 = (bf16[16,4096]{1,0:T(8,128)(2,1)S(1)}, bf16[16,4096]{1,0:T(8,128)(2,1)S(1)}, u32[]{:S(2)}, u32[]{:S(2)}) collective-permute-start(bf16[16,4096]{1,0:T(8,128)(2,1)S(1)} %collective-permute-done.13.refs_9_), channel_id=1, source_target_pairs={{0,4},{1,5},{4,8},{5,9},{8,12},{9,13},{12,14},{13,15},{14,10},{15,... | collective-permute-start | bytes 393224 | tf_op jit(solution)/shard_map/ppermute | solution.py:32
  33.2 1.3 %broadcast_maximum_fusion = s32[8,128]{1,0:T(8,128)S(1)} fusion(s32[8,128]{1,0:T(8,128)} %collective-permute-done.3, s32[]{:T(128)} %get-tuple-element.136), kind=kLoop, calls=%fused_computation.6 | loop fusion | flops 1024 | bytes 8196 | tf_op jit(solution)/shard_map/max | solution.py:356
  35.0 2.0 %collective-permute-done.17.refs_13_ = bf16[16,4096]{1,0:T(8,128)(2,1)S(1)} collective-permute-done((bf16[16,4096]{1,0:T(8,128)(2,1)S(1)}, bf16[16,4096]{1,0:T(8,128)(2,1)S(1)}, u32[]{:S(2)}, u32[]{:S(2)}) %collective-permute-start.17) | collective-permute-done | bytes 131104 | tf_op jit(solution)/shard_map/ppermute | solution.py:32
  37.1 1.5 %collective-permute-done.18.refs_14_ = bf16[16,4096]{1,0:T(8,128)(2,1)S(1)} collective-permute-done((bf16[16,4096]{1,0:T(8,128)(2,1)}, bf16[16,4096]{1,0:T(8,128)(2,1)S(1)}, u32[]{:S(2)}, u32[]{:S(2)}) %collective-permute-start.18) | collective-permute-done | bytes 131104 | tf_op jit(solution)/shard_map/ppermute | solution.py:32
  38.6 4.7 %shrink.1 = (bf16[128,8192]{1,0:T(8,128)(2,1)}, bf16[128,128]{1,0:T(8,128)(2,1)}) custom-call(s32[16]{0:T(128)S(1)} %fusion.place, bf16[64,8192]{1,0:T(8,128)(2,1)S(1)} %bitcast.20, bf16[64,8192]{1,0:T(8,128)(2,1)S(1)} %collective-permute-done.4.other_down_ref, bf16[16,8192]{1,0:T(8,128)(2,1)S(1)} %copy-done.2, ...), custom_call_target="tpu_custom_call" | custom-call | flops 268435456 | bytes 6291456 | tf_op jit(solution)/shard_map/shrink/pallas_call | solution.py:129
  43.4 1.3 %fusion.3 = s32[]{:T(128)} fusion(s32[2]{0:T(128)S(1)} %copy-done.6, s32[]{:T(128)} %bitcast.4), kind=kLoop, calls=%fused_computation.14 | loop fusion | flops 5 | bytes 16 | tf_op jit(solution)/shard_map/reduce_sum | solution.py:360
  45.4 42.5 %conditional.1 = (bf16[256,1024]{1,0:T(8,128)(2,1)S(1)}) conditional(s32[]{:T(128)} %clamp.3, (s32[8,128]{1,0:T(8,128)S(1)}, bf16[128,8192]{1,0:T(8,128)(2,1)}, s32[1]{0:T(128)}, bf16[8192,1024]{1,0:T(8,128)(2,1)}, bf16[8192,1024]{1,0:T(8,128)(2,1)}, /*index=5*/s32[128,128]{1,0:T(8,128)S(1)}, s32[4]{0:T(128)S(1)}, ...), branch_computations={%region_5.6_spmd, %region_6.7_spmd, %region_7.8_spmd} | conditional | flops 9395240960 | bytes 76058760 | solution.py:400
  46.0 3.9 %expand.3 = bf16[8,80,1024]{2,1,0:T(8,128)(2,1)} custom-call(s32[4]{0:T(128)S(1)} %get-tuple-element.82.bounds, s32[80,128]{1,0:T(8,128)S(1)} %slice.17.rows_ref, bf16[128,128]{1,0:T(8,128)(2,1)} %get-tuple-element.84.own_ref, bf16[128,128]{1,0:T(8,128)(2,1)S(1)} %get-tuple-element.85.other_ref, bf16[8,64,1024]{2,1,0:T(8,128)(2,1)} %get-tuple-element.86.keep_ref, ...), custom_call_target="tpu_custom_call" | custom-call | flops 167772160 | bytes 3407872 | tf_op jit(solution)/shard_map/cond/branch_0_fun/expand/pallas_call | solution.py:190
  49.9 3.8 %all-to-all-start = ((bf16[8,80,1024]{2,1,0:T(8,128)(2,1)}), bf16[8,80,1024]{2,1,0:T(8,128)(2,1)S(1)}, u32[]{:S(2)}, u32[]{:S(2)}) async-start(bf16[8,80,1024]{2,1,0:T(8,128)(2,1)} %expand.3), calls=%async_computation | async-start | bytes 2621440 | tf_op jit(solution)/shard_map/cond/branch_0_fun/all_to_all | solution.py:390
  53.8 1.3 %copy-done.3 = bf16[128,8192]{1,0:T(8,128)(2,1)} copy-done((bf16[128,8192]{1,0:T(8,128)(2,1)}, bf16[128,8192]{1,0:T(8,128)(2,1)S(1)}, u32[]{:S(2)}) %copy-start.3) | copy-done | bytes 2097176 | tf_op jit(solution)/shard_map/cond
  55.0 20.2 %project.3 = (f32[256,1024]{1,0:T(8,128)}, f32[256,1024]{1,0:T(8,128)}) custom-call(s32[1]{0:T(128)} %get-tuple-element.76.me, bf16[8192,1024]{1,0:T(8,128)(2,1)} %get-tuple-element.77.gate_weight_ref, bf16[8192,1024]{1,0:T(8,128)(2,1)} %get-tuple-element.78.up_weight_ref, bf16[128,8192]{1,0:T(8,128)(2,1)} %get-tuple-element.79.own_ref, ...), custom_call_target="tpu_custom_call" | custom-call | flops 8589934592 | bytes 37748736 | tf_op jit(solution)/shard_map/cond/branch_0_fun/project/pallas_call | solution.py:256
  75.3 10.0 %all-to-all-done = bf16[8,80,1024]{2,1,0:T(8,128)(2,1)S(1)} async-done(((bf16[8,80,1024]{2,1,0:T(8,128)(2,1)}), bf16[8,80,1024]{2,1,0:T(8,128)(2,1)S(1)}, u32[]{:S(2)}, u32[]{:S(2)}) %all-to-all-start) | async-done | bytes 1310752 | tf_op jit(solution)/shard_map/cond/branch_0_fun/all_to_all | solution.py:390
  85.8 2.1 %combine.3 = bf16[256,1024]{1,0:T(8,128)(2,1)S(1)} custom-call(s32[8,640]{1,0:T(8,128)} %broadcast_in_dim.22.held_ref, f32[256,1024]{1,0:T(8,128)} %get-tuple-element.80.gate_ref, f32[256,1024]{1,0:T(8,128)} %get-tuple-element.81.up_ref, bf16[640,1024]{1,0:T(8,128)(2,1)S(1)} %bitcast.18), custom_call_target="tpu_custom_call" | custom-call | flops 335544320 | bytes 2621440 | tf_op jit(solution)/shard_map/cond/branch_0_fun/combine/pallas_call | solution.py:294
  87.9 0.8 copy-done.5
  (46 shorter events, 4.9 us)
Async XLA Ops:
  0.0 38.6 %copy-start.2 = (bf16[16,8192]{1,0:T(8,128)(2,1)S(1)}, bf16[16,8192]{1,0:T(8,128)(2,1)}, u32[]{:S(2)}) copy-start(bf16[16,8192]{1,0:T(8,128)(2,1)} %refs_0_.1) | copy-start | bytes 786436
  0.0 38.6 %copy-start.1 = (bf16[1,64,8192]{2,1,0:T(8,128)(2,1)S(1)}, bf16[1,64,8192]{2,1,0:T(8,128)(2,1)}, u32[]{:S(2)}) copy-start(bf16[1,64,8192]{2,1,0:T(8,128)(2,1)} %param.16) | copy-start | bytes 3145732
  1.1 7.3 %collective-permute-start.5 = (bf16[16,4096]{1,0:T(8,128)(2,1)S(1)}, bf16[16,4096]{1,0:T(8,128)(2,1)S(1)}, u32[]{:S(2)}, u32[]{:S(2)}) collective-permute-start(bf16[16,4096]{1,0:T(8,128)(2,1)S(1)} %get-tuple-element.139), channel_id=1, source_target_pairs={{0,4},{1,5},{4,8},{5,9},{8,12},{9,13},{12,14},{13,15},{14,10},{15,... | collective-permute-start | bytes 393224 | tf_op jit(solution)/shard_map/ppermute | solution.py:32
  4.2 6.4 %collective-permute-start.6 = (bf16[16,4096]{1,0:T(8,128)(2,1)S(1)}, bf16[16,4096]{1,0:T(8,128)(2,1)S(1)}, u32[]{:S(2)}, u32[]{:S(2)}) collective-permute-start(bf16[16,4096]{1,0:T(8,128)(2,1)S(1)} %get-tuple-element.138), channel_id=1, source_target_pairs={{0,2},{1,3},{4,0},{5,1},{8,4},{9,5},{12,8},{13,9},{14,12},{15,13},... | collective-permute-start | bytes 393224 | tf_op jit(solution)/shard_map/ppermute | solution.py:32
  4.2 6.4 %collective-permute-start.7 = (bf16[16,4096]{1,0:T(8,128)(2,1)S(1)}, bf16[16,4096]{1,0:T(8,128)(2,1)S(1)}, u32[]{:S(2)}, u32[]{:S(2)}) collective-permute-start(bf16[16,4096]{1,0:T(8,128)(2,1)S(1)} %get-tuple-element.138), channel_id=1, source_target_pairs={{0,4},{1,5},{4,8},{5,9},{8,12},{9,13},{12,14},{13,15},{14,10},{15,... | collective-permute-start | bytes 393224 | tf_op jit(solution)/shard_map/ppermute | solution.py:32
  6.2 6.4 %collective-permute-start.8 = (bf16[16,4096]{1,0:T(8,128)(2,1)S(1)}, bf16[16,4096]{1,0:T(8,128)(2,1)S(1)}, u32[]{:S(2)}, u32[]{:S(2)}) collective-permute-start(bf16[16,4096]{1,0:T(8,128)(2,1)S(1)} %get-tuple-element.139), channel_id=1, source_target_pairs={{0,2},{1,3},{4,0},{5,1},{8,4},{9,5},{12,8},{13,9},{14,12},{15,13},... | collective-permute-start | bytes 393224 | tf_op jit(solution)/shard_map/ppermute | solution.py:32
  6.2 32.4 %collective-permute-start.4 = (bf16[64,8192]{1,0:T(8,128)(2,1)}, bf16[64,8192]{1,0:T(8,128)(2,1)S(1)}, u32[]{:S(2)}, u32[]{:S(2)}) collective-permute-start(bf16[64,8192]{1,0:T(8,128)(2,1)} %bitcast.19), channel_id=1, source_target_pairs={{0,1},{1,0},{2,3},{3,2},{4,5},{5,4},{6,7},{7,6},{8,9},{9,8},{10,11... | collective-permute-start | bytes 3145736 | tf_op jit(solution)/shard_map/ppermute | solution.py:337
  8.4 6.4 %collective-permute-start.9 = (bf16[16,4096]{1,0:T(8,128)(2,1)S(1)}, bf16[16,4096]{1,0:T(8,128)(2,1)S(1)}, u32[]{:S(2)}, u32[]{:S(2)}) collective-permute-start(bf16[16,4096]{1,0:T(8,128)(2,1)S(1)} %collective-permute-done.5.refs_1_), channel_id=1, source_target_pairs={{0,4},{1,5},{4,8},{5,9},{8,12},{9,13},{12,14},{13,15},{14,10},{15,... | collective-permute-start | bytes 393224 | tf_op jit(solution)/shard_map/ppermute | solution.py:32
  10.6 6.4 %collective-permute-start.10 = (bf16[16,4096]{1,0:T(8,128)(2,1)S(1)}, bf16[16,4096]{1,0:T(8,128)(2,1)S(1)}, u32[]{:S(2)}, u32[]{:S(2)}) collective-permute-start(bf16[16,4096]{1,0:T(8,128)(2,1)S(1)} %collective-permute-done.6.refs_2_), channel_id=1, source_target_pairs={{0,2},{1,3},{4,0},{5,1},{8,4},{9,5},{12,8},{13,9},{14,12},{15,13},... | collective-permute-start | bytes 393224 | tf_op jit(solution)/shard_map/ppermute | solution.py:32
  10.6 7.1 %collective-permute-start.11 = (bf16[16,4096]{1,0:T(8,128)(2,1)S(1)}, bf16[16,4096]{1,0:T(8,128)(2,1)S(1)}, u32[]{:S(2)}, u32[]{:S(2)}) collective-permute-start(bf16[16,4096]{1,0:T(8,128)(2,1)S(1)} %collective-permute-done.7.refs_3_), channel_id=1, source_target_pairs={{0,4},{1,5},{4,8},{5,9},{8,12},{9,13},{12,14},{13,15},{14,10},{15,... | collective-permute-start | bytes 393224 | tf_op jit(solution)/shard_map/ppermute | solution.py:32
  12.6 7.1 %collective-permute-start.12 = (bf16[16,4096]{1,0:T(8,128)(2,1)S(1)}, bf16[16,4096]{1,0:T(8,128)(2,1)S(1)}, u32[]{:S(2)}, u32[]{:S(2)}) collective-permute-start(bf16[16,4096]{1,0:T(8,128)(2,1)S(1)} %collective-permute-done.8.refs_4_), channel_id=1, source_target_pairs={{0,2},{1,3},{4,0},{5,1},{8,4},{9,5},{12,8},{13,9},{14,12},{15,13},... | collective-permute-start | bytes 393224 | tf_op jit(solution)/shard_map/ppermute | solution.py:32
  14.8 6.2 %collective-permute-start.13 = (bf16[16,4096]{1,0:T(8,128)(2,1)S(1)}, bf16[16,4096]{1,0:T(8,128)(2,1)S(1)}, u32[]{:S(2)}, u32[]{:S(2)}) collective-permute-start(bf16[16,4096]{1,0:T(8,128)(2,1)S(1)} %collective-permute-done.9.refs_5_), channel_id=1, source_target_pairs={{0,4},{1,5},{4,8},{5,9},{8,12},{9,13},{12,14},{13,15},{14,10},{15,... | collective-permute-start | bytes 393224 | tf_op jit(solution)/shard_map/ppermute | solution.py:32
  16.9 6.8 %collective-permute-start.14 = (bf16[16,4096]{1,0:T(8,128)(2,1)S(1)}, bf16[16,4096]{1,0:T(8,128)(2,1)}, u32[]{:S(2)}, u32[]{:S(2)}) collective-permute-start(bf16[16,4096]{1,0:T(8,128)(2,1)S(1)} %collective-permute-done.10.refs_6_), channel_id=1, source_target_pairs={{0,2},{1,3},{4,0},{5,1},{8,4},{9,5},{12,8},{13,9},{14,12},{15,13},... | collective-permute-start | bytes 393224 | tf_op jit(solution)/shard_map/ppermute | solution.py:32
  17.6 6.1 %collective-permute-start.15 = (bf16[16,4096]{1,0:T(8,128)(2,1)S(1)}, bf16[16,4096]{1,0:T(8,128)(2,1)}, u32[]{:S(2)}, u32[]{:S(2)}) collective-permute-start(bf16[16,4096]{1,0:T(8,128)(2,1)S(1)} %collective-permute-done.11.refs_7_), channel_id=1, source_target_pairs={{0,4},{1,5},{4,8},{5,9},{8,12},{9,13},{12,14},{13,15},{14,10},{15,... | collective-permute-start | bytes 393224 | tf_op jit(solution)/shard_map/ppermute | solution.py:32
  19.7 5.1 %collective-permute-start.16 = (bf16[16,4096]{1,0:T(8,128)(2,1)S(1)}, bf16[16,4096]{1,0:T(8,128)(2,1)}, u32[]{:S(2)}, u32[]{:S(2)}) collective-permute-start(bf16[16,4096]{1,0:T(8,128)(2,1)S(1)} %collective-permute-done.12.refs_8_), channel_id=1, source_target_pairs={{0,2},{1,3},{4,0},{5,1},{8,4},{9,5},{12,8},{13,9},{14,12},{15,13},... | collective-permute-start | bytes 393224 | tf_op jit(solution)/shard_map/ppermute | solution.py:32
  21.7 11.5 %collective-permute-start.3 = (s32[8,128]{1,0:T(8,128)S(1)}, s32[8,128]{1,0:T(8,128)}, u32[]{:S(2)}, u32[]{:S(2)}) collective-permute-start(s32[8,128]{1,0:T(8,128)S(1)} %broadcast_in_dim.52), channel_id=1, source_target_pairs={{0,16},{16,0},{1,17},{17,1},{2,18},{18,2},{3,19},{19,3},{4,20},{20... | collective-permute-start | bytes 12296 | tf_op jit(solution)/shard_map/ppermute | solution.py:357
  28.6 16.7 %collective-permute-start.20 = (bf16[8,64,1024]{2,1,0:T(8,128)(2,1)}, bf16[8,64,1024]{2,1,0:T(8,128)(2,1)}, u32[]{:S(2)}, u32[]{:S(2)}) collective-permute-start(bf16[8,64,1024]{2,1,0:T(8,128)(2,1)} %get-tuple-element.133), channel_id=1, source_target_pairs={{0,1},{1,0},{2,3},{3,2},{4,5},{5,4},{6,7},{7,6},{8,9},{9,8},{10,11... | collective-permute-start | bytes 3145736 | tf_op jit(solution)/shard_map/ppermute | solution.py:337
  31.1 5.9 %collective-permute-start.17 = (bf16[16,4096]{1,0:T(8,128)(2,1)S(1)}, bf16[16,4096]{1,0:T(8,128)(2,1)S(1)}, u32[]{:S(2)}, u32[]{:S(2)}) collective-permute-start(bf16[16,4096]{1,0:T(8,128)(2,1)S(1)} %collective-permute-done.13.refs_9_), channel_id=1, source_target_pairs={{0,4},{1,5},{4,8},{5,9},{8,12},{9,13},{12,14},{13,15},{14,10},{15,... | collective-permute-start | bytes 393224 | tf_op jit(solution)/shard_map/ppermute | solution.py:32
  32.7 5.8 %collective-permute-start.18 = (bf16[16,4096]{1,0:T(8,128)(2,1)}, bf16[16,4096]{1,0:T(8,128)(2,1)S(1)}, u32[]{:S(2)}, u32[]{:S(2)}) collective-permute-start(bf16[16,4096]{1,0:T(8,128)(2,1)} %collective-permute-done.14.refs_10_), channel_id=1, source_target_pairs={{0,2},{1,3},{4,0},{5,1},{8,4},{9,5},{12,8},{13,9},{14,12},{15,13},... | collective-permute-start | bytes 393224 | tf_op jit(solution)/shard_map/ppermute | solution.py:32
  35.0 8.4 %copy-start.6 = (s32[2]{0:T(128)S(1)}, s32[2]{0:T(128)}, u32[]{:S(2)}) copy-start(s32[2]{0:T(128)} %constant.52.clone) | copy-start | bytes 28
  43.3 2.0 %collective-permute-start.19 = (bf16[128,128]{1,0:T(8,128)(2,1)}, bf16[128,128]{1,0:T(8,128)(2,1)S(1)}, u32[]{:S(2)}, u32[]{:S(2)}) collective-permute-start(bf16[128,128]{1,0:T(8,128)(2,1)} %get-tuple-element.130), channel_id=1, source_target_pairs={{0,1},{1,0},{2,3},{3,2},{4,5},{5,4},{6,7},{7,6},{8,9},{9,8},{10,11... | collective-permute-start | bytes 98312 | tf_op jit(solution)/shard_map/ppermute | solution.py:337
  45.4 8.3 %collective-permute-start = (bf16[128,8192]{1,0:T(8,128)(2,1)}, bf16[128,8192]{1,0:T(8,128)(2,1)S(1)}, u32[]{:S(2)}, u32[]{:S(2)}) collective-permute-start(bf16[128,8192]{1,0:T(8,128)(2,1)} %get-tuple-element.79.own_ref), channel_id=1, source_target_pairs={{0,1},{1,0},{2,3},{3,2},{4,5},{5,4},{6,7},{7,6},{8,9},{9,8},{10,11... | collective-permute-start | bytes 6291464 | tf_op jit(solution)/shard_map/cond/branch_0_fun/ppermute | solution.py:337
  49.9 35.4 %all-to-all-start = ((bf16[8,80,1024]{2,1,0:T(8,128)(2,1)}), bf16[8,80,1024]{2,1,0:T(8,128)(2,1)S(1)}, u32[]{:S(2)}, u32[]{:S(2)}) async-start(bf16[8,80,1024]{2,1,0:T(8,128)(2,1)} %expand.3), calls=%async_computation | async-start | bytes 2621440 | tf_op jit(solution)/shard_map/cond/branch_0_fun/all_to_all | solution.py:390
  53.7 1.3 %copy-start.3 = (bf16[128,8192]{1,0:T(8,128)(2,1)}, bf16[128,8192]{1,0:T(8,128)(2,1)S(1)}, u32[]{:S(2)}) copy-start(bf16[128,8192]{1,0:T(8,128)(2,1)S(1)} %collective-permute-done.other_ref) | copy-start | bytes 6291460 | tf_op jit(solution)/shard_map/cond
  87.9 0.8 copy-start.5
